TPU v7x, 32 devices: a whole 2x2x4 slice. The times are simulated.
32 devices in a mesh: section: 2 (over x), group: 4 (over z), dp: 4 (over y, core).
Axes of the slice: x: 2, y: 2, z: 4, core: 2. Of those that a mesh axis runs over, the one named last changes fastest.
Arguments:
- enc_input: bfloat16 [2, 16, 256, 768], P('section', ('group', 'dp')), may hold values from -6 to 6
- segments: int32 [2, 16, 256], P(None, ('group', 'dp')), may hold values from 0 to 5, as said below
- slots: int32 [2, 16, 256], P(None, ('group', 'dp')), may hold values from 0 to 195, as said below
- params: bfloat16 [2, 7088128], P('section', 'group'), as said below
- cot: bfloat16 [2, 16, 980, 512], P('section', ('group', 'dp')), may hold values from -6 to 6
Outputs:
- dec_out: bfloat16 [2, 16, 980, 512], P('section', ('group', 'dp'))
- in_grad: float32 [2, 16, 256, 768], P('section', ('group', 'dp'))
- param_grad: float32 [2, 7088128], P('section', 'group')
Inputs may be any that keep to these rules, and one draw needn't show every extreme that they name: `segments`: each packed row holds 5 images numbered 0 to 4 with exactly 49 positions each, in any order of positions; all other positions carry the number 5. The positions of one image have distinct slots; positions numbered 5 have slot 0. `params`: laid out as the first step says.
All inputs are finite; a program needn't handle non-finite values.
Results may differ from a plain program's by a relative error of at most 0.018.
Values may be sent and summed in bfloat16 or wider, within the bound.
No kernel may reach another device: no remote copies, remote signals or barrier semaphores. Data moves between devices by JAX's collectives and lax.ppermute only.
A program may use at most 384 MiB of HBM per device.

v0:
```python
from functools import partial
import math

import jax
import jax.numpy as jnp
import numpy as np
from jax import lax
from jax.experimental import pallas as pl
from jax.experimental.pallas import tpu as pltpu
from jax.sharding import PartitionSpec as P

WIDTH = 768
HEADS = 12
HIDDEN_SIZE = 3072
DEC_WIDTH = 512
DEC_HEADS = 16
DEC_HIDDEN = 2048
SLOTS = 196
IMAGES_ROW = 5
ROW = 256
PARAMS = 7088128
LANES = 128
SEC, GRP, DP = "section", "group", "dp"
(
    N1G, N1B, QKV_W, QB, VB, PROJ_W, PB, N2G,
) = range(0, 8)
(
    N2B, UP_W, UB, DOWN_W, DB, EMBED_W, EB, MT,
) = range(8, 16)
(
    POS, QKV_B, VECS, SENT, H1, QKV, PROBS, ATT,
) = range(16, 24)
(
    MID, H2, ACT, SLOPE, OUT, QKV_L, PROJ_L, UP_L,
) = range(24, 32)
(
    EMBED_L, GSENT, GPOS,
) = range(32, 35)
SLOT_PAD = 208
VMEM_BYTES = 60 * 1024 * 1024

norm_eps = 1e-06
masked_score = -1000000000.0
f32 = jnp.float32
bf16 = jnp.bfloat16


def block_layout(width, hidden):
    return [
        (N1G, (width,)),
        (N1B, (width,)),
        (QKV_W, (width, 3 * width)),
        (QB, (width,)),
        (VB, (width,)),
        (PROJ_W, (width, width)),
        (PB, (width,)),
        (N2G, (width,)),
        (N2B, (width,)),
        (UP_W, (width, hidden)),
        (UB, (hidden,)),
        (DOWN_W, (hidden, width)),
        (DB, (width,)),
    ]


def decoder_layout(enc_width, width, hidden, slot_count):
    return [
        (EMBED_W, (enc_width, width)),
        (EB, (width,)),
        (MT, (width,)),
        (POS, (slot_count, width)),
    ] + block_layout(width, hidden)


ENC_LAYOUT = block_layout(WIDTH, HIDDEN_SIZE)
DEC_LAYOUT = decoder_layout(WIDTH, DEC_WIDTH, DEC_HIDDEN, SLOTS)
VEC = {
    N1G: 0,
    N1B: 1,
    QKV_B: 2,
    PB: 3,
    N2G: 4,
    N2B: 5,
    UB: 6,
    DB: 7,
    EB: 8,
    MT: 9,
}
VEC_ROWS = 16


def dot(a, b):
    return lax.dot_general(a, b, (((1,), (0,)), ((), ())), preferred_element_type=f32)


def dot_nt(a, b):
    return lax.dot_general(a, b, (((1,), (1,)), ((), ())), preferred_element_type=f32)


def dot_tn(a, b):
    return lax.dot_general(a, b, (((0,), (0,)), ((), ())), preferred_element_type=f32)


def normalised(values):
    centered = values - jnp.mean(values, axis=-1, keepdims=True)
    inverse = lax.rsqrt(jnp.mean(centered * centered, axis=-1, keepdims=True) + norm_eps)
    return centered * inverse, inverse


def norm_back(grad, hat, inverse, gain):
    scaled = grad * gain
    first = jnp.mean(scaled, axis=-1, keepdims=True)
    second = jnp.mean(scaled * hat, axis=-1, keepdims=True)
    return inverse * (scaled - first - hat * second)


def col_sum(values):
    return jnp.sum(values, axis=0, keepdims=True)


def gelu_parts(upward):
    half = 0.5 + 0.5 * lax.erf(upward * f32(math.sqrt(0.5)))
    slope = half + upward * (jnp.exp(upward * upward * f32(-0.5)) * f32(1.0 / math.sqrt(2.0 * math.pi)))
    return upward * half, slope


def head_mask(head, head_dim):
    lane = lax.broadcasted_iota(jnp.int32, (1, LANES), 1)
    return jnp.where(lane // head_dim == head, 1.0, 0.0).astype(bf16)


def lane_block(group, start=0):
    return pl.ds(pl.multiple_of(start + group * LANES, LANES), LANES)


def flip(values):
    return values.astype(f32).T.astype(bf16)


def attention_forward(qkv_ref, probs_ref, joined_ref, width, heads, keep):
    head_dim = width // heads
    scale = f32(head_dim ** (-0.5))
    per_group = LANES // head_dim

    def one_group(group, carry):
        queries = qkv_ref[:, lane_block(group)]
        keys = qkv_ref[:, lane_block(group, width)]
        values_t = flip(qkv_ref[:, lane_block(group, 2 * width)])
        for sub in range(per_group):
            scores = dot_nt(keys, queries * head_mask(sub, head_dim)) * scale
            scores = keep(scores)
            expo = jnp.exp(scores - jnp.max(scores, axis=0, keepdims=True))
            probs = expo * (1.0 / col_sum(expo))
            probs_ref[group * per_group + sub] = probs
            rows = pl.ds(pl.multiple_of(group * LANES + sub * head_dim, head_dim), head_dim)
            joined_ref[rows, :] = dot(
                values_t[sub * head_dim : (sub + 1) * head_dim], probs.astype(bf16)
            )
        return carry

    lax.fori_loop(0, width // LANES, one_group, 0)


def attention_backward(qkv_ref, probs_ref, grad_ref, low_ref, width, heads):
    head_dim = width // heads
    scale = f32(head_dim ** (-0.5))
    per_group = LANES // head_dim

    def one_group(group, carry):
        queries = qkv_ref[:, lane_block(group)]
        keys = qkv_ref[:, lane_block(group, width)]
        values = qkv_ref[:, lane_block(group, 2 * width)]
        grads = grad_ref[:, lane_block(group)]
        keys_t = flip(keys)
        grad_values = jnp.zeros(values.shape, f32)
        grad_keys = jnp.zeros(values.shape, f32)
        grad_queries = []
        for sub in range(per_group):
            mask = head_mask(sub, head_dim)
            probs = probs_ref[group * per_group + sub]
            own = grads * mask
            grad_values += dot(probs.astype(bf16), own)
            grad_probs = dot_nt(values, own)
            delta = col_sum(probs * grad_probs)
            low = (probs * (grad_probs - delta)).astype(bf16)
            grad_keys += dot(low, queries * mask)
            grad_queries.append(dot(keys_t[sub * head_dim : (sub + 1) * head_dim], low))
        low_ref[:, lane_block(group)] = (jnp.concatenate(grad_queries, axis=0).T * scale).astype(bf16)
        low_ref[:, lane_block(group, width)] = (grad_keys * scale).astype(bf16)
        low_ref[:, lane_block(group, 2 * width)] = grad_values.astype(bf16)
        return carry

    lax.fori_loop(0, width // LANES, one_group, 0)


def encode_kernel(
    x_ref, seg_row_ref, seg_col_ref, qkv_w, proj_w, up_w, down_w, vec,
    sent_ref, normed1_ref, qkv_ref, probs_ref, attended_ref, middle_ref, normed2_ref, active_ref,
    slope_ref, joined_ref,
):
    width, hidden = WIDTH, HIDDEN_SIZE
    inputs = x_ref[...].astype(f32)
    hat, _ = normalised(inputs)
    normed1 = (hat * vec[0:1, :width] + vec[1:2, :width]).astype(bf16)
    normed1_ref[...] = normed1
    qkv_ref[...] = (dot(normed1, qkv_w[...]) + vec[2:3, : 3 * width]).astype(bf16)
    allowed = seg_col_ref[...] == seg_row_ref[...]
    attention_forward(
        qkv_ref, probs_ref, joined_ref, width, HEADS,
        lambda scores: jnp.where(allowed, scores, f32(masked_score)),
    )
    attended = joined_ref[...].T.astype(bf16)
    attended_ref[...] = attended
    middle = inputs + (dot(attended, proj_w[...]) + vec[3:4, :width])
    middle_ref[...] = middle
    hat, _ = normalised(middle)
    normed2_ref[...] = (hat * vec[4:5, :width] + vec[5:6, :width]).astype(bf16)
    joined_ref[...] = jnp.zeros_like(joined_ref)
    total = jnp.zeros((inputs.shape[0], width), f32)
    part = 512
    for start in range(0, hidden, part):
        cols = slice(start, start + part)
        upward = dot(normed2_ref[...], up_w[:, cols]) + vec[6:7, cols]
        active, slope = gelu_parts(upward)
        active_ref[:, cols] = active.astype(bf16)
        slope_ref[:, cols] = slope.astype(slope_ref.dtype)
        total += dot(active_ref[:, cols], down_w[cols, :])
    sent_ref[...] = (middle + (total + vec[7:8, :width])).astype(bf16)


def encode_back_kernel(
    grad_ref, x_ref, qkv_ref, probs_ref, middle_ref, slope_ref, qkv_w, proj_w, up_w, down_w, vec,
    in_grad_ref, qkv_low_ref, proj_low_ref, up_low_ref, vec_grad, grad_att_ref,
):
    width, hidden = WIDTH, HIDDEN_SIZE
    grad_out = grad_ref[...]
    vec_grad[...] = jnp.zeros_like(vec_grad)
    vec_grad[7:8, :width] = col_sum(grad_out.astype(f32))
    grad_normed2 = jnp.zeros((grad_out.shape[0], width), f32)
    part = 512
    for start in range(0, hidden, part):
        cols = slice(start, start + part)
        low = (dot_nt(grad_out, down_w[cols, :]) * slope_ref[:, cols]).astype(bf16)
        up_low_ref[:, cols] = low
        vec_grad[6:7, cols] = col_sum(low.astype(f32))
        grad_normed2 += dot_nt(low, up_w[:, cols])
    hat, inverse = normalised(middle_ref[...])
    vec_grad[4:5, :width] = col_sum(grad_normed2 * hat)
    vec_grad[5:6, :width] = col_sum(grad_normed2)
    grad_middle = grad_out.astype(f32) + norm_back(grad_normed2, hat, inverse, vec[4:5, :width])
    proj_low = grad_middle.astype(bf16)
    proj_low_ref[...] = proj_low
    vec_grad[3:4, :width] = col_sum(proj_low.astype(f32))
    grad_att_ref[...] = dot_nt(proj_low, proj_w[...]).astype(bf16)
    attention_backward(qkv_ref, probs_ref, grad_att_ref, qkv_low_ref, width, HEADS)
    qkv_low = qkv_low_ref[...]
    vec_grad[2:3, : 3 * width] = col_sum(qkv_low.astype(f32))
    grad_normed1 = dot_nt(qkv_low, qkv_w[...])
    hat, inverse = normalised(x_ref[...].astype(f32))
    vec_grad[0:1, :width] = col_sum(grad_normed1 * hat)
    vec_grad[1:2, :width] = col_sum(grad_normed1)
    in_grad_ref[...] = grad_middle + norm_back(grad_normed1, hat, inverse, vec[0:1, :width])


def decode_kernel(
    sent_ref, embed_w, qkv_w, proj_w, up_w, down_w, vec, pos_ref,
    seg_row, slot_row, seg_col, slot_col, cot_ref,
    out_ref, normed1_ref, qkv_low_ref, attended_ref, proj_low_ref, normed2_ref, up_low_ref,
    active_ref, embed_low_ref, grad_sent_ref, vec_grad, pos_grad,
    embedded_ref, embed_sum, qkv_ref, probs_ref, joined_ref, grad_att_ref,
):
    width, hidden = DEC_WIDTH, DEC_HIDDEN
    image = pl.program_id(0)
    length = SLOT_PAD

    @pl.when(image == 0)
    def _():
        embedded_ref[...] = (dot(sent_ref[...], embed_w[...]) + vec[8:9, :width]).astype(bf16)
        vec_grad[...] = jnp.zeros_like(vec_grad)
        pos_grad[...] = jnp.zeros_like(pos_grad)
        embed_sum[...] = jnp.zeros_like(embed_sum)

    def add_vec(row, values):
        vec_grad[row : row + 1, : values.shape[1]] += values

    place = lax.broadcasted_iota(jnp.int32, (length, ROW), 0)
    match = (seg_row[...] == image) & (slot_row[...] == place)
    onehot = jnp.where(match, 1.0, 0.0)
    free = 1.0 - jnp.sum(onehot, axis=1, keepdims=True)
    x = dot(onehot.astype(bf16), embedded_ref[...]) + free * vec[9:10, :width] + pos_ref[...].astype(f32)
    hat1, inverse1 = normalised(x)
    normed1 = (hat1 * vec[0:1, :width] + vec[1:2, :width]).astype(bf16)
    normed1_ref[...] = normed1
    qkv_ref[...] = (dot(normed1, qkv_w[...]) + vec[2:3, : 3 * width]).astype(bf16)
    key_place = lax.broadcasted_iota(jnp.int32, (length, length), 0)
    attention_forward(
        qkv_ref, probs_ref, joined_ref, width, DEC_HEADS,
        lambda scores: jnp.where(key_place < SLOTS, scores, f32(-1e30)),
    )
    attended = joined_ref[...].T.astype(bf16)
    attended_ref[...] = attended
    middle = x + (dot(attended, proj_w[...]) + vec[3:4, :width])
    hat2, inverse2 = normalised(middle)
    normed2 = (hat2 * vec[4:5, :width] + vec[5:6, :width]).astype(bf16)
    normed2_ref[...] = normed2
    cot = cot_ref[...]
    add_vec(7, col_sum(cot.astype(f32)))
    total = jnp.zeros((length, width), f32)
    grad_normed2 = jnp.zeros((length, width), f32)
    part = 512
    for start in range(0, hidden, part):
        cols = slice(start, start + part)
        upward = dot(normed2_ref[...], up_w[:, cols]) + vec[6:7, cols]
        active, slope = gelu_parts(upward)
        active = active.astype(bf16)
        active_ref[:, cols] = active
        total += dot(active, down_w[cols, :])
        low = (dot_nt(cot_ref[...], down_w[cols, :]) * slope).astype(bf16)
        up_low_ref[:, cols] = low
        vec_grad[6:7, cols] += col_sum(low.astype(f32))
        grad_normed2 += dot_nt(low, up_w[:, cols])
    out_ref[...] = (middle + (total + vec[7:8, :width])).astype(bf16)

    add_vec(4, col_sum(grad_normed2 * hat2))
    add_vec(5, col_sum(grad_normed2))
    grad_middle = cot.astype(f32) + norm_back(grad_normed2, hat2, inverse2, vec[4:5, :width])
    proj_low = grad_middle.astype(bf16)
    proj_low_ref[...] = proj_low
    add_vec(3, col_sum(proj_low.astype(f32)))
    grad_att_ref[...] = dot_nt(proj_low, proj_w[...]).astype(bf16)
    attention_backward(qkv_ref, probs_ref, grad_att_ref, qkv_low_ref, width, DEC_HEADS)
    qkv_low = qkv_low_ref[...]
    add_vec(2, col_sum(qkv_low.astype(f32)))
    grad_normed1 = dot_nt(qkv_low, qkv_w[...])
    add_vec(0, col_sum(grad_normed1 * hat1))
    add_vec(1, col_sum(grad_normed1))
    grad_in = grad_middle + norm_back(grad_normed1, hat1, inverse1, vec[0:1, :width])
    low_in = grad_in.astype(bf16)
    wide = low_in.astype(f32)
    add_vec(9, col_sum(free * wide))
    pos_grad[...] += wide
    place_t = lax.broadcasted_iota(jnp.int32, (ROW, length), 1)
    match_t = (seg_col[...] == image) & (slot_col[...] == place_t)
    embed_sum[...] += dot(jnp.where(match_t, 1.0, 0.0).astype(bf16), low_in)

    @pl.when(image == IMAGES_ROW - 1)
    def _():
        embed_low = embed_sum[...].astype(bf16)
        embed_low_ref[...] = embed_low
        add_vec(8, col_sum(embed_low.astype(f32)))
        grad_sent_ref[...] = dot_nt(embed_low, embed_w[...]).astype(bf16)


def params_of(**extra):
    return pltpu.CompilerParams(vmem_limit_bytes=VMEM_BYTES, **extra)


def shape(dims, kind):
    return jax.ShapeDtypeStruct(dims, kind)


def encode(x, seg, weights):
    width, hidden, length = WIDTH, HIDDEN_SIZE, ROW
    names = [QKV_W, PROJ_W, UP_W, DOWN_W, VECS]
    return pl.pallas_call(
        encode_kernel,
        out_shape=[
            shape((length, width), bf16),
            shape((length, width), bf16),
            shape((length, 3 * width), bf16),
            shape((HEADS, length, length), f32),
            shape((length, width), bf16),
            shape((length, width), f32),
            shape((length, width), bf16),
            shape((length, hidden), bf16),
            shape((length, hidden), bf16),
        ],
        scratch_shapes=[pltpu.VMEM((width, length), f32)],
        compiler_params=params_of(),
        name="encode",
    )(x, seg.reshape(1, length), seg.reshape(length, 1), *[weights[n] for n in names])


def encode_back(grad, x, saved, weights):
    width, hidden, length = WIDTH, HIDDEN_SIZE, ROW
    names = [QKV_W, PROJ_W, UP_W, DOWN_W, VECS]
    return pl.pallas_call(
        encode_back_kernel,
        out_shape=[
            shape((length, width), f32),
            shape((length, 3 * width), bf16),
            shape((length, width), bf16),
            shape((length, hidden), bf16),
            shape((VEC_ROWS, hidden), f32),
        ],
        scratch_shapes=[pltpu.VMEM((length, width), bf16)],
        compiler_params=params_of(),
        name="encode_back",
    )(grad, x, saved[QKV], saved[PROBS], saved[MID], saved[SLOPE], *[weights[n] for n in names])


def decode(sent, seg, slot, cot, weights):
    width, hidden, length = DEC_WIDTH, DEC_HIDDEN, SLOT_PAD
    names = [EMBED_W, QKV_W, PROJ_W, UP_W, DOWN_W, VECS, POS]
    held = [sent] + [weights[n] for n in names]
    held += [seg.reshape(1, ROW), slot.reshape(1, ROW), seg.reshape(ROW, 1), slot.reshape(ROW, 1)]

    def whole(array):
        return pl.BlockSpec(array.shape, lambda i: (0,) * array.ndim, pipeline_mode=pl.Buffered(1))

    def image(cols):
        return pl.BlockSpec((length, cols), lambda i: (i, 0))

    rows = IMAGES_ROW * length
    per_image = [width, width, 3 * width, width, width, width, hidden, hidden]
    kept = [
        shape((ROW, width), bf16),
        shape((ROW, WIDTH), bf16),
        shape((VEC_ROWS, hidden), f32),
        shape((length, width), f32),
    ]
    return pl.pallas_call(
        decode_kernel,
        grid=(IMAGES_ROW,),
        in_specs=[whole(a) for a in held] + [image(width)],
        out_specs=[image(c) for c in per_image]
        + [pl.BlockSpec(s.shape, lambda i: (0, 0)) for s in kept],
        out_shape=[shape((rows, c), bf16) for c in per_image] + kept,
        scratch_shapes=[
            pltpu.VMEM((ROW, width), bf16),
            pltpu.VMEM((ROW, width), f32),
            pltpu.VMEM((length, 3 * width), bf16),
            pltpu.VMEM((DEC_HEADS, length, length), f32),
            pltpu.VMEM((width, length), f32),
            pltpu.VMEM((length, width), bf16),
        ],
        compiler_params=params_of(dimension_semantics=("arbitrary",)),
        name="decode",
    )(*held, cot)


def rows_of(extent):
    return math.prod(extent) // LANES


def up_to(value, step):
    return -(-value // step) * step


def flat_starts(layout):
    starts, here = {}, 0
    for name, extent in layout:
        starts[name] = here
        here += rows_of(extent)
    return starts, here


def kept_starts(layout):
    starts, here = {}, 0
    for name, extent in layout:
        starts[name] = here
        here += up_to(rows_of(extent), 16)
    return starts, here


class Plan:
    def __init__(self, mesh_shape):
        self.ns, self.ng, self.nd = (mesh_shape[a] for a in (SEC, GRP, DP))
        self.ny = self.nd // 2
        self.chunk = PARAMS // LANES // self.ng
        self.pieces = self.ns * self.nd
        self.piece = up_to(-(-self.chunk // self.pieces), 64)
        self.half = self.piece // 2
        self.room = self.piece * self.pieces
        self.units = 2 * self.pieces
        self.full = self.ng // 2
        self.dec_rows = flat_starts(DEC_LAYOUT)[1]
        self.rest = self.dec_rows - self.full * self.chunk
        self.rest_room = up_to(self.rest + 80, 16)
        assert 0 < self.rest <= self.chunk and self.rest_room <= self.half + self.chunk
        self.enc_keep, self.enc_kept = kept_starts(ENC_LAYOUT)
        self.dec_keep, self.dec_kept = kept_starts(DEC_LAYOUT)
        self.enc_starts = [self.kept_row(ENC_LAYOUT, z * self.chunk) // 16 * 16 for z in range(self.ng)]
        self.dec_starts = [self.kept_row(DEC_LAYOUT, z * self.chunk) // 16 * 16 for z in range(self.full)]
        self.rest_start = self.kept_row(DEC_LAYOUT, self.full * self.chunk) // 16 * 16
        for z in range(self.ng):
            last = self.kept_row(ENC_LAYOUT, min((z + 1) * self.chunk, flat_starts(ENC_LAYOUT)[1]) - 1)
            assert last < self.enc_starts[z] + self.room
        for z in range(self.full):
            last = self.kept_row(DEC_LAYOUT, (z + 1) * self.chunk - 1)
            assert last < self.dec_starts[z] + self.room
        assert self.dec_kept <= self.rest_start + self.rest_room
        self.enc_table = self.enc_starts[-1] + self.room
        self.dec_table = max(self.dec_starts[-1] + self.room, self.rest_start + self.rest_room)

    def kept_row(self, layout, flat_row):
        flat, _ = flat_starts(layout)
        kept, _ = kept_starts(layout)
        for name, extent in layout:
            if flat_row < flat[name] + rows_of(extent):
                return kept[name] + flat_row - flat[name]
        return kept[name] + rows_of(extent)

    def ranges(self, first, count, cut, chunks):
        found = []
        whole = self.chunk // cut * cut
        while count:
            z, row = divmod(first, self.chunk)
            if z >= chunks:
                here, room = chunks * self.room + row, count
            elif row < whole:
                here, room = z * self.room + row, whole - row
            else:
                here, room = z * self.room + row + cut - (self.chunk - whole), self.chunk - row
            take = min(count, room)
            found.append((here, take))
            first, count = first + take, count - take
        return found

    def segments(self):
        count = len(DEC_LAYOUT) + 1
        table = np.zeros((self.ns, self.ng, count, 3), np.int32)
        for s, layout in enumerate((ENC_LAYOUT, DEC_LAYOUT)):
            flat, used = flat_starts(layout)
            for z in range(self.ng):
                low, high = z * self.chunk, (z + 1) * self.chunk
                if s == 0:
                    base = -self.enc_starts[z]
                elif z < self.full:
                    base = -self.dec_starts[z]
                else:
                    base = self.room - self.rest_start
                for k, (name, extent) in enumerate(layout):
                    first, last = max(flat[name], low), min(flat[name] + rows_of(extent), high)
                    if first < last:
                        table[s, z, k] = (
                            base + self.kept_row(layout, first), first - low, -(-(last - first) // 8),
                        )
                if used < high:
                    table[s, z, count - 1] = (self.room + self.rest_room, max(used - low, 0), 1)
        return table


def widen_block(held, wide, spare, ranges):
    def load(start, count):
        first = start // 16 * 16
        size = up_to(start + count - first, 16)
        return held[first : first + size, :].astype(f32), size, start - first

    if len(ranges) == 1:
        block, size, skip = load(*ranges[0])
        wide[0:size, :] = block
        return skip
    here = 0
    for start, count in ranges:
        block, size, skip = load(start, count)
        spare[0:size, :] = block
        wide[here : here + count, :] = spare[skip : skip + count, :]
        here += count
    return 0


def unpack_kernel(plan, layout, unit, cut, chunks, counts, place_ref, *refs):
    sources = refs[: len(counts)]
    refs = refs[len(counts) :]
    rest = None
    if chunks < plan.ng:
        rest, refs = refs[0], refs[1:]
    matrices = [(n, e) for n, e in layout if len(e) == 2]
    outs, vec = refs[: len(matrices)], refs[len(matrices)]
    held, wide, spare, sems = refs[len(matrices) + 1 :]
    per_chunk = plan.room // unit
    number = 0
    for source, count in zip(sources, counts):
        for k in range(count):
            slot = place_ref[number]
            number += 1
            target = held.at[pl.ds(pl.multiple_of(slot * unit, 16), unit), :]
            pltpu.make_async_copy(source.at[pl.ds(k * unit, unit), :], target, sems.at[slot // per_chunk]).start()
    if rest is not None:
        target = held.at[pl.ds(chunks * plan.room, rest.shape[0]), :]
        pltpu.make_async_copy(rest, target, sems.at[chunks]).start()
    arrived = set()

    def arrive(ranges):
        for start, count in ranges:
            z = min(start // plan.room, chunks)
            if z not in arrived:
                arrived.add(z)
                rows = plan.room if z < chunks else rest.shape[0]
                part = held.at[pl.ds(z * plan.room, rows), :]
                pltpu.make_async_copy(part, part, sems.at[z]).wait()

    vec[...] = jnp.zeros_like(vec)
    flat, _ = flat_starts(layout)
    by_name = dict(zip([n for n, _ in matrices], outs))
    for name, extent in layout:
        if len(extent) == 2:
            depth, lanes = extent[0], extent[1] // LANES
            step = depth if name == POS else max(128, 2048 // lanes // 128 * 128)
            out = by_name[name]
            if name == POS:
                out[...] = jnp.zeros_like(out)
            for first in range(0, depth, step):
                size = min(step, depth - first)
                ranges = plan.ranges(flat[name] + first * lanes, size * lanes, cut, chunks)
                arrive(ranges)
                skip = widen_block(held, wide, spare, ranges)
                for j in range(lanes):
                    block = wide[pl.ds(skip + j, size, stride=lanes), :].astype(bf16)
                    out[first : first + size, j * LANES : (j + 1) * LANES] = block
        else:
            lanes = extent[0] // LANES
            ranges = plan.ranges(flat[name], lanes, cut, chunks)
            arrive(ranges)
            skip = widen_block(held, wide, spare, ranges)
            row, shift = {QB: (2, 0), VB: (2, 2 * extent[0])}.get(name, (VEC.get(name), 0))
            for j in range(lanes):
                vec[row : row + 1, shift + j * LANES : shift + (j + 1) * LANES] = wide[skip + j : skip + j + 1, :]
    for z in range(chunks + (rest is not None)):
        if z not in arrived:
            arrive([(z * plan.room, 1)])


def unpack(plan, layout, unit, cut, chunks, place, sources, rest=None):
    matrices = [(n, e) for n, e in layout if len(e) == 2]
    outs = [
        shape((SLOT_PAD if n == POS else e[0], e[1]), bf16) for n, e in matrices
    ] + [shape((VEC_ROWS, 4 * dict(layout)[PB][0]), f32)]
    operands = list(sources) + ([] if rest is None else [rest])
    rows = chunks * plan.room + (0 if rest is None else rest.shape[0])
    result = pl.pallas_call(
        partial(unpack_kernel, plan, layout, unit, cut, chunks, [s.shape[0] // unit for s in sources]),
        in_specs=[pl.BlockSpec(memory_space=pltpu.SMEM)]
        + [pl.BlockSpec(memory_space=pl.ANY)] * len(operands),
        out_shape=outs,
        scratch_shapes=[
            pltpu.VMEM((rows, LANES), bf16),
            pltpu.VMEM((3200, LANES), f32),
            pltpu.VMEM((3200, LANES), f32),
            pltpu.SemaphoreType.DMA((chunks + 1,)),
        ],
        compiler_params=params_of(),
        name="unpack",
    )(place, *operands)
    return dict(zip([n for n, _ in matrices] + [VECS], result))


def pack_kernel(layout, names, *refs):
    pairs = {}
    for name in names:
        pairs[name], refs = refs[:2], refs[2:]
    vec, refs = refs[0], refs[1:]
    pos = None
    if POS in dict(layout):
        pos, refs = refs[0], refs[1:]
    table, wide, stage, small, sems, small_sem = refs
    kept, _ = kept_starts(layout)
    extents = dict(layout)
    step = 128
    for name in names:
        left, right = pairs[name]
        depth, width = extents[name]
        lanes = width // LANES
        rows = step * lanes

        def copy(index, slot, rows=rows, name=name):
            start = pl.multiple_of(kept[name] + index * rows, 16)
            return pltpu.make_async_copy(
                stage.at[slot, pl.ds(0, rows), :], table.at[pl.ds(start, rows), :], sems.at[slot]
            )

        def one(index, carry, left=left, right=right, width=width, lanes=lanes, rows=rows, copy=copy):
            slot = lax.rem(index, 2)
            columns = flip(left[:, pl.ds(pl.multiple_of(index * step, step), step)])
            part = 256
            for first in range(0, width, part):
                block = dot(columns, right[:, first : first + part])
                for j in range(part // LANES):
                    wide[pl.ds(first // LANES + j, step, stride=lanes), :] = block[:, j * LANES : (j + 1) * LANES]

            @pl.when(index >= 2)
            def _():
                copy(index - 2, slot).wait()

            stage[slot, 0:rows, :] = wide[0:rows, :].astype(bf16)
            copy(index, slot).start()
            return carry

        count = depth // step
        lax.fori_loop(0, count, one, 0)
        for index in range(max(count - 2, 0), count):
            copy(index, index % 2).wait()
    here = 0
    copies = []
    for name, extent in layout:
        if len(extent) == 2 and name != POS:
            continue
        rows = rows_of(extent)
        room = up_to(rows, 16)
        wide[0:room, :] = jnp.zeros((room, LANES), f32)
        if name == POS:
            lanes = extent[1] // LANES
            for j in range(lanes):
                wide[pl.ds(j, extent[0], stride=lanes), :] = pos[0 : extent[0], j * LANES : (j + 1) * LANES]
        else:
            row, shift = {QB: (2, 0), VB: (2, 2 * extent[0])}.get(name, (VEC.get(name), 0))
            for j in range(rows):
                wide[j : j + 1, :] = vec[row : row + 1, shift + j * LANES : shift + (j + 1) * LANES]
        small[here : here + room, :] = wide[0:room, :].astype(bf16)
        copies.append(
            pltpu.make_async_copy(
                small.at[pl.ds(here, room), :], table.at[pl.ds(kept[name], room), :], small_sem.at[0]
            )
        )
        here += room
    for each in copies:
        each.start()
    pltpu.make_async_copy(small, small, small_sem.at[0]).wait()


def pack(layout, table_rows, pairs, vec, pos=None):
    names = list(pairs)
    operands = [a for name in names for a in pairs[name]] + [vec] + ([] if pos is None else [pos])
    small = sum(
        up_to(rows_of(e), 16) for n, e in layout if len(e) == 1 or n == POS
    )
    most = 128 * max(e[1] for n, e in layout if len(e) == 2) // LANES
    return pl.pallas_call(
        partial(pack_kernel, layout, names),
        in_specs=[pl.BlockSpec(memory_space=pltpu.VMEM)] * len(operands),
        out_specs=pl.BlockSpec(memory_space=pl.ANY),
        out_shape=shape((table_rows, LANES), bf16),
        scratch_shapes=[
            pltpu.VMEM((most, LANES), f32),
            pltpu.VMEM((2, most, LANES), bf16),
            pltpu.VMEM((small, LANES), bf16),
            pltpu.SemaphoreType.DMA((2,)),
            pltpu.SemaphoreType.DMA((1,)),
        ],
        compiler_params=params_of(),
        name="pack",
    )(*operands)


def finish_kernel(plan, counts, place_ref, seg_ref, *refs):
    sources, rest, out, held, wide, sem = refs[: len(counts)], *refs[len(counts) :]
    unit = plan.half
    number = 0
    for source, count in zip(sources, counts):
        for k in range(count):
            target = held.at[pl.ds(pl.multiple_of(place_ref[number] * unit, 16), unit), :]
            number += 1
            pltpu.make_async_copy(source.at[pl.ds(k * unit, unit), :], target, sem.at[0]).start()
    pltpu.make_async_copy(rest, held.at[pl.ds(plan.room, plan.rest_room), :], sem.at[0]).start()
    out[...] = jnp.zeros_like(out)
    pltpu.make_async_copy(held, held, sem.at[0]).wait()
    total = plan.room + plan.rest_room
    wide[total : total + 16, :] = jnp.zeros((16, LANES), f32)
    wide[0:total, :] = held[...].astype(f32)

    def one(k, carry):
        source, first, steps = seg_ref[3 * k], seg_ref[3 * k + 1], seg_ref[3 * k + 2]

        def step(i, carry):
            out[pl.ds(first + 8 * i, 8), :] = wide[pl.ds(source + 8 * i, 8), :]
            return carry

        def steps8(i, carry):
            out[pl.ds(first + 64 * i, 64), :] = wide[pl.ds(source + 64 * i, 64), :]
            return carry

        many = steps // 8
        lax.fori_loop(0, many, steps8, 0)
        return lax.fori_loop(many * 8, steps, step, carry)

    lax.fori_loop(0, seg_ref.shape[0] // 3, one, 0)


def finish(plan, place, segments, sources, rest):
    total = plan.room + plan.rest_room
    return pl.pallas_call(
        partial(finish_kernel, plan, [s.shape[0] // plan.half for s in sources]),
        in_specs=[pl.BlockSpec(memory_space=pltpu.SMEM)] * 2
        + [pl.BlockSpec(memory_space=pl.ANY)] * (len(sources) + 1),
        out_shape=shape((up_to(plan.chunk, 8) + 8, LANES), f32),
        scratch_shapes=[
            pltpu.VMEM((total, LANES), bf16),
            pltpu.VMEM((total + 16, LANES), f32),
            pltpu.SemaphoreType.DMA((1,)),
        ],
        compiler_params=params_of(),
        name="finish",
    )(place, segments, *sources, rest)


def per_device(plan, enc_input, segments, slots, params, cot):
    ns, ng, nd, ny = plan.ns, plan.ng, plan.nd, plan.ny
    piece, half, room, chunk = plan.piece, plan.half, plan.room, plan.chunk
    sec = lax.axis_index(SEC)
    grp = lax.axis_index(GRP)
    dp = lax.axis_index(DP)
    yy, core = dp // 2, dp % 2
    first_section = sec == 0

    def over_x(block):
        return lax.ppermute(block, SEC, [(0, 1), (1, 0)])

    def over_core(block):
        return lax.ppermute(block, DP, [(d, d ^ 1) for d in range(nd)])

    def over_y(block):
        return lax.ppermute(block, DP, [(d, (d + 2) % nd) for d in range(nd)])

    def over_z(block):
        return lax.ppermute(block, GRP, [(g, (g + 1) % ng) for g in range(ng)])

    def share(start):
        cut = lax.dynamic_slice(params, (0, start * LANES), (1, half * LANES))
        return cut.astype(f32).reshape(half, LANES).astype(bf16)

    def shares(section):
        number = section * nd + dp
        enc_first = jnp.minimum(number * piece, chunk - piece)
        dec_first = [jnp.minimum((h * plan.pieces + number) * half, chunk - half) for h in range(2)]
        starts = [
            jnp.where(first_section, enc_first, dec_first[0]),
            jnp.where(first_section, enc_first + half, dec_first[1]),
        ]
        return jnp.concatenate([share(s) for s in starts])

    keep = shares(sec)
    got = over_x(shares(1 - sec))
    enc_piece = jnp.where(first_section, keep, got)
    dec_pieces = jnp.where(first_section, got, keep)
    spread = [
        lax.ppermute(dec_pieces[h * half : (h + 1) * half], GRP, [(z, 2 * z + h) for z in range(plan.full)])
        for h in range(2)
    ]
    dec_piece = jnp.where(grp % 2 == 0, spread[0], spread[1])
    holds_rest = jnp.logical_and(sec == 1, grp == plan.full)
    rest_cut = params[:, : plan.rest * LANES].astype(f32).reshape(plan.rest, LANES)
    rest_weights = lax.psum(
        jnp.where(holds_rest, rest_cut, 0.0).astype(bf16), (SEC, GRP)
    )
    rest_weights = jnp.pad(rest_weights, ((0, plan.rest_room - plan.rest), (0, 0)))

    def gather(block):
        size = block.shape[0]
        sources, places = [], []
        here = block
        for step in range(ng):
            own_group = (grp - step) % ng
            number = lambda s, y, c: (own_group * plan.pieces + s * nd + y * 2 + c) * 2
            if ny == 2:
                from_x, from_y = over_x(here), over_y(here)
                corner_0 = over_y(from_x[: size // 2])
                corner_1 = over_x(from_y[size // 2 :])
                all_four = jnp.concatenate([here, from_x, from_y, corner_0, corner_1])
                owners = [(sec, yy), (1 - sec, yy), (sec, 1 - yy), (1 - sec, 1 - yy)]
            else:
                ring = [here]
                for _ in range(ny - 1):
                    ring.append(over_y(ring[-1]))
                column = jnp.concatenate(ring)
                all_four = jnp.concatenate([column, over_x(column)])
                owners = [(s, (yy - k) % ny) for s in (sec, 1 - sec) for k in range(ny)]
            sources += [all_four, over_core(all_four)]
            for c in (core, 1 - core):
                for s, y in owners:
                    places += [number(s, y, c), number(s, y, c) + 1]
            if step < ng - 1:
                here = over_z(here)
        return sources, jnp.stack(places).astype(jnp.int32)

    enc_sources, enc_places = gather(enc_piece)
    dec_sources, dec_places = gather(dec_piece)

    micro_rows = enc_input.reshape(ROW, WIDTH)
    seg = lax.dynamic_index_in_dim(segments, sec, 0, keepdims=False).reshape(ROW)
    slot = lax.dynamic_index_in_dim(slots, sec, 0, keepdims=False).reshape(ROW)
    cot_rows = jnp.pad(
        cot.reshape(IMAGES_ROW, SLOTS, DEC_WIDTH), ((0, 0), (0, SLOT_PAD - SLOTS), (0, 0))
    ).reshape(IMAGES_ROW * SLOT_PAD, DEC_WIDTH)

    enc_weights = unpack(plan, ENC_LAYOUT, half, piece, ng, enc_places, enc_sources)
    saved = dict(
        zip(
            [SENT, H1, QKV, PROBS, ATT, MID, H2, ACT, SLOPE],
            encode(micro_rows, seg, enc_weights),
        )
    )
    dec_weights = unpack(plan, DEC_LAYOUT, half // 2, half, plan.full, dec_places, dec_sources, rest_weights)
    dec = dict(
        zip(
            [OUT, H1, QKV_L, ATT, PROJ_L, H2, UP_L, ACT,
             EMBED_L, GSENT, VECS, GPOS],
            decode(saved[SENT], seg, slot, cot_rows, dec_weights),
        )
    )
    dec_table = pack(
        DEC_LAYOUT,
        plan.dec_table,
        {
            EMBED_W: (saved[SENT], dec[EMBED_L]),
            QKV_W: (dec[H1], dec[QKV_L]),
            PROJ_W: (dec[ATT], dec[PROJ_L]),
            UP_W: (dec[H2], dec[UP_L]),
            DOWN_W: (dec[ACT], cot_rows),
        },
        dec[VECS],
        dec[GPOS],
    )
    in_grad, qkv_low, proj_low, up_low, enc_vec = encode_back(dec[GSENT], micro_rows, saved, enc_weights)
    enc_table = pack(
        ENC_LAYOUT,
        plan.enc_table,
        {
            DOWN_W: (saved[ACT], dec[GSENT]),
            UP_W: (saved[H2], up_low),
            PROJ_W: (saved[ATT], proj_low),
            QKV_W: (saved[H1], qkv_low),
        },
        enc_vec,
    )

    def add(first, *others):
        total = first.astype(f32)
        for other in others:
            total = total + other.astype(f32)
        return total.astype(bf16)

    def reduce(table, starts, length):
        part = length // 2

        def core_half(which):
            return jnp.stack([lax.dynamic_slice(table, (s + which * part, 0), (part, LANES)) for s in starts])

        held = add(core_half(core), over_core(core_half(1 - core)))
        size = part // (2 * ny)

        def owned_by(s, y):
            return lax.dynamic_slice(held, (0, (s * ny + y) * size, 0), (len(starts), size, LANES))

        if ny == 2:
            corner = owned_by(1 - sec, 1 - yy)
            corner_x = over_x(corner[:, : size // 2])
            corner_y = over_y(corner[:, size // 2 :])
            beside_y = owned_by(sec, 1 - yy)
            beside_x = owned_by(1 - sec, yy)
            send_y = jnp.concatenate([add(beside_y[:, : size // 2], corner_x), beside_y[:, size // 2 :]], axis=1)
            send_x = jnp.concatenate([beside_x[:, : size // 2], add(beside_x[:, size // 2 :], corner_y)], axis=1)
            mine = add(owned_by(sec, yy), over_x(send_x), over_y(send_y))
        else:
            column = lambda s: lax.dynamic_slice(held, (0, s * ny * size, 0), (len(starts), ny * size, LANES))
            own = add(column(sec), over_x(column(1 - sec)))
            block = lambda y: lax.dynamic_slice(own, (0, (y % ny) * size, 0), (len(starts), size, LANES))
            mine = block(yy - 1)
            for step in range(ny - 1):
                mine = add(block(yy - 2 - step), over_y(mine))
        one = lambda g: lax.dynamic_index_in_dim(mine, g % ng, 0, keepdims=False)
        total = one(grp - 1)
        for step in range(ng - 1):
            total = add(one(grp - 2 - step), over_z(total))
        return total

    dec_half_starts = [s + h * (room // 2) for s in plan.dec_starts for h in range(2)]
    dec_sum = reduce(dec_table, dec_half_starts, room // 2)
    dec_sums = [
        lax.ppermute(dec_sum, GRP, [(2 * z + h, z) for z in range(plan.full)]) for h in range(2)
    ]
    dec_own = jnp.concatenate(dec_sums)
    rest_sum = lax.psum(
        dec_table[plan.rest_start : plan.rest_start + plan.rest_room], (SEC, GRP, DP)
    )
    enc_own = reduce(enc_table, plan.enc_starts, room)
    own = jnp.where(first_section, enc_own, dec_own)
    other = over_x(jnp.where(first_section, dec_own, enc_own))
    pair = jnp.concatenate([own, other])
    column = [pair]
    for _ in range(ny - 1):
        column.append(over_y(column[-1]))
    sources = column + [over_core(c) for c in column]
    places = []
    for c in (core, 1 - core):
        for k in range(ny):
            for s in (sec, 1 - sec):
                number = (c * 2 + s) * ny + (yy - k) % ny
                places += [
                    jnp.where(first_section, 2 * number, number),
                    jnp.where(first_section, 2 * number + 1, plan.pieces + number),
                ]
    table = jnp.asarray(plan.segments())[sec, grp].reshape(-1)
    flat = finish(plan, jnp.stack(places).astype(jnp.int32), table, sources, rest_sum)
    param_grad = flat.reshape(-1)[: chunk * LANES].reshape(1, chunk * LANES)
    dec_out = dec[OUT].reshape(IMAGES_ROW, SLOT_PAD, DEC_WIDTH)[:, :SLOTS]
    return (
        dec_out.reshape(1, 1, IMAGES_ROW * SLOTS, DEC_WIDTH),
        in_grad.reshape(1, 1, ROW, WIDTH),
        param_grad,
    )


def solution(mesh):
    placed = (
        P(SEC, (GRP, DP), None, None),
        P(None, (GRP, DP), None),
        P(None, (GRP, DP), None),
        P(SEC, GRP),
        P(SEC, (GRP, DP), None, None),
    )
    return jax.shard_map(
        partial(per_device, Plan(dict(mesh.shape))),
        mesh=mesh,
        in_specs=placed,
        out_specs=(
            P(SEC, (GRP, DP), None, None),
            P(SEC, (GRP, DP), None, None),
            P(SEC, GRP),
        ),
        check_vma=False,
    )
```

profile of v0, /device:TPU:1, one launch (start us, length us, event | category | flops | bytes accessed | tf_op | source)
XLA Modules:
  0.0 853.4 jit_solution(147713560024996496)
XLA Ops:
  7.2 6.8 dynamic-slice_reduce_fusion.3
  16.2 10.2 %collective-permute-done = bf16[1792,128]{1,0:T(8,128)(2,1)S(1)} collective-permute-done((bf16[1792,128]{1,0:T(8,128)(2,1)S(1)}, bf16[1792,128]{1,0:T(8,128)(2,1)S(1)}, u32[]{:S(2)}, u32[]{:S(2)}) %collective-permute-start) | collective-permute-done | bytes 458784 | tf_op jit(solution)/shard_map/ppermute | solution.py:807
  28.1 5.7 collective-permute-start.25
  39.3 3.4 collective-permute-start.31
  42.7 6.0 collective-permute-done.26
  52.9 6.8 collective-permute-done.6
  63.8 2.5 collective-permute-done.32
  73.0 4.6 collective-permute-done.35
  78.7 3.8 collective-permute-done.38
  87.6 3.4 collective-permute-done.8
  95.9 7.4 collective-permute-done.45
  104.3 12.3 %collective-permute-start.30 = (bf16[3584,128]{1,0:T(8,128)(2,1)S(1)}, bf16[3584,128]{1,0:T(8,128)(2,1)S(1)}, u32[]{:S(2)}, u32[]{:S(2)}) collective-permute-start(bf16[3584,128]{1,0:T(8,128)(2,1)S(1)} %constant_dynamic-update-slice_fusion.20.refs_0_), channel_id=1, source_target_pairs={{0,1},{1,0},{2,3},{3,2},{4,5},{5,4},{6,7},{7,6},{8,9},{9,8},{10,11... | collective-permute-start | bytes 2752520 | tf_op jit(solution)/shard_map/ppermute | solution.py:810
  122.2 7.6 collective-permute-start.36
  142.7 5.4 collective-permute-start.42
  155.4 2.9 fusion.7
  164.4 62.1 %all-reduce.5.cloned.1.call-done = bf16[800,128]{1,0:T(8,128)(2,1)} async-done(((bf16[800,128]{1,0:T(8,128)(2,1)}), bf16[800,128]{1,0:T(8,128)(2,1)}) %all-reduce.5.cloned.1.call-update) | async-done | bytes 204816 | tf_op jit(solution)/shard_map/psum | solution.py:843
  228.1 10.1 %unpack.3 = (bf16[768,512]{1,0:T(8,128)(2,1)}, bf16[208,512]{1,0:T(8,128)(2,1)}, bf16[512,1536]{1,0:T(8,128)(2,1)}, bf16[512,512]{1,0:T(8,128)(2,1)}, bf16[512,2...) custom-call(s32[64]{0:T(128)} %stack.435.place_ref, bf16[3584,128]{1,0:T(8,128)(2,1)} %copy-done.9, ...), custom_call_target="tpu_custom_call" | custom-call | tf_op jit(solution)/shard_map/unpack/pallas_call | solution.py:632
  238.3 14.3 %unpack.2 = (bf16[768,2304]{1,0:T(8,128)(2,1)}, bf16[768,768]{1,0:T(8,128)(2,1)}, bf16[768,3072]{1,0:T(8,128)(2,1)}, bf16[3072,768]{1,0:T(8,128)(2,1)}, f32[16,3072]{1,0:T(8,128)}) custom-call(s32[64]{0:T(128)} %stack.435.place_ref, bf16[7168,128]{1,0:T(8,128)(2,1)} %constant_dynamic-update-slice_fusion.refs_0_, ...), custom_call_target="tpu_custom_call" | custom-call | tf_op jit(solution)/shard_map/unpack/pallas_call | solution.py:632
  252.6 18.3 %encode.1 = (bf16[256,768]{1,0:T(8,128)(2,1)}, bf16[256,768]{1,0:T(8,128)(2,1)}, bf16[256,2304]{1,0:T(8,128)(2,1)}, f32[12,256,256]{2,1,0:T(8,128)}, bf16[256,76...) custom-call(bf16[256,768]{1,0:T(8,128)(2,1)} %bitcast.164, ...), custom_call_target="tpu_custom_call" | custom-call | tf_op jit(solution)/shard_map/encode/pallas_call | solution.py:365
  270.9 85.2 %decode.1 = (bf16[1040,512]{1,0:T(8,128)(2,1)}, bf16[1040,512]{1,0:T(8,128)(2,1)}, bf16[1040,1536]{1,0:T(8,128)(2,1)}, bf16[1040,512]{1,0:T(8,128)(2,1)}, bf16[1...) custom-call(bf16[256,768]{1,0:T(8,128)(2,1)} %get-tuple-element.46.s, ...), custom_call_target="tpu_custom_call" | custom-call | tf_op jit(solution)/shard_map/decode/pallas_call | solution.py:422
  356.1 18.9 %encode_back.1 = (f32[256,768]{1,0:T(8,128)}, bf16[256,2304]{1,0:T(8,128)(2,1)}, bf16[256,768]{1,0:T(8,128)(2,1)}, bf16[256,3072]{1,0:T(8,128)(2,1)}, f32[16,3072]{1,0:T(8,128)}) custom-call(bf16[256,768]{1,0:T(8,128)(2,1)} %get-tuple-element.55.grad_ref.refs_1_, bf16[256,768]{1,0:T(8,128)(2,1)} %bitcast.165, bf16[256,2304]{1,0:T(8,128)(2,1)} %get-tuple-element.56.qkv_ref, ...), custom_call_target="tpu_custom_call" | custom-call | tf_op jit(solution)/shard_map/encode_back/pallas_call | solution.py:387
  375.0 23.2 %pack.2 = bf16[55936,128]{1,0:T(8,128)(2,1)} custom-call(bf16[256,3072]{1,0:T(8,128)(2,1)} %get-tuple-element.61.refs_0_, bf16[256,768]{1,0:T(8,128)(2,1)} %get-tuple-element.55.grad_ref.refs_1_, bf16[256,768]{1,0:T(8,128)(2,1)} %get-tuple-element.62.refs_2_, bf16[256,3072]{1,0:T(8,128)(2,1)} %get-tuple-element.63.refs_3_, ...), custom_call_target="tpu_custom_call" | custom-call | tf_op jit(solution)/shard_map/pack/pallas_call | solution.py:729
  398.2 8.0 dynamic-slice_bitcast_fusion.7
  406.2 3.6 pad_maximum_fusion
  409.7 2.5 collective-permute-start.49
  412.2 28.3 %pack.3 = bf16[28672,128]{1,0:T(8,128)(2,1)} custom-call(bf16[256,768]{1,0:T(8,128)(2,1)} %get-tuple-element.46.sent_ref.refs_0_, bf16[256,512]{1,0:T(8,128)(2,1)} %get-tuple-element.69.refs_1_, bf16[1040,512]{1,0:T(8,128)(2,1)} %get-tuple-element.70.refs_2_, bf16[1040,1536]{1,0:T(8,128)(2,1)} %get-tuple-element.71.refs_3_, ...), custom_call_target="tpu_custom_call" | custom-call | tf_op jit(solution)/shard_map/pack/pallas_call | solution.py:729
  440.5 4.9 dynamic-slice_bitcast_fusion.15
  447.4 6.7 collective-permute-done.57
  454.2 3.5 add_convert_fusion.1
  458.8 5.0 add_convert_fusion
  471.2 28.1 %collective-permute-done.58 = bf16[4,448,128]{2,1,0:T(8,128)(2,1)} collective-permute-done((bf16[4,448,128]{2,1,0:T(8,128)(2,1)}, bf16[4,448,128]{2,1,0:T(8,128)(2,1)}, u32[]{:S(2)}, u32[]{:S(2)}) %collective-permute-start.58) | collective-permute-done | bytes 458784 | tf_op jit(solution)/shard_map/ppermute | solution.py:813
  503.9 2.5 add_convert_fusion.5
  511.2 12.5 %collective-permute-done.59 = bf16[4,896,128]{2,1,0:T(8,128)(2,1)S(1)} collective-permute-done((bf16[4,896,128]{2,1,0:T(8,128)(2,1)}, bf16[4,896,128]{2,1,0:T(8,128)(2,1)S(1)}, u32[]{:S(2)}, u32[]{:S(2)}) %collective-permute-start.59) | collective-permute-done | bytes 917536 | tf_op jit(solution)/shard_map/ppermute | solution.py:807
  524.7 44.5 %collective-permute-done.61 = bf16[4,896,128]{2,1,0:T(8,128)(2,1)S(1)} collective-permute-done((bf16[4,896,128]{2,1,0:T(8,128)(2,1)S(1)}, bf16[4,896,128]{2,1,0:T(8,128)(2,1)S(1)}, u32[]{:S(2)}, u32[]{:S(2)}) %collective-permute-start.61) | collective-permute-done | bytes 917536 | tf_op jit(solution)/shard_map/ppermute | solution.py:813
  571.1 6.6 collective-permute-done.62
  577.9 3.3 add_convert_fusion.2
  581.4 3.2 collective-permute-done.63
  586.3 8.6 %collective-permute-done.54 = bf16[1792,128]{1,0:T(8,128)(2,1)} collective-permute-done((bf16[1792,128]{1,0:T(8,128)(2,1)S(1)}, bf16[1792,128]{1,0:T(8,128)(2,1)}, u32[]{:S(2)}, u32[]{:S(2)}) %collective-permute-start.54) | collective-permute-done | bytes 458784 | tf_op jit(solution)/shard_map/ppermute | solution.py:816
  596.1 3.7 collective-permute-done.64
  600.6 8.2 collective-permute-done.55
  611.3 17.8 %collective-permute-done.66 = bf16[896,128]{1,0:T(8,128)(2,1)S(1)} collective-permute-done((bf16[896,128]{1,0:T(8,128)(2,1)S(1)}, bf16[896,128]{1,0:T(8,128)(2,1)S(1)}, u32[]{:S(2)}, u32[]{:S(2)}) %collective-permute-start.66) | collective-permute-done | bytes 229408 | tf_op jit(solution)/shard_map/ppermute | solution.py:970
  630.4 10.4 %collective-permute-done.67 = bf16[1792,128]{1,0:T(8,128)(2,1)S(1)} collective-permute-done((bf16[1792,128]{1,0:T(8,128)(2,1)S(1)}, bf16[1792,128]{1,0:T(8,128)(2,1)S(1)}, u32[]{:S(2)}, u32[]{:S(2)}) %collective-permute-start.67) | collective-permute-done | bytes 458784 | tf_op jit(solution)/shard_map/ppermute | solution.py:807
  643.2 18.3 %collective-permute-done.68.refs_1_ = bf16[3584,128]{1,0:T(8,128)(2,1)} collective-permute-done((bf16[3584,128]{1,0:T(8,128)(2,1)S(1)}, bf16[3584,128]{1,0:T(8,128)(2,1)}, u32[]{:S(2)}, u32[]{:S(2)}) %collective-permute-start.68) | collective-permute-done | bytes 917536 | tf_op jit(solution)/shard_map/ppermute | solution.py:813
  661.5 2.4 collective-permute-start.70
  668.8 121.2 %all-reduce.7.cloned.1.call-done.refs_4_ = bf16[880,128]{1,0:T(8,128)(2,1)} async-done(((bf16[880,128]{1,0:T(8,128)(2,1)}), bf16[880,128]{1,0:T(8,128)(2,1)}) %all-reduce.7.cloned.1.call-update) | async-done | bytes 225296 | tf_op jit(solution)/shard_map/psum | solution.py:973
  790.0 8.1 finish.1
  798.0 3.3 slice_bitcast_fusion
  801.4 44.9 %copy.14 = f32[1,1,13844,128]{3,1,2,0:T(1,128)} copy(f32[1,1,13844,128]{3,2,1,0:T(8,128)S(1)} %slice_bitcast_fusion) | data formatting | bytes 14176256
  (245 shorter events, 107.4 us)
Async XLA Ops:
  7.2 219.3 %all-reduce.5.cloned.1.call-start = ((), (), s32[]{:S(2)}) async-start(), calls=%async_computation | async-start | bytes 409600 | tf_op jit(solution)/shard_map/psum | solution.py:843
  14.1 12.4 %collective-permute-start = (bf16[1792,128]{1,0:T(8,128)(2,1)S(1)}, bf16[1792,128]{1,0:T(8,128)(2,1)S(1)}, u32[]{:S(2)}, u32[]{:S(2)}) collective-permute-start(bf16[1792,128]{1,0:T(8,128)(2,1)S(1)} %pad_maximum_fusion.8), channel_id=1, source_target_pairs={{0,16},{16,0},{1,17},{17,1},{2,18},{18,2},{3,19},{19,3},{4,20},{20... | collective-permute-start | bytes 1376264 | tf_op jit(solution)/shard_map/ppermute | solution.py:807
  33.8 17.1 %collective-permute-start.1 = (bf16[1792,128]{1,0:T(8,128)(2,1)S(1)}, bf16[1792,128]{1,0:T(8,128)(2,1)S(1)}, u32[]{:S(2)}, u32[]{:S(2)}) collective-permute-start(bf16[1792,128]{1,0:T(8,128)(2,1)S(1)} %get-tuple-element.86), channel_id=1, source_target_pairs={{0,16},{16,0},{1,17},{17,1},{2,18},{18,2},{3,19},{19,3},{4,20},{20... | collective-permute-start | bytes 1376264 | tf_op jit(solution)/shard_map/ppermute | solution.py:807
  35.1 16.5 %collective-permute-start.2 = (bf16[1792,128]{1,0:T(8,128)(2,1)S(1)}, bf16[1792,128]{1,0:T(8,128)(2,1)S(1)}, u32[]{:S(2)}, u32[]{:S(2)}) collective-permute-start(bf16[1792,128]{1,0:T(8,128)(2,1)S(1)} %get-tuple-element.86), channel_id=1, source_target_pairs={{0,2},{1,3},{2,0},{3,1},{4,6},{5,7},{6,4},{7,5},{8,10},{9,11},{10,... | collective-permute-start | bytes 1376264 | tf_op jit(solution)/shard_map/ppermute | solution.py:813
  36.8 11.9 %collective-permute-start.26 = (bf16[896,128]{1,0:T(8,128)(2,1)S(1)}, bf16[896,128]{1,0:T(8,128)(2,1)S(1)}, u32[]{:S(2)}, u32[]{:S(2)}) collective-permute-start(bf16[896,128]{1,0:T(8,128)(2,1)S(1)} %get-tuple-element.84), channel_id=1, source_target_pairs={{0,16},{16,0},{1,17},{17,1},{2,18},{18,2},{3,19},{19,3},{4,20},{20... | collective-permute-start | bytes 688136 | tf_op jit(solution)/shard_map/ppermute | solution.py:807
  39.3 12.6 %collective-permute-start.31 = (bf16[896,128]{1,0:T(8,128)(2,1)S(1)}, bf16[896,128]{1,0:T(8,128)(2,1)S(1)}, u32[]{:S(2)}, u32[]{:S(2)}) collective-permute-start(bf16[896,128]{1,0:T(8,128)(2,1)S(1)} %get-tuple-element.84), channel_id=1, source_target_pairs={{0,4},{4,8},{8,12},{12,0},{1,5},{5,9},{9,13},{13,1},{2,6},{6,10},{... | collective-permute-start | bytes 688136 | tf_op jit(solution)/shard_map/ppermute | solution.py:816
  49.6 11.7 %collective-permute-start.28 = (bf16[448,128]{1,0:T(8,128)(2,1)S(1)}, bf16[448,128]{1,0:T(8,128)(2,1)S(1)}, u32[]{:S(2)}, u32[]{:S(2)}) collective-permute-start(bf16[448,128]{1,0:T(8,128)(2,1)S(1)} %slice.147), channel_id=1, source_target_pairs={{0,2},{1,3},{2,0},{3,1},{4,6},{5,7},{6,4},{7,5},{8,10},{9,11},{10,... | collective-permute-start | bytes 344072 | tf_op jit(solution)/shard_map/ppermute | solution.py:813
  50.9 11.6 %collective-permute-start.29 = (bf16[448,128]{1,0:T(8,128)(2,1)S(1)}, bf16[448,128]{1,0:T(8,128)(2,1)S(1)}, u32[]{:S(2)}, u32[]{:S(2)}) collective-permute-start(bf16[448,128]{1,0:T(8,128)(2,1)S(1)} %slice.148), channel_id=1, source_target_pairs={{0,16},{16,0},{1,17},{17,1},{2,18},{18,2},{3,19},{19,3},{4,20},{20... | collective-permute-start | bytes 344072 | tf_op jit(solution)/shard_map/ppermute | solution.py:807
  51.6 17.2 %collective-permute-start.3 = (bf16[896,128]{1,0:T(8,128)(2,1)S(1)}, bf16[896,128]{1,0:T(8,128)(2,1)S(1)}, u32[]{:S(2)}, u32[]{:S(2)}) collective-permute-start(bf16[896,128]{1,0:T(8,128)(2,1)S(1)} %slice.137), channel_id=1, source_target_pairs={{0,2},{1,3},{2,0},{3,1},{4,6},{5,7},{6,4},{7,5},{8,10},{9,11},{10,... | collective-permute-start | bytes 688136 | tf_op jit(solution)/shard_map/ppermute | solution.py:813
  51.9 17.9 %collective-permute-start.4 = (bf16[896,128]{1,0:T(8,128)(2,1)S(1)}, bf16[896,128]{1,0:T(8,128)(2,1)S(1)}, u32[]{:S(2)}, u32[]{:S(2)}) collective-permute-start(bf16[896,128]{1,0:T(8,128)(2,1)S(1)} %slice.138), channel_id=1, source_target_pairs={{0,16},{16,0},{1,17},{17,1},{2,18},{18,2},{3,19},{19,3},{4,20},{20... | collective-permute-start | bytes 688136 | tf_op jit(solution)/shard_map/ppermute | solution.py:807
  66.3 20.2 %collective-permute-start.12 = (bf16[1792,128]{1,0:T(8,128)(2,1)S(1)}, bf16[1792,128]{1,0:T(8,128)(2,1)S(1)}, u32[]{:S(2)}, u32[]{:S(2)}) collective-permute-start(bf16[1792,128]{1,0:T(8,128)(2,1)S(1)} %collective-permute-done.6), channel_id=1, source_target_pairs={{0,4},{4,8},{8,12},{12,0},{1,5},{5,9},{9,13},{13,1},{2,6},{6,10},{... | collective-permute-start | bytes 1376264 | tf_op jit(solution)/shard_map/ppermute | solution.py:816
  66.3 17.8 %collective-permute-start.7 = (bf16[1792,128]{1,0:T(8,128)(2,1)S(1)}, bf16[1792,128]{1,0:T(8,128)(2,1)S(1)}, u32[]{:S(2)}, u32[]{:S(2)}) collective-permute-start(bf16[1792,128]{1,0:T(8,128)(2,1)S(1)} %collective-permute-done.6), channel_id=1, source_target_pairs={{0,16},{16,0},{1,17},{17,1},{2,18},{18,2},{3,19},{19,3},{4,20},{20... | collective-permute-start | bytes 1376264 | tf_op jit(solution)/shard_map/ppermute | solution.py:807
  69.9 15.3 %collective-permute-start.43 = (bf16[896,128]{1,0:T(8,128)(2,1)S(1)}, bf16[896,128]{1,0:T(8,128)(2,1)S(1)}, u32[]{:S(2)}, u32[]{:S(2)}) collective-permute-start(bf16[896,128]{1,0:T(8,128)(2,1)S(1)} %collective-permute-done.37), channel_id=1, source_target_pairs={{0,4},{4,8},{8,12},{12,0},{1,5},{5,9},{9,13},{13,1},{2,6},{6,10},{... | collective-permute-start | bytes 688136 | tf_op jit(solution)/shard_map/ppermute | solution.py:816
  85.2 19.1 %collective-permute-start.9 = (bf16[896,128]{1,0:T(8,128)(2,1)S(1)}, bf16[896,128]{1,0:T(8,128)(2,1)S(1)}, u32[]{:S(2)}, u32[]{:S(2)}) collective-permute-start(bf16[896,128]{1,0:T(8,128)(2,1)S(1)} %slice.139), channel_id=1, source_target_pairs={{0,2},{1,3},{2,0},{3,1},{4,6},{5,7},{6,4},{7,5},{8,10},{9,11},{10,... | collective-permute-start | bytes 688136 | tf_op jit(solution)/shard_map/ppermute | solution.py:813
  91.0 12.3 %collective-permute-start.45 = (bf16[896,128]{1,0:T(8,128)(2,1)S(1)}, bf16[896,128]{1,0:T(8,128)(2,1)S(1)}, u32[]{:S(2)}, u32[]{:S(2)}) collective-permute-start(bf16[896,128]{1,0:T(8,128)(2,1)S(1)} %collective-permute-done.43), channel_id=1, source_target_pairs={{0,2},{1,3},{2,0},{3,1},{4,6},{5,7},{6,4},{7,5},{8,10},{9,11},{10,... | collective-permute-start | bytes 688136 | tf_op jit(solution)/shard_map/ppermute | solution.py:813
  93.4 24.9 %collective-permute-start.18 = (bf16[1792,128]{1,0:T(8,128)(2,1)S(1)}, bf16[1792,128]{1,0:T(8,128)(2,1)S(1)}, u32[]{:S(2)}, u32[]{:S(2)}) collective-permute-start(bf16[1792,128]{1,0:T(8,128)(2,1)S(1)} %collective-permute-done.12), channel_id=1, source_target_pairs={{0,4},{4,8},{8,12},{12,0},{1,5},{5,9},{9,13},{13,1},{2,6},{6,10},{... | collective-permute-start | bytes 1376264 | tf_op jit(solution)/shard_map/ppermute | solution.py:816
  93.6 23.0 %collective-permute-start.13 = (bf16[1792,128]{1,0:T(8,128)(2,1)S(1)}, bf16[1792,128]{1,0:T(8,128)(2,1)S(1)}, u32[]{:S(2)}, u32[]{:S(2)}) collective-permute-start(bf16[1792,128]{1,0:T(8,128)(2,1)S(1)} %collective-permute-done.12), channel_id=1, source_target_pairs={{0,16},{16,0},{1,17},{17,1},{2,18},{18,2},{3,19},{19,3},{4,20},{20... | collective-permute-start | bytes 1376264 | tf_op jit(solution)/shard_map/ppermute | solution.py:807
  94.6 23.4 %collective-permute-start.14 = (bf16[1792,128]{1,0:T(8,128)(2,1)S(1)}, bf16[1792,128]{1,0:T(8,128)(2,1)S(1)}, u32[]{:S(2)}, u32[]{:S(2)}) collective-permute-start(bf16[1792,128]{1,0:T(8,128)(2,1)S(1)} %collective-permute-done.12), channel_id=1, source_target_pairs={{0,2},{1,3},{2,0},{3,1},{4,6},{5,7},{6,4},{7,5},{8,10},{9,11},{10,... | collective-permute-start | bytes 1376264 | tf_op jit(solution)/shard_map/ppermute | solution.py:813
  103.3 13.3 %collective-permute-start.10 = (bf16[896,128]{1,0:T(8,128)(2,1)S(1)}, bf16[896,128]{1,0:T(8,128)(2,1)S(1)}, u32[]{:S(2)}, u32[]{:S(2)}) collective-permute-start(bf16[896,128]{1,0:T(8,128)(2,1)S(1)} %slice.140), channel_id=1, source_target_pairs={{0,16},{16,0},{1,17},{17,1},{2,18},{18,2},{3,19},{19,3},{4,20},{20... | collective-permute-start | bytes 688136 | tf_op jit(solution)/shard_map/ppermute | solution.py:807
  104.3 46.0 %collective-permute-start.30 = (bf16[3584,128]{1,0:T(8,128)(2,1)S(1)}, bf16[3584,128]{1,0:T(8,128)(2,1)S(1)}, u32[]{:S(2)}, u32[]{:S(2)}) collective-permute-start(bf16[3584,128]{1,0:T(8,128)(2,1)S(1)} %constant_dynamic-update-slice_fusion.20.refs_0_), channel_id=1, source_target_pairs={{0,1},{1,0},{2,3},{3,2},{4,5},{5,4},{6,7},{7,6},{8,9},{9,8},{10,11... | collective-permute-start | bytes 2752520 | tf_op jit(solution)/shard_map/ppermute | solution.py:810
  118.0 12.5 %collective-permute-start.16 = (bf16[896,128]{1,0:T(8,128)(2,1)S(1)}, bf16[896,128]{1,0:T(8,128)(2,1)S(1)}, u32[]{:S(2)}, u32[]{:S(2)}) collective-permute-start(bf16[896,128]{1,0:T(8,128)(2,1)S(1)} %slice.142), channel_id=1, source_target_pairs={{0,16},{16,0},{1,17},{17,1},{2,18},{18,2},{3,19},{19,3},{4,20},{20... | collective-permute-start | bytes 688136 | tf_op jit(solution)/shard_map/ppermute | solution.py:807
  119.1 12.6 %collective-permute-start.19 = (bf16[1792,128]{1,0:T(8,128)(2,1)S(1)}, bf16[1792,128]{1,0:T(8,128)(2,1)S(1)}, u32[]{:S(2)}, u32[]{:S(2)}) collective-permute-start(bf16[1792,128]{1,0:T(8,128)(2,1)S(1)} %collective-permute-done.18), channel_id=1, source_target_pairs={{0,16},{16,0},{1,17},{17,1},{2,18},{18,2},{3,19},{19,3},{4,20},{20... | collective-permute-start | bytes 1376264 | tf_op jit(solution)/shard_map/ppermute | solution.py:807
  120.3 12.4 %collective-permute-start.20 = (bf16[1792,128]{1,0:T(8,128)(2,1)S(1)}, bf16[1792,128]{1,0:T(8,128)(2,1)S(1)}, u32[]{:S(2)}, u32[]{:S(2)}) collective-permute-start(bf16[1792,128]{1,0:T(8,128)(2,1)S(1)} %collective-permute-done.18), channel_id=1, source_target_pairs={{0,2},{1,3},{2,0},{3,1},{4,6},{5,7},{6,4},{7,5},{8,10},{9,11},{10,... | collective-permute-start | bytes 1376264 | tf_op jit(solution)/shard_map/ppermute | solution.py:813
  122.2 28.2 %collective-permute-start.36 = (bf16[3584,128]{1,0:T(8,128)(2,1)S(1)}, bf16[3584,128]{1,0:T(8,128)(2,1)S(1)}, u32[]{:S(2)}, u32[]{:S(2)}) collective-permute-start(bf16[3584,128]{1,0:T(8,128)(2,1)S(1)} %constant_dynamic-update-slice_fusion.25.refs_2_), channel_id=1, source_target_pairs={{0,1},{1,0},{2,3},{3,2},{4,5},{5,4},{6,7},{7,6},{8,9},{9,8},{10,11... | collective-permute-start | bytes 2752520 | tf_op jit(solution)/shard_map/ppermute | solution.py:810
  130.5 107.7 %collective-permute-start.5 = (bf16[7168,128]{1,0:T(8,128)(2,1)}, bf16[7168,128]{1,0:T(8,128)(2,1)}, u32[]{:S(2)}, u32[]{:S(2)}) collective-permute-start(bf16[7168,128]{1,0:T(8,128)(2,1)} %constant_dynamic-update-slice_fusion.refs_0_), channel_id=1, source_target_pairs={{0,1},{1,0},{2,3},{3,2},{4,5},{5,4},{6,7},{7,6},{8,9},{9,8},{10,11... | collective-permute-start | bytes 5505032 | tf_op jit(solution)/shard_map/ppermute | solution.py:810
  142.7 11.7 %collective-permute-start.42 = (bf16[3584,128]{1,0:T(8,128)(2,1)S(1)}, bf16[3584,128]{1,0:T(8,128)(2,1)S(1)}, u32[]{:S(2)}, u32[]{:S(2)}) collective-permute-start(bf16[3584,128]{1,0:T(8,128)(2,1)S(1)} %constant_dynamic-update-slice_fusion.30.refs_4_), channel_id=1, source_target_pairs={{0,1},{1,0},{2,3},{3,2},{4,5},{5,4},{6,7},{7,6},{8,9},{9,8},{10,11... | collective-permute-start | bytes 2752520 | tf_op jit(solution)/shard_map/ppermute | solution.py:810
  148.1 90.2 %collective-permute-start.11 = (bf16[7168,128]{1,0:T(8,128)(2,1)S(1)}, bf16[7168,128]{1,0:T(8,128)(2,1)}, u32[]{:S(2)}, u32[]{:S(2)}) collective-permute-start(bf16[7168,128]{1,0:T(8,128)(2,1)S(1)} %constant_dynamic-update-slice_fusion.5.refs_2_), channel_id=1, source_target_pairs={{0,1},{1,0},{2,3},{3,2},{4,5},{5,4},{6,7},{7,6},{8,9},{9,8},{10,11... | collective-permute-start | bytes 5505032 | tf_op jit(solution)/shard_map/ppermute | solution.py:810
  150.3 87.9 %collective-permute-start.17 = (bf16[7168,128]{1,0:T(8,128)(2,1)}, bf16[7168,128]{1,0:T(8,128)(2,1)}, u32[]{:S(2)}, u32[]{:S(2)}) collective-permute-start(bf16[7168,128]{1,0:T(8,128)(2,1)} %constant_dynamic-update-slice_fusion.10.refs_4_), channel_id=1, source_target_pairs={{0,1},{1,0},{2,3},{3,2},{4,5},{5,4},{6,7},{7,6},{8,9},{9,8},{10,11... | collective-permute-start | bytes 5505032 | tf_op jit(solution)/shard_map/ppermute | solution.py:810
  150.4 87.8 %collective-permute-start.23 = (bf16[7168,128]{1,0:T(8,128)(2,1)}, bf16[7168,128]{1,0:T(8,128)(2,1)}, u32[]{:S(2)}, u32[]{:S(2)}) collective-permute-start(bf16[7168,128]{1,0:T(8,128)(2,1)} %constant_dynamic-update-slice_fusion.15.refs_6_), channel_id=1, source_target_pairs={{0,1},{1,0},{2,3},{3,2},{4,5},{5,4},{6,7},{7,6},{8,9},{9,8},{10,11... | collective-permute-start | bytes 5505032 | tf_op jit(solution)/shard_map/ppermute | solution.py:810
  155.3 72.8 %collective-permute-start.48 = (bf16[3584,128]{1,0:T(8,128)(2,1)}, bf16[3584,128]{1,0:T(8,128)(2,1)}, u32[]{:S(2)}, u32[]{:S(2)}) collective-permute-start(bf16[3584,128]{1,0:T(8,128)(2,1)} %constant_dynamic-update-slice_fusion.35.refs_6_), channel_id=1, source_target_pairs={{0,1},{1,0},{2,3},{3,2},{4,5},{5,4},{6,7},{7,6},{8,9},{9,8},{10,11... | collective-permute-start | bytes 2752520 | tf_op jit(solution)/shard_map/ppermute | solution.py:810
  158.3 631.6 %all-reduce.7.cloned.1.call-start = ((), (), s32[]{:S(2)}) async-start(), calls=%async_computation.1 | async-start | bytes 450560 | tf_op jit(solution)/shard_map/psum | solution.py:973
  409.7 47.9 %collective-permute-start.49 = (bf16[4,7168,128]{2,1,0:T(8,128)(2,1)}, bf16[4,7168,128]{2,1,0:T(8,128)(2,1)}, u32[]{:S(2)}, u32[]{:S(2)}) collective-permute-start(bf16[4,7168,128]{2,1,0:T(8,128)(2,1)} %pad_maximum_fusion), channel_id=1, source_target_pairs={{0,1},{1,0},{2,3},{3,2},{4,5},{5,4},{6,7},{7,6},{8,9},{9,8},{10,11... | collective-permute-start | bytes 22020104 | tf_op jit(solution)/shard_map/ppermute | solution.py:810
  467.4 36.5 %collective-permute-start.50 = (bf16[4,896,128]{2,1,0:T(8,128)(2,1)}, bf16[4,896,128]{2,1,0:T(8,128)(2,1)}, u32[]{:S(2)}, u32[]{:S(2)}) collective-permute-start(bf16[4,896,128]{2,1,0:T(8,128)(2,1)} %get-tuple-element.96), channel_id=1, source_target_pairs={{0,2},{1,3},{2,0},{3,1},{4,6},{5,7},{6,4},{7,5},{8,10},{9,11},{10,... | collective-permute-start | bytes 2752520 | tf_op jit(solution)/shard_map/ppermute | solution.py:813
  468.6 35.3 %collective-permute-start.52 = (bf16[4,896,128]{2,1,0:T(8,128)(2,1)}, bf16[4,896,128]{2,1,0:T(8,128)(2,1)}, u32[]{:S(2)}, u32[]{:S(2)}) collective-permute-start(bf16[4,896,128]{2,1,0:T(8,128)(2,1)} %get-tuple-element.98), channel_id=1, source_target_pairs={{0,16},{16,0},{1,17},{17,1},{2,18},{18,2},{3,19},{19,3},{4,20},{20... | collective-permute-start | bytes 2752520 | tf_op jit(solution)/shard_map/ppermute | solution.py:807
  470.5 28.9 %collective-permute-start.58 = (bf16[4,448,128]{2,1,0:T(8,128)(2,1)}, bf16[4,448,128]{2,1,0:T(8,128)(2,1)}, u32[]{:S(2)}, u32[]{:S(2)}) collective-permute-start(bf16[4,448,128]{2,1,0:T(8,128)(2,1)} %get-tuple-element.110), channel_id=1, source_target_pairs={{0,2},{1,3},{2,0},{3,1},{4,6},{5,7},{6,4},{7,5},{8,10},{9,11},{10,... | collective-permute-start | bytes 1376264 | tf_op jit(solution)/shard_map/ppermute | solution.py:813
  470.7 29.5 %collective-permute-start.60 = (bf16[4,448,128]{2,1,0:T(8,128)(2,1)S(1)}, bf16[4,448,128]{2,1,0:T(8,128)(2,1)}, u32[]{:S(2)}, u32[]{:S(2)}) collective-permute-start(bf16[4,448,128]{2,1,0:T(8,128)(2,1)S(1)} %get-tuple-element.112), channel_id=1, source_target_pairs={{0,16},{16,0},{1,17},{17,1},{2,18},{18,2},{3,19},{19,3},{4,20},{20... | collective-permute-start | bytes 1376264 | tf_op jit(solution)/shard_map/ppermute | solution.py:807
  502.9 20.9 %collective-permute-start.59 = (bf16[4,896,128]{2,1,0:T(8,128)(2,1)}, bf16[4,896,128]{2,1,0:T(8,128)(2,1)S(1)}, u32[]{:S(2)}, u32[]{:S(2)}) collective-permute-start(bf16[4,896,128]{2,1,0:T(8,128)(2,1)} %pad_maximum_fusion.4), channel_id=1, source_target_pairs={{0,16},{16,0},{1,17},{17,1},{2,18},{18,2},{3,19},{19,3},{4,20},{20... | collective-permute-start | bytes 2752520 | tf_op jit(solution)/shard_map/ppermute | solution.py:807
  507.7 70.1 %collective-permute-start.51 = (bf16[4,1792,128]{2,1,0:T(8,128)(2,1)}, bf16[4,1792,128]{2,1,0:T(8,128)(2,1)}, u32[]{:S(2)}, u32[]{:S(2)}) collective-permute-start(bf16[4,1792,128]{2,1,0:T(8,128)(2,1)} %pad_maximum_fusion.2), channel_id=1, source_target_pairs={{0,16},{16,0},{1,17},{17,1},{2,18},{18,2},{3,19},{19,3},{4,20},{20... | collective-permute-start | bytes 5505032 | tf_op jit(solution)/shard_map/ppermute | solution.py:807
  509.6 68.3 %collective-permute-start.53 = (bf16[4,1792,128]{2,1,0:T(8,128)(2,1)}, bf16[4,1792,128]{2,1,0:T(8,128)(2,1)}, u32[]{:S(2)}, u32[]{:S(2)}) collective-permute-start(bf16[4,1792,128]{2,1,0:T(8,128)(2,1)} %pad_maximum_fusion.3), channel_id=1, source_target_pairs={{0,2},{1,3},{2,0},{3,1},{4,6},{5,7},{6,4},{7,5},{8,10},{9,11},{10,... | collective-permute-start | bytes 5505032 | tf_op jit(solution)/shard_map/ppermute | solution.py:813
  510.0 59.2 %collective-permute-start.61 = (bf16[4,896,128]{2,1,0:T(8,128)(2,1)S(1)}, bf16[4,896,128]{2,1,0:T(8,128)(2,1)S(1)}, u32[]{:S(2)}, u32[]{:S(2)}) collective-permute-start(bf16[4,896,128]{2,1,0:T(8,128)(2,1)S(1)} %pad_maximum_fusion.5), channel_id=1, source_target_pairs={{0,2},{1,3},{2,0},{3,1},{4,6},{5,7},{6,4},{7,5},{8,10},{9,11},{10,... | collective-permute-start | bytes 2752520 | tf_op jit(solution)/shard_map/ppermute | solution.py:813
  581.3 13.6 %collective-permute-start.54 = (bf16[1792,128]{1,0:T(8,128)(2,1)S(1)}, bf16[1792,128]{1,0:T(8,128)(2,1)}, u32[]{:S(2)}, u32[]{:S(2)}) collective-permute-start(bf16[1792,128]{1,0:T(8,128)(2,1)S(1)} %dynamic-slice_bitcast_fusion.16), channel_id=1, source_target_pairs={{0,4},{4,8},{8,12},{12,0},{1,5},{5,9},{9,13},{13,1},{2,6},{6,10},{... | collective-permute-start | bytes 1376264 | tf_op jit(solution)/shard_map/ppermute | solution.py:816
  586.3 13.5 %collective-permute-start.64 = (bf16[896,128]{1,0:T(8,128)(2,1)}, bf16[896,128]{1,0:T(8,128)(2,1)S(1)}, u32[]{:S(2)}, u32[]{:S(2)}) collective-permute-start(bf16[896,128]{1,0:T(8,128)(2,1)} %fusion.4), channel_id=1, source_target_pairs={{0,4},{4,8},{8,12},{12,0},{1,5},{5,9},{9,13},{13,1},{2,6},{6,10},{... | collective-permute-start | bytes 688136 | tf_op jit(solution)/shard_map/ppermute | solution.py:816
  596.0 12.8 %collective-permute-start.55 = (bf16[1792,128]{1,0:T(8,128)(2,1)S(1)}, bf16[1792,128]{1,0:T(8,128)(2,1)}, u32[]{:S(2)}, u32[]{:S(2)}) collective-permute-start(bf16[1792,128]{1,0:T(8,128)(2,1)S(1)} %fusion), channel_id=1, source_target_pairs={{0,4},{4,8},{8,12},{12,0},{1,5},{5,9},{9,13},{13,1},{2,6},{6,10},{... | collective-permute-start | bytes 1376264 | tf_op jit(solution)/shard_map/ppermute | solution.py:816
  609.9 19.2 %collective-permute-start.56 = (bf16[1792,128]{1,0:T(8,128)(2,1)S(1)}, bf16[1792,128]{1,0:T(8,128)(2,1)S(1)}, u32[]{:S(2)}, u32[]{:S(2)}) collective-permute-start(bf16[1792,128]{1,0:T(8,128)(2,1)S(1)} %fusion.1), channel_id=1, source_target_pairs={{0,4},{4,8},{8,12},{12,0},{1,5},{5,9},{9,13},{13,1},{2,6},{6,10},{... | collective-permute-start | bytes 1376264 | tf_op jit(solution)/shard_map/ppermute | solution.py:816
  610.0 19.1 %collective-permute-start.66 = (bf16[896,128]{1,0:T(8,128)(2,1)S(1)}, bf16[896,128]{1,0:T(8,128)(2,1)S(1)}, u32[]{:S(2)}, u32[]{:S(2)}) collective-permute-start(bf16[896,128]{1,0:T(8,128)(2,1)S(1)} %fusion.5), channel_id=1, source_target_pairs={{4,0},{12,4},{5,1},{13,5},{6,2},{14,6},{7,3},{15,7},{20,16},{28,20... | collective-permute-start | bytes 688136 | tf_op jit(solution)/shard_map/ppermute | solution.py:970
  641.0 20.5 %collective-permute-start.68 = (bf16[3584,128]{1,0:T(8,128)(2,1)S(1)}, bf16[3584,128]{1,0:T(8,128)(2,1)}, u32[]{:S(2)}, u32[]{:S(2)}) collective-permute-start(bf16[3584,128]{1,0:T(8,128)(2,1)S(1)} %pad_maximum_fusion.6.refs_0_), channel_id=1, source_target_pairs={{0,2},{1,3},{2,0},{3,1},{4,6},{5,7},{6,4},{7,5},{8,10},{9,11},{10,... | collective-permute-start | bytes 2752520 | tf_op jit(solution)/shard_map/ppermute | solution.py:813
  641.4 148.5 %collective-permute-start.69 = (bf16[3584,128]{1,0:T(8,128)(2,1)S(1)}, bf16[3584,128]{1,0:T(8,128)(2,1)}, u32[]{:S(2)}, u32[]{:S(2)}) collective-permute-start(bf16[3584,128]{1,0:T(8,128)(2,1)S(1)} %pad_maximum_fusion.6.refs_0_), channel_id=1, source_target_pairs={{0,1},{1,0},{2,3},{3,2},{4,5},{5,4},{6,7},{7,6},{8,9},{9,8},{10,11... | collective-permute-start | bytes 2752520 | tf_op jit(solution)/shard_map/ppermute | solution.py:810
  661.5 128.5 %collective-permute-start.70 = (bf16[3584,128]{1,0:T(8,128)(2,1)}, bf16[3584,128]{1,0:T(8,128)(2,1)}, u32[]{:S(2)}, u32[]{:S(2)}) collective-permute-start(bf16[3584,128]{1,0:T(8,128)(2,1)} %collective-permute-done.68.refs_1_), channel_id=1, source_target_pairs={{0,1},{1,0},{2,3},{3,2},{4,5},{5,4},{6,7},{7,6},{8,9},{9,8},{10,11... | collective-permute-start | bytes 2752520 | tf_op jit(solution)/shard_map/ppermute | solution.py:810
  (42 other events, 496.3 us)
Sparse Core Ops, SparseCore 0:
  158.5 67.9 all-reduce.4
  665.7 124.2 all-reduce.6
where the time goes:
time: 861 us; the launch traced here: 853 us
  waiting for transfers between devices  405 us (47%)
  Pallas kernels  206 us (24%)
  local copies, waits for them, and re-layouts  103 us (12%)
  starting transfers between devices  88.7 us (10%)
  other arithmetic  35.5 us (4%)
  between operations  15.3 us (2%)
    psum x1, waiting for transfers between devices, per_device(): lax.psum(dec_table[plan.rest_start:plan.rest_start + plan.rest_room], (SE...  121 us
    ppermute x21, waiting for transfers between devices, over_y(): return lax.ppermute(block, DP, [(d, (d + 2) % nd) for d in range(nd)])  108 us
    pallas_call x1, Pallas kernels, decode(): pl.pallas_call(decode_kernel, grid=(IMAGES_ROW,), in_specs=[whole(a) for...  85.2 us
    unnamed x67, local copies, waits for them, and re-layouts  65 us
    psum x1, waiting for transfers between devices, per_device(): lax.psum(jnp.where(holds_rest, rest_cut, 0.0).astype(bf16), (SEC, GRP))  62.1 us
    pallas_call x2, Pallas kernels, pack(): pl.pallas_call(partial(pack_kernel, layout, names), in_specs=[pl.BlockSpe...  51.5 us
    ppermute x22, waiting for transfers between devices, over_x(): return lax.ppermute(block, SEC, [(0, 1), (1, 0)])  51 us
    ppermute x12, waiting for transfers between devices, over_z(): return lax.ppermute(block, GRP, [(g, (g + 1) % ng) for g in range(ng)])  37.1 us
  transfers between devices with their start and end apart: 73, of which 29 were waited for; matrix products, arithmetic and copies ran while one was open for 7% of the time, Pallas kernels for 4%

commit v1 on v0

--- a/solution.py
+++ b/solution.py
@@ -228,9 +228,9 @@
     sent_ref[...] = (middle + (total + vec[7:8, :width])).astype(bf16)
 
 
-def encode_back_kernel(
-    grad_ref, x_ref, qkv_ref, probs_ref, middle_ref, slope_ref, qkv_w, proj_w, up_w, down_w, vec,
-    in_grad_ref, qkv_low_ref, proj_low_ref, up_low_ref, vec_grad, grad_att_ref,
+def mlp_back_kernel(
+    grad_ref, middle_ref, slope_ref, up_w, down_w, vec,
+    up_low_ref, proj_low_ref, grad_middle_ref, vec_grad,
 ):
     width, hidden = WIDTH, HIDDEN_SIZE
     grad_out = grad_ref[...]
@@ -248,10 +248,19 @@
     vec_grad[4:5, :width] = col_sum(grad_normed2 * hat)
     vec_grad[5:6, :width] = col_sum(grad_normed2)
     grad_middle = grad_out.astype(f32) + norm_back(grad_normed2, hat, inverse, vec[4:5, :width])
+    grad_middle_ref[...] = grad_middle
     proj_low = grad_middle.astype(bf16)
     proj_low_ref[...] = proj_low
     vec_grad[3:4, :width] = col_sum(proj_low.astype(f32))
-    grad_att_ref[...] = dot_nt(proj_low, proj_w[...]).astype(bf16)
+
+
+def attention_back_kernel(
+    grad_middle_ref, proj_low_ref, x_ref, qkv_ref, probs_ref, qkv_w, proj_w, vec, vec_in,
+    in_grad_ref, qkv_low_ref, vec_grad, grad_att_ref,
+):
+    width = WIDTH
+    vec_grad[...] = vec_in[...]
+    grad_att_ref[...] = dot_nt(proj_low_ref[...], proj_w[...]).astype(bf16)
     attention_backward(qkv_ref, probs_ref, grad_att_ref, qkv_low_ref, width, HEADS)
     qkv_low = qkv_low_ref[...]
     vec_grad[2:3, : 3 * width] = col_sum(qkv_low.astype(f32))
@@ -259,7 +268,7 @@
     hat, inverse = normalised(x_ref[...].astype(f32))
     vec_grad[0:1, :width] = col_sum(grad_normed1 * hat)
     vec_grad[1:2, :width] = col_sum(grad_normed1)
-    in_grad_ref[...] = grad_middle + norm_back(grad_normed1, hat, inverse, vec[0:1, :width])
+    in_grad_ref[...] = grad_middle_ref[...] + norm_back(grad_normed1, hat, inverse, vec[0:1, :width])
 
 
 def decode_kernel(
@@ -351,6 +360,10 @@
         grad_sent_ref[...] = dot_nt(embed_low, embed_w[...]).astype(bf16)
 
 
+def cost(microseconds):
+    return pl.CostEstimate(flops=int(microseconds * 1e9), bytes_accessed=0, transcendentals=0)
+
+
 def params_of(**extra):
     return pltpu.CompilerParams(vmem_limit_bytes=VMEM_BYTES, **extra)
 
@@ -377,26 +390,44 @@
         ],
         scratch_shapes=[pltpu.VMEM((width, length), f32)],
         compiler_params=params_of(),
+        cost_estimate=cost(18),
         name="encode",
     )(x, seg.reshape(1, length), seg.reshape(length, 1), *[weights[n] for n in names])
 
 
-def encode_back(grad, x, saved, weights):
+def mlp_back(grad, saved, weights):
     width, hidden, length = WIDTH, HIDDEN_SIZE, ROW
-    names = [QKV_W, PROJ_W, UP_W, DOWN_W, VECS]
     return pl.pallas_call(
-        encode_back_kernel,
+        mlp_back_kernel,
+        out_shape=[
+            shape((length, hidden), bf16),
+            shape((length, width), bf16),
+            shape((length, width), f32),
+            shape((VEC_ROWS, hidden), f32),
+        ],
+        compiler_params=params_of(),
+        cost_estimate=cost(9),
+        name="mlp_back",
+    )(grad, saved[MID], saved[SLOPE], weights[UP_W], weights[DOWN_W], weights[VECS])
+
+
+def attention_back(grad_middle, proj_low, x, saved, weights, vec_grad):
+    width, hidden, length = WIDTH, HIDDEN_SIZE, ROW
+    return pl.pallas_call(
+        attention_back_kernel,
         out_shape=[
             shape((length, width), f32),
             shape((length, 3 * width), bf16),
-            shape((length, width), bf16),
-            shape((length, hidden), bf16),
             shape((VEC_ROWS, hidden), f32),
         ],
         scratch_shapes=[pltpu.VMEM((length, width), bf16)],
         compiler_params=params_of(),
-        name="encode_back",
-    )(grad, x, saved[QKV], saved[PROBS], saved[MID], saved[SLOPE], *[weights[n] for n in names])
+        cost_estimate=cost(10),
+        name="attention_back",
+    )(
+        grad_middle, proj_low, x, saved[QKV], saved[PROBS],
+        weights[QKV_W], weights[PROJ_W], weights[VECS], vec_grad,
+    )
 
 
 def decode(sent, seg, slot, cot, weights):
@@ -435,6 +466,7 @@
             pltpu.VMEM((length, width), bf16),
         ],
         compiler_params=params_of(dimension_semantics=("arbitrary",)),
+        cost_estimate=cost(85),
         name="decode",
     )(*held, cot)
 
@@ -472,26 +504,30 @@
         self.piece = up_to(-(-self.chunk // self.pieces), 64)
         self.half = self.piece // 2
         self.room = self.piece * self.pieces
-        self.units = 2 * self.pieces
         self.full = self.ng // 2
-        self.dec_rows = flat_starts(DEC_LAYOUT)[1]
-        self.rest = self.dec_rows - self.full * self.chunk
-        self.rest_room = up_to(self.rest + 80, 16)
-        assert 0 < self.rest <= self.chunk and self.rest_room <= self.half + self.chunk
-        self.enc_keep, self.enc_kept = kept_starts(ENC_LAYOUT)
-        self.dec_keep, self.dec_kept = kept_starts(DEC_LAYOUT)
+        self.rest = flat_starts(DEC_LAYOUT)[1] - self.full * self.chunk
+        assert 0 < self.rest <= self.chunk
+        whole = self.chunk // self.half * self.half
+        last_piece_used = whole == self.room - self.half
+        free = self.half - (self.chunk - whole) if last_piece_used else self.half
+        self.part_in = free // 16 * 16
+        self.parts_in = -(-self.rest // self.part_in)
+        assert self.parts_in <= self.full
         self.enc_starts = [self.kept_row(ENC_LAYOUT, z * self.chunk) // 16 * 16 for z in range(self.ng)]
+        self.enc_ends = [
+            up_to(self.kept_row(ENC_LAYOUT, min((z + 1) * self.chunk, flat_starts(ENC_LAYOUT)[1]) - 1) + 1, 16)
+            for z in range(self.ng)
+        ]
         self.dec_starts = [self.kept_row(DEC_LAYOUT, z * self.chunk) // 16 * 16 for z in range(self.full)]
+        self.dec_ends = [
+            up_to(self.kept_row(DEC_LAYOUT, (z + 1) * self.chunk - 1) + 1, 16) for z in range(self.full)
+        ]
+        assert all(e - s <= self.room for s, e in zip(self.enc_starts, self.enc_ends))
         self.rest_start = self.kept_row(DEC_LAYOUT, self.full * self.chunk) // 16 * 16
-        for z in range(self.ng):
-            last = self.kept_row(ENC_LAYOUT, min((z + 1) * self.chunk, flat_starts(ENC_LAYOUT)[1]) - 1)
-            assert last < self.enc_starts[z] + self.room
-        for z in range(self.full):
-            last = self.kept_row(DEC_LAYOUT, (z + 1) * self.chunk - 1)
-            assert last < self.dec_starts[z] + self.room
-        assert self.dec_kept <= self.rest_start + self.rest_room
-        self.enc_table = self.enc_starts[-1] + self.room
-        self.dec_table = max(self.dec_starts[-1] + self.room, self.rest_start + self.rest_room)
+        self.rest_end = kept_starts(DEC_LAYOUT)[1]
+        self.part_out = [self.room - (self.dec_ends[k] - self.dec_starts[k]) for k in range(2)]
+        assert max(self.part_out) <= self.room // 2
+        assert self.part_out[0] < self.rest_end - self.rest_start <= sum(self.part_out)
 
     def kept_row(self, layout, flat_row):
         flat, _ = flat_starts(layout)
@@ -507,7 +543,8 @@
         while count:
             z, row = divmod(first, self.chunk)
             if z >= chunks:
-                here, room = chunks * self.room + row, count
+                k, row = divmod(row, self.part_in)
+                here, room = (k + 1) * self.room - self.half + row, self.part_in - row
             elif row < whole:
                 here, room = z * self.room + row, whole - row
             else:
@@ -517,27 +554,48 @@
             first, count = first + take, count - take
         return found
 
+    def enc_regions(self, groups):
+        return [(self.enc_starts[z], self.enc_ends[z], k, 0) for k, z in enumerate(groups)]
+
+    def dec_regions(self):
+        length = self.room // 2
+        found = []
+        for z in range(self.full):
+            low, high = self.dec_starts[z], self.dec_ends[z]
+            found += [(low, low + length, 2 * z, 0), (low + length, high, 2 * z + 1, 0)]
+        middle = self.rest_start + self.part_out[0]
+        found.append((self.rest_start, middle, 1, length - self.part_out[0]))
+        found.append((middle, self.rest_end, 3, length - self.part_out[1]))
+        return found
+
     def segments(self):
-        count = len(DEC_LAYOUT) + 1
+        count = len(DEC_LAYOUT) + 2
         table = np.zeros((self.ns, self.ng, count, 3), np.int32)
+        length = self.room // 2
         for s, layout in enumerate((ENC_LAYOUT, DEC_LAYOUT)):
             flat, used = flat_starts(layout)
             for z in range(self.ng):
                 low, high = z * self.chunk, (z + 1) * self.chunk
-                if s == 0:
-                    base = -self.enc_starts[z]
-                elif z < self.full:
-                    base = -self.dec_starts[z]
-                else:
-                    base = self.room - self.rest_start
-                for k, (name, extent) in enumerate(layout):
+                found = []
+                for name, extent in layout:
                     first, last = max(flat[name], low), min(flat[name] + rows_of(extent), high)
-                    if first < last:
-                        table[s, z, k] = (
-                            base + self.kept_row(layout, first), first - low, -(-(last - first) // 8),
-                        )
+                    while first < last:
+                        row, stop = self.kept_row(layout, first), last
+                        if s == 0:
+                            source = row - self.enc_starts[z]
+                        elif z < self.full:
+                            source = row - self.dec_starts[z]
+                        else:
+                            row -= self.rest_start
+                            k = int(row >= self.part_out[0])
+                            row -= k * self.part_out[0]
+                            source = (k + 1) * length - self.part_out[k] + row
+                            stop = min(last, first + self.part_out[k] - row)
+                        found.append((source, first - low, -(-(stop - first) // 8)))
+                        first = stop
                 if used < high:
-                    table[s, z, count - 1] = (self.room + self.rest_room, max(used - low, 0), 1)
+                    found.append((self.room, max(used - low, 0), 1))
+                table[s, z, : len(found)] = found
         return table
 
 
@@ -563,9 +621,6 @@
 def unpack_kernel(plan, layout, unit, cut, chunks, counts, place_ref, *refs):
     sources = refs[: len(counts)]
     refs = refs[len(counts) :]
-    rest = None
-    if chunks < plan.ng:
-        rest, refs = refs[0], refs[1:]
     matrices = [(n, e) for n, e in layout if len(e) == 2]
     outs, vec = refs[: len(matrices)], refs[len(matrices)]
     held, wide, spare, sems = refs[len(matrices) + 1 :]
@@ -577,18 +632,14 @@
             number += 1
             target = held.at[pl.ds(pl.multiple_of(slot * unit, 16), unit), :]
             pltpu.make_async_copy(source.at[pl.ds(k * unit, unit), :], target, sems.at[slot // per_chunk]).start()
-    if rest is not None:
-        target = held.at[pl.ds(chunks * plan.room, rest.shape[0]), :]
-        pltpu.make_async_copy(rest, target, sems.at[chunks]).start()
     arrived = set()
 
     def arrive(ranges):
         for start, count in ranges:
-            z = min(start // plan.room, chunks)
+            z = start // plan.room
             if z not in arrived:
                 arrived.add(z)
-                rows = plan.room if z < chunks else rest.shape[0]
-                part = held.at[pl.ds(z * plan.room, rows), :]
+                part = held.at[pl.ds(z * plan.room, plan.room), :]
                 pltpu.make_async_copy(part, part, sems.at[z]).wait()
 
     vec[...] = jnp.zeros_like(vec)
@@ -617,18 +668,17 @@
             row, shift = {QB: (2, 0), VB: (2, 2 * extent[0])}.get(name, (VEC.get(name), 0))
             for j in range(lanes):
                 vec[row : row + 1, shift + j * LANES : shift + (j + 1) * LANES] = wide[skip + j : skip + j + 1, :]
-    for z in range(chunks + (rest is not None)):
-        if z not in arrived:
-            arrive([(z * plan.room, 1)])
-
-
-def unpack(plan, layout, unit, cut, chunks, place, sources, rest=None):
+    for z in range(chunks):
+        arrive([(z * plan.room, 1)])
+
+
+def unpack(plan, layout, unit, cut, chunks, place, sources):
     matrices = [(n, e) for n, e in layout if len(e) == 2]
     outs = [
         shape((SLOT_PAD if n == POS else e[0], e[1]), bf16) for n, e in matrices
     ] + [shape((VEC_ROWS, 4 * dict(layout)[PB][0]), f32)]
-    operands = list(sources) + ([] if rest is None else [rest])
-    rows = chunks * plan.room + (0 if rest is None else rest.shape[0])
+    operands = list(sources)
+    rows = chunks * plan.room
     result = pl.pallas_call(
         partial(unpack_kernel, plan, layout, unit, cut, chunks, [s.shape[0] // unit for s in sources]),
         in_specs=[pl.BlockSpec(memory_space=pltpu.SMEM)]
@@ -638,62 +688,84 @@
             pltpu.VMEM((rows, LANES), bf16),
             pltpu.VMEM((3200, LANES), f32),
             pltpu.VMEM((3200, LANES), f32),
-            pltpu.SemaphoreType.DMA((chunks + 1,)),
+            pltpu.SemaphoreType.DMA((chunks,)),
         ],
         compiler_params=params_of(),
+        cost_estimate=cost(12),
         name="unpack",
     )(place, *operands)
     return dict(zip([n for n, _ in matrices] + [VECS], result))
 
 
-def pack_kernel(layout, names, *refs):
+def pack_kernel(plan, layout, names, regions, size, groups, place_ref, *refs):
     pairs = {}
     for name in names:
         pairs[name], refs = refs[:2], refs[2:]
     vec, refs = refs[0], refs[1:]
     pos = None
-    if POS in dict(layout):
-        pos, refs = refs[0], refs[1:]
-    table, wide, stage, small, sems, small_sem = refs
+    if POS in names:
+        pos, refs = pairs[POS][0], refs
+    mine, theirs, wide, stage, small, sems = refs
     kept, _ = kept_starts(layout)
     extents = dict(layout)
-    step = 128
+    ny = plan.ny
+
+    def send(source, first, rows, sem):
+        moved = 0
+        for low, high, index, base in regions:
+            start, stop = max(first, low), min(first + rows, high)
+            while start < stop:
+                number, row = divmod(base + start - low, size)
+                count = min(stop - start, size - row)
+                c, s, y = number // (2 * ny), number // ny % 2, number % ny
+                owner = lax.rem(s - place_ref[0] + 2, 2) * ny + lax.rem(y - place_ref[1] + ny, ny)
+                target = pl.ds(pl.multiple_of(owner * (groups * size), 16) + index * size + row, count)
+                block = source.at[pl.ds(start - first, count), :]
+                for same, table in ((True, mine), (False, theirs)):
+
+                    @pl.when((place_ref[2] == c) == same)
+                    def _():
+                        pltpu.make_async_copy(block, table.at[target, :], sem).start()
+
+                moved += count
+                start += count
+        return moved
+
+    def wait(rows, slot):
+        if rows:
+            block = stage.at[slot, pl.ds(0, rows), :]
+            pltpu.make_async_copy(block, block, sems.at[slot]).wait()
+
+    turn = 0
+    pending = [0, 0]
     for name in names:
+        if name == POS:
+            continue
         left, right = pairs[name]
         depth, width = extents[name]
         lanes = width // LANES
+        step = max(k for k in (128, 256, 384, 512) if depth % k == 0 and k * lanes <= 3072)
         rows = step * lanes
-
-        def copy(index, slot, rows=rows, name=name):
-            start = pl.multiple_of(kept[name] + index * rows, 16)
-            return pltpu.make_async_copy(
-                stage.at[slot, pl.ds(0, rows), :], table.at[pl.ds(start, rows), :], sems.at[slot]
-            )
-
-        def one(index, carry, left=left, right=right, width=width, lanes=lanes, rows=rows, copy=copy):
-            slot = lax.rem(index, 2)
-            columns = flip(left[:, pl.ds(pl.multiple_of(index * step, step), step)])
+        for first in range(0, depth, step):
+            start = kept[name] + first * lanes
+            if all(start >= high or start + rows <= low for low, high, _, _ in regions):
+                continue
+            slot = turn % 2
+            turn += 1
+            columns = flip(left[:, first : first + step])
             part = 256
-            for first in range(0, width, part):
-                block = dot(columns, right[:, first : first + part])
+            for start in range(0, width, part):
+                block = dot(columns, right[:, start : start + part])
                 for j in range(part // LANES):
-                    wide[pl.ds(first // LANES + j, step, stride=lanes), :] = block[:, j * LANES : (j + 1) * LANES]
-
-            @pl.when(index >= 2)
-            def _():
-                copy(index - 2, slot).wait()
-
+                    wide[pl.ds(start // LANES + j, step, stride=lanes), :] = block[:, j * LANES : (j + 1) * LANES]
+            wait(pending[slot], slot)
             stage[slot, 0:rows, :] = wide[0:rows, :].astype(bf16)
-            copy(index, slot).start()
-            return carry
-
-        count = depth // step
-        lax.fori_loop(0, count, one, 0)
-        for index in range(max(count - 2, 0), count):
-            copy(index, index % 2).wait()
+            pending[slot] = send(stage.at[slot], kept[name] + first * lanes, rows, sems.at[slot])
     here = 0
-    copies = []
+    total = 0
     for name, extent in layout:
+        if name not in names and len(extent) == 2 or name not in kept_names(names):
+            continue
         if len(extent) == 2 and name != POS:
             continue
         rows = rows_of(extent)
@@ -708,43 +780,52 @@
             for j in range(rows):
                 wide[j : j + 1, :] = vec[row : row + 1, shift + j * LANES : shift + (j + 1) * LANES]
         small[here : here + room, :] = wide[0:room, :].astype(bf16)
-        copies.append(
-            pltpu.make_async_copy(
-                small.at[pl.ds(here, room), :], table.at[pl.ds(kept[name], room), :], small_sem.at[0]
-            )
-        )
+        total += send(small.at[pl.ds(here, room), :], kept[name], room, sems.at[2])
         here += room
-    for each in copies:
-        each.start()
-    pltpu.make_async_copy(small, small, small_sem.at[0]).wait()
-
-
-def pack(layout, table_rows, pairs, vec, pos=None):
+    wait(pending[0], 0)
+    wait(pending[1], 1)
+    block = small.at[pl.ds(0, total), :]
+    pltpu.make_async_copy(block, block, sems.at[2]).wait()
+
+
+def kept_names(names):
+    with_matrix = {
+        QKV_W: [N1G, N1B, QB, VB],
+        PROJ_W: [PB, N2G, N2B],
+        UP_W: [UB],
+        DOWN_W: [DB],
+        EMBED_W: [EB, MT],
+        POS: [POS],
+    }
+    return [v for n in names for v in with_matrix[n]]
+
+
+def pack(plan, layout, regions, size, groups, place, pairs, vec):
     names = list(pairs)
-    operands = [a for name in names for a in pairs[name]] + [vec] + ([] if pos is None else [pos])
-    small = sum(
-        up_to(rows_of(e), 16) for n, e in layout if len(e) == 1 or n == POS
-    )
-    most = 128 * max(e[1] for n, e in layout if len(e) == 2) // LANES
+    operands = [a for name in names for a in pairs[name]] + [vec]
+    extents = dict(layout)
+    small = sum(up_to(rows_of(extents[n]), 16) for n in kept_names(names))
+    rows = 2 * plan.ny * groups * size
     return pl.pallas_call(
-        partial(pack_kernel, layout, names),
-        in_specs=[pl.BlockSpec(memory_space=pltpu.VMEM)] * len(operands),
-        out_specs=pl.BlockSpec(memory_space=pl.ANY),
-        out_shape=shape((table_rows, LANES), bf16),
+        partial(pack_kernel, plan, layout, names, regions, size, groups),
+        in_specs=[pl.BlockSpec(memory_space=pltpu.SMEM)]
+        + [pl.BlockSpec(memory_space=pltpu.VMEM)] * len(operands),
+        out_specs=[pl.BlockSpec(memory_space=pl.ANY)] * 2,
+        out_shape=[shape((rows, LANES), bf16)] * 2,
         scratch_shapes=[
-            pltpu.VMEM((most, LANES), f32),
-            pltpu.VMEM((2, most, LANES), bf16),
-            pltpu.VMEM((small, LANES), bf16),
-            pltpu.SemaphoreType.DMA((2,)),
-            pltpu.SemaphoreType.DMA((1,)),
+            pltpu.VMEM((3072, LANES), f32),
+            pltpu.VMEM((2, 3072 + 64, LANES), bf16),
+            pltpu.VMEM((small + 64, LANES), bf16),
+            pltpu.SemaphoreType.DMA((3,)),
         ],
         compiler_params=params_of(),
+        cost_estimate=cost(25 if EMBED_W in names else 12),
         name="pack",
-    )(*operands)
+    )(place, *operands)
 
 
 def finish_kernel(plan, counts, place_ref, seg_ref, *refs):
-    sources, rest, out, held, wide, sem = refs[: len(counts)], *refs[len(counts) :]
+    sources, result, held, wide, out, sem = refs[: len(counts)], *refs[len(counts) :]
     unit = plan.half
     number = 0
     for source, count in zip(sources, counts):
@@ -752,10 +833,9 @@
             target = held.at[pl.ds(pl.multiple_of(place_ref[number] * unit, 16), unit), :]
             number += 1
             pltpu.make_async_copy(source.at[pl.ds(k * unit, unit), :], target, sem.at[0]).start()
-    pltpu.make_async_copy(rest, held.at[pl.ds(plan.room, plan.rest_room), :], sem.at[0]).start()
     out[...] = jnp.zeros_like(out)
     pltpu.make_async_copy(held, held, sem.at[0]).wait()
-    total = plan.room + plan.rest_room
+    total = plan.room
     wide[total : total + 16, :] = jnp.zeros((16, LANES), f32)
     wide[0:total, :] = held[...].astype(f32)
 
@@ -775,23 +855,35 @@
         return lax.fori_loop(many * 8, steps, step, carry)
 
     lax.fori_loop(0, seg_ref.shape[0] // 3, one, 0)
-
-
-def finish(plan, place, segments, sources, rest):
-    total = plan.room + plan.rest_room
+    rows = up_to(plan.chunk, 8)
+    lines = out.at[pl.ds(0, rows), :].reshape(rows, 1, LANES)
+    copy = pltpu.make_async_copy(lines.at[pl.ds(0, plan.chunk)], result, sem.at[0])
+    copy.start()
+    copy.wait()
+
+
+def finish(plan, place, segments, sources):
+    total = plan.room
     return pl.pallas_call(
         partial(finish_kernel, plan, [s.shape[0] // plan.half for s in sources]),
         in_specs=[pl.BlockSpec(memory_space=pltpu.SMEM)] * 2
-        + [pl.BlockSpec(memory_space=pl.ANY)] * (len(sources) + 1),
-        out_shape=shape((up_to(plan.chunk, 8) + 8, LANES), f32),
+        + [pl.BlockSpec(memory_space=pl.ANY)] * len(sources),
+        out_specs=pl.BlockSpec(memory_space=pl.ANY),
+        out_shape=shape((plan.chunk, 1, LANES), f32),
         scratch_shapes=[
             pltpu.VMEM((total, LANES), bf16),
             pltpu.VMEM((total + 16, LANES), f32),
+            pltpu.VMEM((up_to(plan.chunk, 8) + 8, LANES), f32),
             pltpu.SemaphoreType.DMA((1,)),
         ],
         compiler_params=params_of(),
+        cost_estimate=cost(8),
         name="finish",
-    )(place, segments, *sources, rest)
+    )(place, segments, *sources)
+
+
+def after(values, *before):
+    return lax.optimization_barrier((values, before))[0]
 
 
 def per_device(plan, enc_input, segments, slots, params, cot):
@@ -812,8 +904,9 @@
     def over_y(block):
         return lax.ppermute(block, DP, [(d, (d + 2) % nd) for d in range(nd)])
 
-    def over_z(block):
-        return lax.ppermute(block, GRP, [(g, (g + 1) % ng) for g in range(ng)])
+    def over_z(block, senders=None):
+        senders = range(ng) if senders is None else senders
+        return lax.ppermute(block, GRP, [(g, (g + 1) % ng) for g in senders])
 
     def share(start):
         cut = lax.dynamic_slice(params, (0, start * LANES), (1, half * LANES))
@@ -829,52 +922,69 @@
         ]
         return jnp.concatenate([share(s) for s in starts])
 
+    send = shares(1 - sec)
+    got = over_x(send)
     keep = shares(sec)
-    got = over_x(shares(1 - sec))
+    rest = params[:, : plan.part_in * plan.parts_in * LANES].astype(f32).reshape(-1, LANES).astype(bf16)
     enc_piece = jnp.where(first_section, keep, got)
     dec_pieces = jnp.where(first_section, got, keep)
+
+    def gather(parts, first, wait_for=()):
+        here = jnp.concatenate(parts) if len(parts) > 1 else parts[0]
+        here = after(here, *wait_for)
+        size = here.shape[0]
+        if ny == 2:
+            from_x, from_y = over_x(here), over_y(here)
+            corner_0 = over_y(from_x[: size // 2])
+            corner_1 = over_x(from_y[size // 2 :])
+            sources = [here, from_x, from_y, corner_0, corner_1]
+            owners = [(sec, yy), (1 - sec, yy), (sec, 1 - yy), (1 - sec, 1 - yy)]
+            early, late = (from_x, from_y), (corner_0, corner_1)
+        else:
+            column = [here]
+            for _ in range(ny - 1):
+                column.append(over_y(column[-1]))
+            sources = column + [over_x(block) for block in column]
+            owners = [(s, (yy - k) % ny) for s in (sec, 1 - sec) for k in range(ny)]
+            early, late = (column[1],), (sources[-1],)
+        sources = sources + [over_core(block) for block in sources]
+        places = []
+        for c in (core, 1 - core):
+            for s, y in owners:
+                for k in range(len(parts)):
+                    number = (grp - first - k) % ng * plan.pieces + s * nd + y * 2 + c
+                    places += [2 * number, 2 * number + 1]
+        return sources, jnp.stack(places).astype(jnp.int32), early, late
+
+    near = ng // 2
+    enc_parts = [enc_piece]
+    for _ in range(near - 1):
+        enc_parts.append(over_z(enc_parts[-1]))
+    sources_0, places_0, early_0, late_0 = gather(enc_parts[:near], 0)
+    enc_parts.append(over_z(enc_parts[-1]))
+    enc_parts[-1] = after(enc_parts[-1], *early_0)
+    for _ in range(ng - near - 1):
+        enc_parts.append(over_z(enc_parts[-1]))
+    sources_1, places_1, early_1, late_1 = gather(enc_parts[near:], near, late_0)
+    enc_sources, enc_places = sources_0 + sources_1, jnp.concatenate([places_0, places_1])
+
+    dec_pieces, rest = after((dec_pieces, rest), enc_parts[-1])
     spread = [
         lax.ppermute(dec_pieces[h * half : (h + 1) * half], GRP, [(z, 2 * z + h) for z in range(plan.full)])
         for h in range(2)
     ]
     dec_piece = jnp.where(grp % 2 == 0, spread[0], spread[1])
-    holds_rest = jnp.logical_and(sec == 1, grp == plan.full)
-    rest_cut = params[:, : plan.rest * LANES].astype(f32).reshape(plan.rest, LANES)
-    rest_weights = lax.psum(
-        jnp.where(holds_rest, rest_cut, 0.0).astype(bf16), (SEC, GRP)
-    )
-    rest_weights = jnp.pad(rest_weights, ((0, plan.rest_room - plan.rest), (0, 0)))
-
-    def gather(block):
-        size = block.shape[0]
-        sources, places = [], []
-        here = block
-        for step in range(ng):
-            own_group = (grp - step) % ng
-            number = lambda s, y, c: (own_group * plan.pieces + s * nd + y * 2 + c) * 2
-            if ny == 2:
-                from_x, from_y = over_x(here), over_y(here)
-                corner_0 = over_y(from_x[: size // 2])
-                corner_1 = over_x(from_y[size // 2 :])
-                all_four = jnp.concatenate([here, from_x, from_y, corner_0, corner_1])
-                owners = [(sec, yy), (1 - sec, yy), (sec, 1 - yy), (1 - sec, 1 - yy)]
-            else:
-                ring = [here]
-                for _ in range(ny - 1):
-                    ring.append(over_y(ring[-1]))
-                column = jnp.concatenate(ring)
-                all_four = jnp.concatenate([column, over_x(column)])
-                owners = [(s, (yy - k) % ny) for s in (sec, 1 - sec) for k in range(ny)]
-            sources += [all_four, over_core(all_four)]
-            for c in (core, 1 - core):
-                for s, y in owners:
-                    places += [number(s, y, c), number(s, y, c) + 1]
-            if step < ng - 1:
-                here = over_z(here)
-        return sources, jnp.stack(places).astype(jnp.int32)
-
-    enc_sources, enc_places = gather(enc_piece)
-    dec_sources, dec_places = gather(dec_piece)
+    last = jnp.logical_and(sec == ns - 1, dp == nd - 1)
+    for k in range(plan.parts_in):
+        part = lax.ppermute(
+            rest[k * plan.part_in : (k + 1) * plan.part_in], GRP, [(plan.full, 2 * k + 1)]
+        )
+        filled = lax.dynamic_update_slice(dec_piece, part, (0, 0))
+        dec_piece = jnp.where(jnp.logical_and(last, grp == 2 * k + 1), filled, dec_piece)
+    dec_parts = [dec_piece]
+    for _ in range(ng - 1):
+        dec_parts.append(over_z(dec_parts[-1]))
+    dec_sources, dec_places, early_2, late_2 = gather(dec_parts, 0, late_1)
 
     micro_rows = enc_input.reshape(ROW, WIDTH)
     seg = lax.dynamic_index_in_dim(segments, sec, 0, keepdims=False).reshape(ROW)
@@ -884,44 +994,16 @@
     ).reshape(IMAGES_ROW * SLOT_PAD, DEC_WIDTH)
 
     enc_weights = unpack(plan, ENC_LAYOUT, half, piece, ng, enc_places, enc_sources)
+    micro_rows = after(micro_rows, *early_2)
     saved = dict(
-        zip(
-            [SENT, H1, QKV, PROBS, ATT, MID, H2, ACT, SLOPE],
-            encode(micro_rows, seg, enc_weights),
-        )
+        zip([SENT, H1, QKV, PROBS, ATT, MID, H2, ACT, SLOPE], encode(micro_rows, seg, enc_weights))
     )
-    dec_weights = unpack(plan, DEC_LAYOUT, half // 2, half, plan.full, dec_places, dec_sources, rest_weights)
+    dec_weights = unpack(plan, DEC_LAYOUT, half // 2, half, plan.full, dec_places, dec_sources)
     dec = dict(
         zip(
-            [OUT, H1, QKV_L, ATT, PROJ_L, H2, UP_L, ACT,
-             EMBED_L, GSENT, VECS, GPOS],
+            [OUT, H1, QKV_L, ATT, PROJ_L, H2, UP_L, ACT, EMBED_L, GSENT, VECS, GPOS],
             decode(saved[SENT], seg, slot, cot_rows, dec_weights),
         )
-    )
-    dec_table = pack(
-        DEC_LAYOUT,
-        plan.dec_table,
-        {
-            EMBED_W: (saved[SENT], dec[EMBED_L]),
-            QKV_W: (dec[H1], dec[QKV_L]),
-            PROJ_W: (dec[ATT], dec[PROJ_L]),
-            UP_W: (dec[H2], dec[UP_L]),
-            DOWN_W: (dec[ACT], cot_rows),
-        },
-        dec[VECS],
-        dec[GPOS],
-    )
-    in_grad, qkv_low, proj_low, up_low, enc_vec = encode_back(dec[GSENT], micro_rows, saved, enc_weights)
-    enc_table = pack(
-        ENC_LAYOUT,
-        plan.enc_table,
-        {
-            DOWN_W: (saved[ACT], dec[GSENT]),
-            UP_W: (saved[H2], up_low),
-            PROJ_W: (saved[ATT], proj_low),
-            QKV_W: (saved[H1], qkv_low),
-        },
-        enc_vec,
     )
 
     def add(first, *others):
@@ -930,69 +1012,145 @@
             total = total + other.astype(f32)
         return total.astype(bf16)
 
-    def reduce(table, starts, length):
-        part = length // 2
-
-        def core_half(which):
-            return jnp.stack([lax.dynamic_slice(table, (s + which * part, 0), (part, LANES)) for s in starts])
-
-        held = add(core_half(core), over_core(core_half(1 - core)))
-        size = part // (2 * ny)
-
-        def owned_by(s, y):
-            return lax.dynamic_slice(held, (0, (s * ny + y) * size, 0), (len(starts), size, LANES))
-
-        if ny == 2:
-            corner = owned_by(1 - sec, 1 - yy)
-            corner_x = over_x(corner[:, : size // 2])
-            corner_y = over_y(corner[:, size // 2 :])
-            beside_y = owned_by(sec, 1 - yy)
-            beside_x = owned_by(1 - sec, yy)
-            send_y = jnp.concatenate([add(beside_y[:, : size // 2], corner_x), beside_y[:, size // 2 :]], axis=1)
-            send_x = jnp.concatenate([beside_x[:, : size // 2], add(beside_x[:, size // 2 :], corner_y)], axis=1)
-            mine = add(owned_by(sec, yy), over_x(send_x), over_y(send_y))
-        else:
-            column = lambda s: lax.dynamic_slice(held, (0, s * ny * size, 0), (len(starts), ny * size, LANES))
-            own = add(column(sec), over_x(column(1 - sec)))
-            block = lambda y: lax.dynamic_slice(own, (0, (y % ny) * size, 0), (len(starts), size, LANES))
-            mine = block(yy - 1)
-            for step in range(ny - 1):
-                mine = add(block(yy - 2 - step), over_y(mine))
-        one = lambda g: lax.dynamic_index_in_dim(mine, g % ng, 0, keepdims=False)
-        total = one(grp - 1)
-        for step in range(ng - 1):
-            total = add(one(grp - 2 - step), over_z(total))
-        return total
-
-    dec_half_starts = [s + h * (room // 2) for s in plan.dec_starts for h in range(2)]
-    dec_sum = reduce(dec_table, dec_half_starts, room // 2)
-    dec_sums = [
-        lax.ppermute(dec_sum, GRP, [(2 * z + h, z) for z in range(plan.full)]) for h in range(2)
-    ]
-    dec_own = jnp.concatenate(dec_sums)
-    rest_sum = lax.psum(
-        dec_table[plan.rest_start : plan.rest_start + plan.rest_room], (SEC, GRP, DP)
+    class Reduction:
+        def __init__(self, tables, groups, size):
+            self.mine, theirs = tables
+            self.groups, self.size = groups, size
+            self.from_core = over_core(theirs)
+
+        def block(self, k, low=0, high=None):
+            rows = len(self.groups) * self.size
+            low, high = k * rows + low, k * rows + (rows if high is None else high)
+            return add(self.mine[low:high], self.from_core[low:high])
+
+        def corners(self):
+            rows = len(self.groups) * self.size
+            if ny == 2:
+                self.middle = rows // 2
+                self.corner_x = over_x(self.block(3, 0, self.middle))
+                self.corner_y = over_y(self.block(3, self.middle))
+                self.early_y = over_y(self.block(1, self.middle))
+                self.early_x = over_x(self.block(2, 0, self.middle))
+                return self.corner_x, self.corner_y
+            held = [self.block(k) for k in range(2 * ny)]
+            self.column = [add(held[k], over_x(held[ny + k])) for k in range(ny)]
+            return tuple(self.column)
+
+        def sides(self):
+            rows = len(self.groups) * self.size
+            if ny == 2:
+                m = self.middle
+                late_y = over_y(add(self.mine[rows : rows + m], self.from_core[rows : rows + m], self.corner_x))
+                low, high = 2 * rows + m, 3 * rows
+                late_x = over_x(add(self.mine[low:high], self.from_core[low:high], self.corner_y))
+                self.own = jnp.concatenate(
+                    [
+                        add(self.mine[:m], self.from_core[:m], self.early_x, late_y),
+                        add(self.mine[m:rows], self.from_core[m:rows], late_x, self.early_y),
+                    ]
+                )
+            else:
+                total = self.column[ny - 1]
+                for k in range(ny - 2, -1, -1):
+                    total = add(self.column[k], over_y(total))
+                self.own = total
+            return self.own
+
+        def along(self):
+            def one(g):
+                index = (g - self.groups[0]) % ng
+                index = jnp.minimum(index, len(self.groups) - 1)
+                return lax.dynamic_slice(self.own, (index * self.size, 0), (self.size, LANES))
+
+            total = one(grp - 1)
+            for step in range(ng - 1):
+                senders = [g for g in range(ng) if (g - 1 - step) % ng in self.groups]
+                total = add(one(grp - 2 - step), over_z(total, senders))
+            return total
+
+    place = jnp.stack([sec, yy, core]).astype(jnp.int32)
+    every = list(range(ng))
+    dec_red = Reduction(
+        pack(
+            plan, DEC_LAYOUT, plan.dec_regions(), half, ng, place,
+            {
+                EMBED_W: (saved[SENT], dec[EMBED_L]),
+                QKV_W: (dec[H1], dec[QKV_L]),
+                PROJ_W: (dec[ATT], dec[PROJ_L]),
+                UP_W: (dec[H2], dec[UP_L]),
+                DOWN_W: (dec[ACT], cot_rows),
+                POS: (dec[GPOS], dec[GPOS]),
+            },
+            dec[VECS],
+        ),
+        every,
+        half,
     )
-    enc_own = reduce(enc_table, plan.enc_starts, room)
+    grad_sent = after(dec[GSENT], dec_red.mine)
+    up_low, proj_low, grad_middle, enc_vec = mlp_back(grad_sent, saved, enc_weights)
+    up_low = after(up_low, *dec_red.corners())
+    upper, lower = every[near:], every[:near]
+    enc_up = Reduction(
+        pack(
+            plan, ENC_LAYOUT, plan.enc_regions(upper), piece, len(upper), place,
+            {DOWN_W: (saved[ACT], grad_sent), UP_W: (saved[H2], up_low)},
+            enc_vec,
+        ),
+        upper,
+        piece,
+    )
+    grad_middle = after(grad_middle, enc_up.mine, dec_red.sides())
+    in_grad, qkv_low, enc_vec = attention_back(grad_middle, proj_low, micro_rows, saved, enc_weights, enc_vec)
+    qkv_low = after(qkv_low, *enc_up.corners())
+    enc_low = Reduction(
+        pack(
+            plan, ENC_LAYOUT, plan.enc_regions(lower), piece, len(lower), place,
+            {
+                PROJ_W: (saved[ATT], proj_low),
+                QKV_W: (saved[H1], qkv_low),
+                UP_W: (saved[H2], up_low),
+            },
+            enc_vec,
+        ),
+        lower,
+        piece,
+    )
+    dec_sum = dec_red.along()
+    spread_back = [[(2 * z + h, z) for z in range(plan.full)] for h in range(2)]
+    spread_back[0].append((1, plan.full))
+    dec_low, dec_high = (lax.ppermute(dec_sum, GRP, pairs) for pairs in spread_back)
+    dec_rest = lax.ppermute(dec_sum, GRP, [(3, plan.full)])
+    dec_own = jnp.concatenate([dec_low, jnp.where(grp == plan.full, dec_rest, dec_high)])
+    enc_up.sides()
+    up_own = enc_up.along()
+    enc_low.corners()
+    enc_low.sides()
+    enc_own = jnp.where(grp >= near, up_own, enc_low.along())
+
     own = jnp.where(first_section, enc_own, dec_own)
-    other = over_x(jnp.where(first_section, dec_own, enc_own))
-    pair = jnp.concatenate([own, other])
-    column = [pair]
-    for _ in range(ny - 1):
-        column.append(over_y(column[-1]))
-    sources = column + [over_core(c) for c in column]
+    other = jnp.where(first_section, dec_own, enc_own)
+    if ny == 2:
+        from_x, from_y = over_x(other), over_y(own)
+        sources = [own, from_x, from_y, over_y(from_x)]
+        owners = [(sec, yy), (1 - sec, yy), (sec, 1 - yy), (1 - sec, 1 - yy)]
+    else:
+        column = [jnp.concatenate([own, over_x(other)])]
+        for _ in range(ny - 1):
+            column.append(over_y(column[-1]))
+        sources = column
+        owners = [(s, (yy - k) % ny) for k in range(ny) for s in (sec, 1 - sec)]
+    sources = sources + [over_core(block) for block in sources]
     places = []
     for c in (core, 1 - core):
-        for k in range(ny):
-            for s in (sec, 1 - sec):
-                number = (c * 2 + s) * ny + (yy - k) % ny
-                places += [
-                    jnp.where(first_section, 2 * number, number),
-                    jnp.where(first_section, 2 * number + 1, plan.pieces + number),
-                ]
+        for s, y in owners:
+            number = (c * 2 + s) * ny + y
+            places += [
+                jnp.where(first_section, 2 * number, number),
+                jnp.where(first_section, 2 * number + 1, plan.pieces + number),
+            ]
     table = jnp.asarray(plan.segments())[sec, grp].reshape(-1)
-    flat = finish(plan, jnp.stack(places).astype(jnp.int32), table, sources, rest_sum)
-    param_grad = flat.reshape(-1)[: chunk * LANES].reshape(1, chunk * LANES)
+    flat = finish(plan, jnp.stack(places).astype(jnp.int32), table, sources)
+    param_grad = flat.reshape(1, chunk * LANES)
     dec_out = dec[OUT].reshape(IMAGES_ROW, SLOT_PAD, DEC_WIDTH)[:, :SLOTS]
     return (
         dec_out.reshape(1, 1, IMAGES_ROW * SLOTS, DEC_WIDTH),

time: 861 us -> 594 us (0.69)
  waiting for transfers between devices: 405 us -> 200 us
  local copies, waits for them, and re-layouts: 103 us -> 26 us
  starting transfers between devices: 88.7 us -> 116 us
  between operations: 15.3 us -> 1.75 us
  other arithmetic: 35.5 us -> 47.1 us
  Pallas kernels: 206 us -> 195 us
    psum x2 -> x0, waiting for transfers between devices: 183 us -> none  [the longest x1 121 us: per_device(): lax.psum(dec_table[plan.rest_start:plan.rest_start + plan.rest_room], (SE...]
    ppermute x21 -> x17, waiting for transfers between devices: 108 us -> 25.3 us  [over_y(): return lax.ppermute(block, DP, [(d, (d + 2) % nd) for d in range(nd)])]
    unnamed x67 -> x61, local copies, waits for them, and re-layouts: 65 us -> 2.93 us
    ppermute x22 -> x17, waiting for transfers between devices: 51 us -> 98.4 us  [over_x(): return lax.ppermute(block, SEC, [(0, 1), (1, 0)])]
    ppermute x12 -> x22, starting transfers between devices: 35.3 us -> 54.8 us  [over_core(): return lax.ppermute(block, DP, [(d, d ^ 1) for d in range(nd)])]
    ppermute x14 -> x20, starting transfers between devices: 7.65 us -> 24.8 us  [the longest x15 19.1 us: over_z(): return lax.ppermute(block, GRP, [(g, (g + 1) % ng) for g in senders])]
    convert_element_type x11 -> x21, other arithmetic: 21.9 us -> 35.7 us  [add(): return total.astype(bf16)]
    another operation x4 -> x2, local copies, waits for them, and re-layouts: 14.1 us -> 1.28 us  [the longest x1 0.67 us: gather(): return (sources, jnp.stack(places).astype(jnp.int32), early, late)]
  transfers between devices with their start and end apart: 73 -> 78, of which waited for: 29 -> 35; matrix products, arithmetic and copies ran while one was open for 7% -> 9% of each run, Pallas kernels for 4% -> 9%
where the time goes in v1:
time: 594 us; the launch traced here: 586 us
  waiting for transfers between devices  200 us (34%)
  Pallas kernels  195 us (33%)
  starting transfers between devices  116 us (20%)
  other arithmetic  47.1 us (8%)
  local copies, waits for them, and re-layouts  26 us (4%)
    ppermute x17, waiting for transfers between devices, over_x(): return lax.ppermute(block, SEC, [(0, 1), (1, 0)])  98.4 us
    pallas_call x1, Pallas kernels, decode(): pl.pallas_call(decode_kernel, grid=(IMAGES_ROW,), in_specs=[whole(a) for...  85.2 us
    ppermute x15, waiting for transfers between devices, over_z(): return lax.ppermute(block, GRP, [(g, (g + 1) % ng) for g in senders])  61.3 us
    ppermute x22, starting transfers between devices, over_core(): return lax.ppermute(block, DP, [(d, d ^ 1) for d in range(nd)])  54.8 us
    pallas_call x3, Pallas kernels, pack(): pl.pallas_call(partial(pack_kernel, plan, layout, names, regions, size, g...  37.2 us
    convert_element_type x21, other arithmetic, add(): return total.astype(bf16)  35.7 us
    ppermute x17, waiting for transfers between devices, over_y(): return lax.ppermute(block, DP, [(d, (d + 2) % nd) for d in range(nd)])  25.3 us
    pallas_call x2, Pallas kernels, unpack(): pl.pallas_call(partial(unpack_kernel, plan, layout, unit, cut, chunks, [s...  24.7 us
  transfers between devices with their start and end apart: 78, of which 35 were waited for; matrix products, arithmetic and copies ran while one was open for 9% of the time, Pallas kernels for 9%

profile of v1, /device:TPU:1, one launch (start us, length us, event | category | flops | bytes accessed | tf_op | source)
XLA Modules:
  0.0 585.6 jit_solution(14856530841465456728)
XLA Ops:
  0.7 6.8 %dynamic-slice_reduce_fusion.1 = (bf16[114688]{0:T(1024)(128)(2,1)S(1)}, bf16[114688]{0:T(1024)(128)(2,1)S(1)}, bf16[114688]{0:T(1024)(128)(2,1)S(1)}, bf16[114688]{0:T(1024)(128)(2,1)S(1)}) fusion(bf16[1,1772032]{1,0:T(2,128)(2,1)} %param.9, s32[]{:T(128)S(6)} %select_n.360, s32[]{:T(128)S(6)} %select_n.358, s32[]{:T(128)S(6)} %select_n.356, s32[]{:T(128)S(6)} %select_n.362), kind=kLoop, calls=%fused_computation.75 | loop fusion | bytes 1835024 | tf_op jit(solution)/shard_map/dynamic_slice | solution.py:912
  9.6 10.2 %collective-permute-done = bf16[1792,128]{1,0:T(8,128)(2,1)S(1)} collective-permute-done((bf16[1792,128]{1,0:T(8,128)(2,1)S(1)}, bf16[1792,128]{1,0:T(8,128)(2,1)S(1)}, u32[]{:S(2)}, u32[]{:S(2)}) %collective-permute-start) | collective-permute-done | bytes 458784 | tf_op jit(solution)/shard_map/ppermute | solution.py:899
  21.3 11.3 %collective-permute-done.1 = bf16[1792,128]{1,0:T(8,128)(2,1)S(1)} collective-permute-done((bf16[1792,128]{1,0:T(8,128)(2,1)S(1)}, bf16[1792,128]{1,0:T(8,128)(2,1)S(1)}, u32[]{:S(2)}, u32[]{:S(2)}) %collective-permute-start.1) | collective-permute-done | bytes 458784 | tf_op jit(solution)/shard_map/ppermute | solution.py:909
  35.0 10.8 %collective-permute-done.2 = bf16[1792,128]{1,0:T(8,128)(2,1)S(1)} collective-permute-done((bf16[1792,128]{1,0:T(8,128)(2,1)S(1)}, bf16[1792,128]{1,0:T(8,128)(2,1)S(1)}, u32[]{:S(2)}, u32[]{:S(2)}) %collective-permute-start.2) | collective-permute-done | bytes 458784 | tf_op jit(solution)/shard_map/ppermute | solution.py:909
  45.8 6.6 %collective-permute-done.3.refs_1_ = bf16[3584,128]{1,0:T(8,128)(2,1)S(1)} collective-permute-done((bf16[3584,128]{1,0:T(8,128)(2,1)S(1)}, bf16[3584,128]{1,0:T(8,128)(2,1)S(1)}, u32[]{:S(2)}, u32[]{:S(2)}) %collective-permute-start.3) | collective-permute-done | bytes 917536 | tf_op jit(solution)/shard_map/ppermute | solution.py:899
  53.8 2.5 slice_reduce_fusion
  59.1 4.9 collective-permute-done.5
  68.9 4.1 collective-permute-start.7
  76.2 4.2 collective-permute-start.10
  80.4 5.5 collective-permute-done.10
  88.4 10.3 %collective-permute-start.21 = (bf16[3584,128]{1,0:T(8,128)(2,1)S(1)}, bf16[3584,128]{1,0:T(8,128)(2,1)S(1)}, u32[]{:S(2)}, u32[]{:S(2)}) collective-permute-start(bf16[3584,128]{1,0:T(8,128)(2,1)S(1)} %pad_maximum_fusion.1.refs_0_), channel_id=1, source_target_pairs={{0,1},{1,0},{2,3},{3,2},{4,5},{5,4},{6,7},{7,6},{8,9},{9,8},{10,11... | collective-permute-start | bytes 2752520 | tf_op jit(solution)/shard_map/ppermute | solution.py:902
  99.3 7.0 %collective-permute-start.22 = (bf16[3584,128]{1,0:T(8,128)(2,1)S(1)}, bf16[3584,128]{1,0:T(8,128)(2,1)S(1)}, u32[]{:S(2)}, u32[]{:S(2)}) collective-permute-start(bf16[3584,128]{1,0:T(8,128)(2,1)S(1)} %collective-permute-done.3.refs_1_), channel_id=1, source_target_pairs={{0,1},{1,0},{2,3},{3,2},{4,5},{5,4},{6,7},{7,6},{8,9},{9,8},{10,11... | collective-permute-start | bytes 2752520 | tf_op jit(solution)/shard_map/ppermute | solution.py:902
  107.4 6.6 %collective-permute-start.24 = (bf16[1792,128]{1,0:T(8,128)(2,1)S(1)}, bf16[1792,128]{1,0:T(8,128)(2,1)S(1)}, u32[]{:S(2)}, u32[]{:S(2)}) collective-permute-start(bf16[1792,128]{1,0:T(8,128)(2,1)S(1)} %collective-permute-done.13.refs_3_), channel_id=1, source_target_pairs={{0,1},{1,0},{2,3},{3,2},{4,5},{5,4},{6,7},{7,6},{8,9},{9,8},{10,11... | collective-permute-start | bytes 1376264 | tf_op jit(solution)/shard_map/ppermute | solution.py:902
  114.1 12.2 %collective-permute-done.18.refs_14_ = bf16[1792,128]{1,0:T(8,128)(2,1)} collective-permute-done((bf16[1792,128]{1,0:T(8,128)(2,1)S(1)}, bf16[1792,128]{1,0:T(8,128)(2,1)}, u32[]{:S(2)}, u32[]{:S(2)}) %collective-permute-start.18) | collective-permute-done | bytes 458784 | tf_op jit(solution)/shard_map/ppermute | solution.py:899
  129.4 19.6 %collective-permute-done.19.refs_1_ = bf16[3584,128]{1,0:T(8,128)(2,1)S(1)} collective-permute-done((bf16[3584,128]{1,0:T(8,128)(2,1)S(1)}, bf16[3584,128]{1,0:T(8,128)(2,1)S(1)}, u32[]{:S(2)}, u32[]{:S(2)}) %collective-permute-start.19) | collective-permute-done | bytes 917536 | tf_op jit(solution)/shard_map/ppermute | solution.py:899
  160.9 14.4 %unpack.2 = (bf16[768,2304]{1,0:T(8,128)(2,1)}, bf16[768,768]{1,0:T(8,128)(2,1)}, bf16[768,3072]{1,0:T(8,128)(2,1)}, bf16[3072,768]{1,0:T(8,128)(2,1)}, f32[16,3072]{1,0:T(8,128)}) custom-call(s32[64]{0:T(128)} %concatenate.35.place_ref, bf16[3584,128]{1,0:T(8,128)(2,1)} %copy-done.4, bf16[3584,128]{1,0:T(8,128)(2,1)} %copy-done.9, ...), custom_call_target="tpu_custom_call" | custom-call | flops 12000000000 | tf_op jit(solution)/shard_map/unpack/pallas_call | solution.py:682
  177.0 18.2 %encode.1 = (bf16[256,768]{1,0:T(8,128)(2,1)}, bf16[256,768]{1,0:T(8,128)(2,1)}, bf16[256,2304]{1,0:T(8,128)(2,1)}, f32[12,256,256]{2,1,0:T(8,128)}, bf16[256,76...) custom-call(bf16[256,768]{1,0:T(8,128)(2,1)} %bitcast.109, ...), custom_call_target="tpu_custom_call" | custom-call | flops 17999998976 | tf_op jit(solution)/shard_map/encode/pallas_call | solution.py:378
  196.2 10.3 %unpack.3 = (bf16[768,512]{1,0:T(8,128)(2,1)}, bf16[208,512]{1,0:T(8,128)(2,1)}, bf16[512,1536]{1,0:T(8,128)(2,1)}, bf16[512,512]{1,0:T(8,128)(2,1)}, bf16[512,2...) custom-call(s32[64]{0:T(128)} %stack.386.place_ref, bf16[3584,128]{1,0:T(8,128)(2,1)} %copy-done.5, ...), custom_call_target="tpu_custom_call" | custom-call | flops 12000000000 | tf_op jit(solution)/shard_map/unpack/pallas_call | solution.py:682
  206.6 85.2 %decode.1 = (bf16[1040,512]{1,0:T(8,128)(2,1)}, bf16[1040,512]{1,0:T(8,128)(2,1)}, bf16[1040,1536]{1,0:T(8,128)(2,1)}, bf16[1040,512]{1,0:T(8,128)(2,1)}, bf16[1...) custom-call(bf16[256,768]{1,0:T(8,128)(2,1)} %get-tuple-element.70.s, ...), custom_call_target="tpu_custom_call" | custom-call | flops 85000003584 | tf_op jit(solution)/shard_map/decode/pallas_call | solution.py:453
  291.8 19.1 %pack.3 = (bf16[14336,128]{1,0:T(8,128)(2,1)}, bf16[14336,128]{1,0:T(8,128)(2,1)}) custom-call(s32[3]{0:T(128)} %pad_add_fusion.place_ref, bf16[256,768]{1,0:T(8,128)(2,1)} %get-tuple-element.70.sent_ref.refs_0_, bf16[256,512]{1,0:T(8,128)(2,1)} %get-tuple-element.80.refs_1_, bf16[1040,512]{1,0:T(8,128)(2,1)} %get-tuple-element.81.refs_2_, ...), custom_call_target="tpu_custom_call" | custom-call | flops 24999999488 | tf_op jit(solution)/shard_map/pack/pallas_call | solution.py:809
  311.3 6.3 %collective-permute-done.38 = bf16[14336,128]{1,0:T(8,128)(2,1)S(1)} collective-permute-done((bf16[14336,128]{1,0:T(8,128)(2,1)}, bf16[14336,128]{1,0:T(8,128)(2,1)S(1)}, u32[]{:S(2)}, u32[]{:S(2)}) %collective-permute-start.38) | collective-permute-done | bytes 3670048 | tf_op jit(solution)/shard_map/ppermute | solution.py:902
  320.3 10.6 %collective-permute-done.40 = bf16[1792,128]{1,0:T(8,128)(2,1)S(1)} collective-permute-done((bf16[1792,128]{1,0:T(8,128)(2,1)S(1)}, bf16[1792,128]{1,0:T(8,128)(2,1)S(1)}, u32[]{:S(2)}, u32[]{:S(2)}) %collective-permute-start.40) | collective-permute-done | bytes 458784 | tf_op jit(solution)/shard_map/ppermute | solution.py:905
  333.3 9.4 %mlp_back.1 = (bf16[256,3072]{1,0:T(8,128)(2,1)}, bf16[256,768]{1,0:T(8,128)(2,1)}, f32[256,768]{1,0:T(8,128)}, f32[16,3072]{1,0:T(8,128)}) custom-call(bf16[256,768]{1,0:T(8,128)(2,1)} %get-tuple-element.91.grad_ref.refs_1_, f32[256,768]{1,0:T(8,128)} %get-tuple-element.92.middle_ref, bf16[256,3072]{1,0:T(8,128)(2,1)} %get-tuple-element.93.slope_ref, ...), custom_call_target="tpu_custom_call" | custom-call | flops 8999999488 | tf_op jit(solution)/shard_map/mlp_back/pallas_call | solution.py:400
  343.4 8.9 %pack.4 = (bf16[14336,128]{1,0:T(8,128)(2,1)}, bf16[14336,128]{1,0:T(8,128)(2,1)}) custom-call(s32[3]{0:T(128)} %pad_add_fusion.place_ref, bf16[256,3072]{1,0:T(8,128)(2,1)} %get-tuple-element.95.refs_0_, bf16[256,768]{1,0:T(8,128)(2,1)} %get-tuple-element.91.grad_ref.refs_1_, bf16[256,768]{1,0:T(8,128)(2,1)} %get-tuple-element.96.refs_2_.refs_4_, ...), custom_call_target="tpu_custom_call" | custom-call | flops 12000000000 | tf_op jit(solution)/shard_map/pack/pallas_call | solution.py:809
  354.5 6.2 %collective-permute-done.45 = bf16[14336,128]{1,0:T(8,128)(2,1)S(1)} collective-permute-done((bf16[14336,128]{1,0:T(8,128)(2,1)}, bf16[14336,128]{1,0:T(8,128)(2,1)S(1)}, u32[]{:S(2)}, u32[]{:S(2)}) %collective-permute-start.45) | collective-permute-done | bytes 3670048 | tf_op jit(solution)/shard_map/ppermute | solution.py:902
  363.5 10.6 %collective-permute-done.49 = bf16[1792,128]{1,0:T(8,128)(2,1)S(1)} collective-permute-done((bf16[1792,128]{1,0:T(8,128)(2,1)S(1)}, bf16[1792,128]{1,0:T(8,128)(2,1)S(1)}, u32[]{:S(2)}, u32[]{:S(2)}) %collective-permute-start.49) | collective-permute-done | bytes 458784 | tf_op jit(solution)/shard_map/ppermute | solution.py:905
  377.5 8.8 %collective-permute-done.50 = bf16[1792,128]{1,0:T(8,128)(2,1)S(1)} collective-permute-done((bf16[1792,128]{1,0:T(8,128)(2,1)S(1)}, bf16[1792,128]{1,0:T(8,128)(2,1)S(1)}, u32[]{:S(2)}, u32[]{:S(2)}) %collective-permute-start.50) | collective-permute-done | bytes 458784 | tf_op jit(solution)/shard_map/ppermute | solution.py:899
  389.4 12.6 %attention_back.1 = (f32[256,768]{1,0:T(8,128)}, bf16[256,2304]{1,0:T(8,128)(2,1)}, f32[16,3072]{1,0:T(8,128)}) custom-call(f32[256,768]{1,0:T(8,128)} %get-tuple-element.102.grad_middle_ref, bf16[256,768]{1,0:T(8,128)(2,1)} %get-tuple-element.103.proj_low_ref.refs_1_, bf16[256,768]{1,0:T(8,128)(2,1)} %bitcast.110, ...), custom_call_target="tpu_custom_call" | custom-call | flops 10000000000 | tf_op jit(solution)/shard_map/attention_back/pallas_call | solution.py:416
  402.0 9.3 %pack.5 = (bf16[14336,128]{1,0:T(8,128)(2,1)}, bf16[14336,128]{1,0:T(8,128)(2,1)}) custom-call(s32[3]{0:T(128)} %pad_add_fusion.place_ref, bf16[256,768]{1,0:T(8,128)(2,1)} %get-tuple-element.108.refs_0_, bf16[256,768]{1,0:T(8,128)(2,1)} %get-tuple-element.103.proj_low_ref.refs_1_, bf16[256,768]{1,0:T(8,128)(2,1)} %get-tuple-element.109.refs_2_, ...), custom_call_target="tpu_custom_call" | custom-call | flops 12000000000 | tf_op jit(solution)/shard_map/pack/pallas_call | solution.py:809
  411.3 2.7 collective-permute-start.55
  415.9 10.1 %collective-permute-done.43 = bf16[1792,128]{1,0:T(8,128)(2,1)S(1)} collective-permute-done((bf16[1792,128]{1,0:T(8,128)(2,1)S(1)}, bf16[1792,128]{1,0:T(8,128)(2,1)S(1)}, u32[]{:S(2)}, u32[]{:S(2)}) %collective-permute-start.43) | collective-permute-done | bytes 458784 | tf_op jit(solution)/shard_map/ppermute | solution.py:899
  430.7 8.9 %collective-permute-done.41 = bf16[1792,128]{1,0:T(8,128)(2,1)S(1)} collective-permute-done((bf16[1792,128]{1,0:T(8,128)(2,1)S(1)}, bf16[1792,128]{1,0:T(8,128)(2,1)S(1)}, u32[]{:S(2)}, u32[]{:S(2)}) %collective-permute-start.41) | collective-permute-done | bytes 458784 | tf_op jit(solution)/shard_map/ppermute | solution.py:899
  442.4 6.6 %collective-permute-done.65 = bf16[896,128]{1,0:T(8,128)(2,1)S(1)} collective-permute-done((bf16[896,128]{1,0:T(8,128)(2,1)S(1)}, bf16[896,128]{1,0:T(8,128)(2,1)S(1)}, u32[]{:S(2)}, u32[]{:S(2)}) %collective-permute-start.65) | collective-permute-done | bytes 229408 | tf_op jit(solution)/shard_map/ppermute | solution.py:909
  452.4 4.1 collective-permute-done.66
  459.7 2.5 add_convert_fusion.5
  465.0 2.4 add_convert_fusion.30
  476.8 13.5 %collective-permute-done.57 = bf16[1792,128]{1,0:T(8,128)(2,1)S(1)} collective-permute-done((bf16[1792,128]{1,0:T(8,128)(2,1)S(1)}, bf16[1792,128]{1,0:T(8,128)(2,1)S(1)}, u32[]{:S(2)}, u32[]{:S(2)}) %collective-permute-start.57) | collective-permute-done | bytes 458784 | tf_op jit(solution)/shard_map/ppermute | solution.py:899
  503.7 4.7 collective-permute-done.52
  514.2 4.5 collective-permute-done.53
  521.9 4.0 collective-permute-done.63
  525.9 2.4 add_convert_fusion.1
  528.3 5.5 collective-permute-start.64
  536.4 3.9 collective-permute-done.64
  540.4 4.2 broadcast_select_fusion
  547.0 5.2 collective-permute-done.71.refs_1_
  553.5 13.4 %collective-permute-start.74 = (bf16[1792,128]{1,0:T(8,128)(2,1)S(1)}, bf16[1792,128]{1,0:T(8,128)(2,1)}, u32[]{:S(2)}, u32[]{:S(2)}) collective-permute-start(bf16[1792,128]{1,0:T(8,128)(2,1)S(1)} %broadcast_select_fusion.1.refs_0_), channel_id=1, source_target_pairs={{0,1},{1,0},{2,3},{3,2},{4,5},{5,4},{6,7},{7,6},{8,9},{9,8},{10,11... | collective-permute-start | bytes 1376264 | tf_op jit(solution)/shard_map/ppermute | solution.py:902
  567.4 6.5 %collective-permute-start.77 = (bf16[1792,128]{1,0:T(8,128)(2,1)}, bf16[1792,128]{1,0:T(8,128)(2,1)}, u32[]{:S(2)}, u32[]{:S(2)}) collective-permute-start(bf16[1792,128]{1,0:T(8,128)(2,1)} %collective-permute-done.73.refs_3_), channel_id=1, source_target_pairs={{0,1},{1,0},{2,3},{3,2},{4,5},{5,4},{6,7},{7,6},{8,9},{9,8},{10,11... | collective-permute-start | bytes 1376264 | tf_op jit(solution)/shard_map/ppermute | solution.py:902
  577.2 8.1 %finish.1 = f32[13844,1,128]{2,1,0:T(1,128)} custom-call(s32[16]{0:T(128)} %stack.407.place_ref, s32[57]{0:T(128)} %reshape_squeeze.3.seg_ref, bf16[1792,128]{1,0:T(8,128)(2,1)} %copy-done.8, bf16[1792,128]{1,0:T(8,128)(2,1)} %copy-done.24, bf16[1792,128]{1,0:T(8,128)(2,1)} %copy-done.25, bf16[1792,128]{1,0:T(8,128)(2,1)} %collective-permute-done.73.refs_3_, ...), custom_call_target="tpu_custom_call" | custom-call | flops 8000000000 | tf_op jit(solution)/shard_map/finish/pallas_call | solution.py:867
  (238 shorter events, 118.3 us)
Async XLA Ops:
  7.5 12.4 %collective-permute-start = (bf16[1792,128]{1,0:T(8,128)(2,1)S(1)}, bf16[1792,128]{1,0:T(8,128)(2,1)S(1)}, u32[]{:S(2)}, u32[]{:S(2)}) collective-permute-start(bf16[1792,128]{1,0:T(8,128)(2,1)S(1)} %pad_maximum_fusion.4), channel_id=1, source_target_pairs={{0,16},{16,0},{1,17},{17,1},{2,18},{18,2},{3,19},{19,3},{4,20},{20... | collective-permute-start | bytes 1376264 | tf_op jit(solution)/shard_map/ppermute | solution.py:899
  20.0 12.6 %collective-permute-start.1 = (bf16[1792,128]{1,0:T(8,128)(2,1)S(1)}, bf16[1792,128]{1,0:T(8,128)(2,1)S(1)}, u32[]{:S(2)}, u32[]{:S(2)}) collective-permute-start(bf16[1792,128]{1,0:T(8,128)(2,1)S(1)} %get-tuple-element.137), channel_id=1, source_target_pairs={{0,4},{4,8},{8,12},{12,0},{1,5},{5,9},{9,13},{13,1},{2,6},{6,10},{... | collective-permute-start | bytes 1376264 | tf_op jit(solution)/shard_map/ppermute | solution.py:909
  32.7 19.7 %collective-permute-start.3 = (bf16[3584,128]{1,0:T(8,128)(2,1)S(1)}, bf16[3584,128]{1,0:T(8,128)(2,1)S(1)}, u32[]{:S(2)}, u32[]{:S(2)}) collective-permute-start(bf16[3584,128]{1,0:T(8,128)(2,1)S(1)} %pad_maximum_fusion.1.refs_0_), channel_id=1, source_target_pairs={{0,16},{16,0},{1,17},{17,1},{2,18},{18,2},{3,19},{19,3},{4,20},{20... | collective-permute-start | bytes 2752520 | tf_op jit(solution)/shard_map/ppermute | solution.py:899
  33.7 19.2 %collective-permute-start.4 = (bf16[3584,128]{1,0:T(8,128)(2,1)S(1)}, bf16[3584,128]{1,0:T(8,128)(2,1)S(1)}, u32[]{:S(2)}, u32[]{:S(2)}) collective-permute-start(bf16[3584,128]{1,0:T(8,128)(2,1)S(1)} %pad_maximum_fusion.1.refs_0_), channel_id=1, source_target_pairs={{0,2},{1,3},{2,0},{3,1},{4,6},{5,7},{6,4},{7,5},{8,10},{9,11},{10,... | collective-permute-start | bytes 2752520 | tf_op jit(solution)/shard_map/ppermute | solution.py:905
  35.0 10.8 %collective-permute-start.2 = (bf16[1792,128]{1,0:T(8,128)(2,1)S(1)}, bf16[1792,128]{1,0:T(8,128)(2,1)S(1)}, u32[]{:S(2)}, u32[]{:S(2)}) collective-permute-start(bf16[1792,128]{1,0:T(8,128)(2,1)S(1)} %collective-permute-done.1), channel_id=1, source_target_pairs={{0,4},{4,8},{8,12},{12,0},{1,5},{5,9},{9,13},{13,1},{2,6},{6,10},{... | collective-permute-start | bytes 1376264 | tf_op jit(solution)/shard_map/ppermute | solution.py:909
  66.9 20.4 %collective-permute-start.15 = (bf16[3584,128]{1,0:T(8,128)(2,1)}, bf16[3584,128]{1,0:T(8,128)(2,1)}, u32[]{:S(2)}, u32[]{:S(2)}) collective-permute-start(bf16[3584,128]{1,0:T(8,128)(2,1)} %pad_maximum_fusion.3.refs_10_), channel_id=1, source_target_pairs={{0,16},{16,0},{1,17},{17,1},{2,18},{18,2},{3,19},{19,3},{4,20},{20... | collective-permute-start | bytes 2752520 | tf_op jit(solution)/shard_map/ppermute | solution.py:899
  67.2 39.1 %collective-permute-start.17 = (bf16[3584,128]{1,0:T(8,128)(2,1)}, bf16[3584,128]{1,0:T(8,128)(2,1)}, u32[]{:S(2)}, u32[]{:S(2)}) collective-permute-start(bf16[3584,128]{1,0:T(8,128)(2,1)} %pad_maximum_fusion.3.refs_10_), channel_id=1, source_target_pairs={{0,2},{1,3},{2,0},{3,1},{4,6},{5,7},{6,4},{7,5},{8,10},{9,11},{10,... | collective-permute-start | bytes 2752520 | tf_op jit(solution)/shard_map/ppermute | solution.py:905
  85.9 12.8 %collective-permute-start.11 = (bf16[896,128]{1,0:T(8,128)(2,1)S(1)}, bf16[896,128]{1,0:T(8,128)(2,1)S(1)}, u32[]{:S(2)}, u32[]{:S(2)}) collective-permute-start(bf16[896,128]{1,0:T(8,128)(2,1)S(1)} %collective-permute-done.10), channel_id=1, source_target_pairs={{0,4},{4,8},{8,12},{12,0},{1,5},{5,9},{9,13},{13,1},{2,6},{6,10},{... | collective-permute-start | bytes 688136 | tf_op jit(solution)/shard_map/ppermute | solution.py:909
  88.3 25.7 %collective-permute-start.16 = (bf16[1792,128]{1,0:T(8,128)(2,1)S(1)}, bf16[1792,128]{1,0:T(8,128)(2,1)}, u32[]{:S(2)}, u32[]{:S(2)}) collective-permute-start(bf16[1792,128]{1,0:T(8,128)(2,1)S(1)} %slice.244), channel_id=1, source_target_pairs={{0,2},{1,3},{2,0},{3,1},{4,6},{5,7},{6,4},{7,5},{8,10},{9,11},{10,... | collective-permute-start | bytes 1376264 | tf_op jit(solution)/shard_map/ppermute | solution.py:905
  88.4 38.6 %collective-permute-start.21 = (bf16[3584,128]{1,0:T(8,128)(2,1)S(1)}, bf16[3584,128]{1,0:T(8,128)(2,1)S(1)}, u32[]{:S(2)}, u32[]{:S(2)}) collective-permute-start(bf16[3584,128]{1,0:T(8,128)(2,1)S(1)} %pad_maximum_fusion.1.refs_0_), channel_id=1, source_target_pairs={{0,1},{1,0},{2,3},{3,2},{4,5},{5,4},{6,7},{7,6},{8,9},{9,8},{10,11... | collective-permute-start | bytes 2752520 | tf_op jit(solution)/shard_map/ppermute | solution.py:902
  99.3 29.6 %collective-permute-start.22 = (bf16[3584,128]{1,0:T(8,128)(2,1)S(1)}, bf16[3584,128]{1,0:T(8,128)(2,1)S(1)}, u32[]{:S(2)}, u32[]{:S(2)}) collective-permute-start(bf16[3584,128]{1,0:T(8,128)(2,1)S(1)} %collective-permute-done.3.refs_1_), channel_id=1, source_target_pairs={{0,1},{1,0},{2,3},{3,2},{4,5},{5,4},{6,7},{7,6},{8,9},{9,8},{10,11... | collective-permute-start | bytes 2752520 | tf_op jit(solution)/shard_map/ppermute | solution.py:902
  106.3 22.7 %collective-permute-start.23 = (bf16[3584,128]{1,0:T(8,128)(2,1)S(1)}, bf16[3584,128]{1,0:T(8,128)(2,1)S(1)}, u32[]{:S(2)}, u32[]{:S(2)}) collective-permute-start(bf16[3584,128]{1,0:T(8,128)(2,1)S(1)} %copy-done.11), channel_id=1, source_target_pairs={{0,1},{1,0},{2,3},{3,2},{4,5},{5,4},{6,7},{7,6},{8,9},{9,8},{10,11... | collective-permute-start | bytes 2752520 | tf_op jit(solution)/shard_map/ppermute | solution.py:902
  107.4 19.6 %collective-permute-start.24 = (bf16[1792,128]{1,0:T(8,128)(2,1)S(1)}, bf16[1792,128]{1,0:T(8,128)(2,1)S(1)}, u32[]{:S(2)}, u32[]{:S(2)}) collective-permute-start(bf16[1792,128]{1,0:T(8,128)(2,1)S(1)} %collective-permute-done.13.refs_3_), channel_id=1, source_target_pairs={{0,1},{1,0},{2,3},{3,2},{4,5},{5,4},{6,7},{7,6},{8,9},{9,8},{10,11... | collective-permute-start | bytes 1376264 | tf_op jit(solution)/shard_map/ppermute | solution.py:902
  114.0 12.3 %collective-permute-start.18 = (bf16[1792,128]{1,0:T(8,128)(2,1)S(1)}, bf16[1792,128]{1,0:T(8,128)(2,1)}, u32[]{:S(2)}, u32[]{:S(2)}) collective-permute-start(bf16[1792,128]{1,0:T(8,128)(2,1)S(1)} %slice.245), channel_id=1, source_target_pairs={{0,16},{16,0},{1,17},{17,1},{2,18},{18,2},{3,19},{19,3},{4,20},{20... | collective-permute-start | bytes 1376264 | tf_op jit(solution)/shard_map/ppermute | solution.py:899
  127.1 21.9 %collective-permute-start.19 = (bf16[3584,128]{1,0:T(8,128)(2,1)S(1)}, bf16[3584,128]{1,0:T(8,128)(2,1)S(1)}, u32[]{:S(2)}, u32[]{:S(2)}) collective-permute-start(bf16[3584,128]{1,0:T(8,128)(2,1)S(1)} %pad_maximum_fusion.2.refs_0_), channel_id=1, source_target_pairs={{0,16},{16,0},{1,17},{17,1},{2,18},{18,2},{3,19},{19,3},{4,20},{20... | collective-permute-start | bytes 2752520 | tf_op jit(solution)/shard_map/ppermute | solution.py:899
  127.1 22.7 %collective-permute-start.20 = (bf16[3584,128]{1,0:T(8,128)(2,1)S(1)}, bf16[3584,128]{1,0:T(8,128)(2,1)S(1)}, u32[]{:S(2)}, u32[]{:S(2)}) collective-permute-start(bf16[3584,128]{1,0:T(8,128)(2,1)S(1)} %pad_maximum_fusion.2.refs_0_), channel_id=1, source_target_pairs={{0,2},{1,3},{2,0},{3,1},{4,6},{5,7},{6,4},{7,5},{8,10},{9,11},{10,... | collective-permute-start | bytes 2752520 | tf_op jit(solution)/shard_map/ppermute | solution.py:905
  128.5 31.3 %collective-permute-start.26 = (bf16[3584,128]{1,0:T(8,128)(2,1)}, bf16[3584,128]{1,0:T(8,128)(2,1)}, u32[]{:S(2)}, u32[]{:S(2)}) collective-permute-start(bf16[3584,128]{1,0:T(8,128)(2,1)} %pad_maximum_fusion.3.refs_10_), channel_id=1, source_target_pairs={{0,1},{1,0},{2,3},{3,2},{4,5},{5,4},{6,7},{7,6},{8,9},{9,8},{10,11... | collective-permute-start | bytes 2752520 | tf_op jit(solution)/shard_map/ppermute | solution.py:902
  128.9 32.0 %collective-permute-start.27 = (bf16[3584,128]{1,0:T(8,128)(2,1)}, bf16[3584,128]{1,0:T(8,128)(2,1)}, u32[]{:S(2)}, u32[]{:S(2)}) collective-permute-start(bf16[3584,128]{1,0:T(8,128)(2,1)} %collective-permute-done.15.refs_11_), channel_id=1, source_target_pairs={{0,1},{1,0},{2,3},{3,2},{4,5},{5,4},{6,7},{7,6},{8,9},{9,8},{10,11... | collective-permute-start | bytes 2752520 | tf_op jit(solution)/shard_map/ppermute | solution.py:902
  129.0 31.9 %collective-permute-start.28 = (bf16[3584,128]{1,0:T(8,128)(2,1)}, bf16[3584,128]{1,0:T(8,128)(2,1)}, u32[]{:S(2)}, u32[]{:S(2)}) collective-permute-start(bf16[3584,128]{1,0:T(8,128)(2,1)} %collective-permute-done.17.refs_12_), channel_id=1, source_target_pairs={{0,1},{1,0},{2,3},{3,2},{4,5},{5,4},{6,7},{7,6},{8,9},{9,8},{10,11... | collective-permute-start | bytes 2752520 | tf_op jit(solution)/shard_map/ppermute | solution.py:902
  149.0 10.9 %collective-permute-start.29 = (bf16[1792,128]{1,0:T(8,128)(2,1)}, bf16[1792,128]{1,0:T(8,128)(2,1)}, u32[]{:S(2)}, u32[]{:S(2)}) collective-permute-start(bf16[1792,128]{1,0:T(8,128)(2,1)} %collective-permute-done.16.refs_13_), channel_id=1, source_target_pairs={{0,1},{1,0},{2,3},{3,2},{4,5},{5,4},{6,7},{7,6},{8,9},{9,8},{10,11... | collective-permute-start | bytes 1376264 | tf_op jit(solution)/shard_map/ppermute | solution.py:902
  159.8 35.4 %collective-permute-start.33 = (bf16[3584,128]{1,0:T(8,128)(2,1)S(1)}, bf16[3584,128]{1,0:T(8,128)(2,1)}, u32[]{:S(2)}, u32[]{:S(2)}) collective-permute-start(bf16[3584,128]{1,0:T(8,128)(2,1)S(1)} %copy-done.6), channel_id=1, source_target_pairs={{0,1},{1,0},{2,3},{3,2},{4,5},{5,4},{6,7},{7,6},{8,9},{9,8},{10,11... | collective-permute-start | bytes 2752520 | tf_op jit(solution)/shard_map/ppermute | solution.py:902
  159.9 16.5 %collective-permute-start.31 = (bf16[1792,128]{1,0:T(8,128)(2,1)S(1)}, bf16[1792,128]{1,0:T(8,128)(2,1)S(1)}, u32[]{:S(2)}, u32[]{:S(2)}) collective-permute-start(bf16[1792,128]{1,0:T(8,128)(2,1)S(1)} %slice.246), channel_id=1, source_target_pairs={{0,2},{1,3},{2,0},{3,1},{4,6},{5,7},{6,4},{7,5},{8,10},{9,11},{10,... | collective-permute-start | bytes 1376264 | tf_op jit(solution)/shard_map/ppermute | solution.py:905
  160.1 16.7 %collective-permute-start.32 = (bf16[1792,128]{1,0:T(8,128)(2,1)S(1)}, bf16[1792,128]{1,0:T(8,128)(2,1)S(1)}, u32[]{:S(2)}, u32[]{:S(2)}) collective-permute-start(bf16[1792,128]{1,0:T(8,128)(2,1)S(1)} %slice.247), channel_id=1, source_target_pairs={{0,16},{16,0},{1,17},{17,1},{2,18},{18,2},{3,19},{19,3},{4,20},{20... | collective-permute-start | bytes 1376264 | tf_op jit(solution)/shard_map/ppermute | solution.py:899
  175.3 19.9 %collective-permute-start.34 = (bf16[3584,128]{1,0:T(8,128)(2,1)S(1)}, bf16[3584,128]{1,0:T(8,128)(2,1)}, u32[]{:S(2)}, u32[]{:S(2)}) collective-permute-start(bf16[3584,128]{1,0:T(8,128)(2,1)S(1)} %copy-done.13), channel_id=1, source_target_pairs={{0,1},{1,0},{2,3},{3,2},{4,5},{5,4},{6,7},{7,6},{8,9},{9,8},{10,11... | collective-permute-start | bytes 2752520 | tf_op jit(solution)/shard_map/ppermute | solution.py:902
  176.4 18.9 %collective-permute-start.35 = (bf16[3584,128]{1,0:T(8,128)(2,1)}, bf16[3584,128]{1,0:T(8,128)(2,1)}, u32[]{:S(2)}, u32[]{:S(2)}) collective-permute-start(bf16[3584,128]{1,0:T(8,128)(2,1)} %copy-done.14), channel_id=1, source_target_pairs={{0,1},{1,0},{2,3},{3,2},{4,5},{5,4},{6,7},{7,6},{8,9},{9,8},{10,11... | collective-permute-start | bytes 2752520 | tf_op jit(solution)/shard_map/ppermute | solution.py:902
  176.4 18.8 %collective-permute-start.36 = (bf16[1792,128]{1,0:T(8,128)(2,1)S(1)}, bf16[1792,128]{1,0:T(8,128)(2,1)S(1)}, u32[]{:S(2)}, u32[]{:S(2)}) collective-permute-start(bf16[1792,128]{1,0:T(8,128)(2,1)S(1)} %collective-permute-done.31.refs_3_), channel_id=1, source_target_pairs={{0,1},{1,0},{2,3},{3,2},{4,5},{5,4},{6,7},{7,6},{8,9},{9,8},{10,11... | collective-permute-start | bytes 1376264 | tf_op jit(solution)/shard_map/ppermute | solution.py:902
  176.9 18.4 %collective-permute-start.37 = (bf16[1792,128]{1,0:T(8,128)(2,1)S(1)}, bf16[1792,128]{1,0:T(8,128)(2,1)S(1)}, u32[]{:S(2)}, u32[]{:S(2)}) collective-permute-start(bf16[1792,128]{1,0:T(8,128)(2,1)S(1)} %collective-permute-done.32.refs_4_), channel_id=1, source_target_pairs={{0,1},{1,0},{2,3},{3,2},{4,5},{5,4},{6,7},{7,6},{8,9},{9,8},{10,11... | collective-permute-start | bytes 1376264 | tf_op jit(solution)/shard_map/ppermute | solution.py:902
  319.0 11.8 %collective-permute-start.40 = (bf16[1792,128]{1,0:T(8,128)(2,1)S(1)}, bf16[1792,128]{1,0:T(8,128)(2,1)S(1)}, u32[]{:S(2)}, u32[]{:S(2)}) collective-permute-start(bf16[1792,128]{1,0:T(8,128)(2,1)S(1)} %add_convert_fusion.28), channel_id=1, source_target_pairs={{0,2},{1,3},{2,0},{3,1},{4,6},{5,7},{6,4},{7,5},{8,10},{9,11},{10,... | collective-permute-start | bytes 1376264 | tf_op jit(solution)/shard_map/ppermute | solution.py:905
  332.5 10.9 %collective-permute-start.39 = (bf16[1792,128]{1,0:T(8,128)(2,1)S(1)}, bf16[1792,128]{1,0:T(8,128)(2,1)S(1)}, u32[]{:S(2)}, u32[]{:S(2)}) collective-permute-start(bf16[1792,128]{1,0:T(8,128)(2,1)S(1)} %get-tuple-element.136), channel_id=1, source_target_pairs={{0,16},{16,0},{1,17},{17,1},{2,18},{18,2},{3,19},{19,3},{4,20},{20... | collective-permute-start | bytes 1376264 | tf_op jit(solution)/shard_map/ppermute | solution.py:899
  362.2 11.8 %collective-permute-start.49 = (bf16[1792,128]{1,0:T(8,128)(2,1)S(1)}, bf16[1792,128]{1,0:T(8,128)(2,1)S(1)}, u32[]{:S(2)}, u32[]{:S(2)}) collective-permute-start(bf16[1792,128]{1,0:T(8,128)(2,1)S(1)} %add_convert_fusion.17), channel_id=1, source_target_pairs={{0,2},{1,3},{2,0},{3,1},{4,6},{5,7},{6,4},{7,5},{8,10},{9,11},{10,... | collective-permute-start | bytes 1376264 | tf_op jit(solution)/shard_map/ppermute | solution.py:905
  375.5 10.9 %collective-permute-start.50 = (bf16[1792,128]{1,0:T(8,128)(2,1)S(1)}, bf16[1792,128]{1,0:T(8,128)(2,1)S(1)}, u32[]{:S(2)}, u32[]{:S(2)}) collective-permute-start(bf16[1792,128]{1,0:T(8,128)(2,1)S(1)} %get-tuple-element.124), channel_id=1, source_target_pairs={{0,16},{16,0},{1,17},{17,1},{2,18},{18,2},{3,19},{19,3},{4,20},{20... | collective-permute-start | bytes 1376264 | tf_op jit(solution)/shard_map/ppermute | solution.py:899
  388.5 13.5 %collective-permute-start.47 = (bf16[1792,128]{1,0:T(8,128)(2,1)S(1)}, bf16[1792,128]{1,0:T(8,128)(2,1)S(1)}, u32[]{:S(2)}, u32[]{:S(2)}) collective-permute-start(bf16[1792,128]{1,0:T(8,128)(2,1)S(1)} %get-tuple-element.122), channel_id=1, source_target_pairs={{0,16},{16,0},{1,17},{17,1},{2,18},{18,2},{3,19},{19,3},{4,20},{20... | collective-permute-start | bytes 1376264 | tf_op jit(solution)/shard_map/ppermute | solution.py:899
  411.3 38.6 %collective-permute-start.55 = (bf16[14336,128]{1,0:T(8,128)(2,1)}, bf16[14336,128]{1,0:T(8,128)(2,1)}, u32[]{:S(2)}, u32[]{:S(2)}) collective-permute-start(bf16[14336,128]{1,0:T(8,128)(2,1)} %get-tuple-element.114), channel_id=1, source_target_pairs={{0,1},{1,0},{2,3},{3,2},{4,5},{5,4},{6,7},{7,6},{8,9},{9,8},{10,11... | collective-permute-start | bytes 11010056 | tf_op jit(solution)/shard_map/ppermute | solution.py:902
  414.0 12.1 %collective-permute-start.43 = (bf16[1792,128]{1,0:T(8,128)(2,1)S(1)}, bf16[1792,128]{1,0:T(8,128)(2,1)S(1)}, u32[]{:S(2)}, u32[]{:S(2)}) collective-permute-start(bf16[1792,128]{1,0:T(8,128)(2,1)S(1)} %get-tuple-element.134), channel_id=1, source_target_pairs={{0,16},{16,0},{1,17},{17,1},{2,18},{18,2},{3,19},{19,3},{4,20},{20... | collective-permute-start | bytes 1376264 | tf_op jit(solution)/shard_map/ppermute | solution.py:899
  414.7 11.8 %collective-permute-start.44 = (bf16[1792,128]{1,0:T(8,128)(2,1)S(1)}, bf16[1792,128]{1,0:T(8,128)(2,1)S(1)}, u32[]{:S(2)}, u32[]{:S(2)}) collective-permute-start(bf16[1792,128]{1,0:T(8,128)(2,1)S(1)} %get-tuple-element.135), channel_id=1, source_target_pairs={{0,2},{1,3},{2,0},{3,1},{4,6},{5,7},{6,4},{7,5},{8,10},{9,11},{10,... | collective-permute-start | bytes 1376264 | tf_op jit(solution)/shard_map/ppermute | solution.py:905
  428.7 10.9 %collective-permute-start.41 = (bf16[1792,128]{1,0:T(8,128)(2,1)S(1)}, bf16[1792,128]{1,0:T(8,128)(2,1)S(1)}, u32[]{:S(2)}, u32[]{:S(2)}) collective-permute-start(bf16[1792,128]{1,0:T(8,128)(2,1)S(1)} %get-tuple-element.133), channel_id=1, source_target_pairs={{0,16},{16,0},{1,17},{17,1},{2,18},{18,2},{3,19},{19,3},{4,20},{20... | collective-permute-start | bytes 1376264 | tf_op jit(solution)/shard_map/ppermute | solution.py:899
  467.4 68.0 %collective-permute-start.69 = (bf16[896,128]{1,0:T(8,128)(2,1)}, bf16[896,128]{1,0:T(8,128)(2,1)}, u32[]{:S(2)}, u32[]{:S(2)}) collective-permute-start(bf16[896,128]{1,0:T(8,128)(2,1)} %add_convert_fusion.30), channel_id=1, source_target_pairs={{12,8},{13,9},{14,10},{15,11},{28,24},{29,25},{30,26},{31,27}} | collective-permute-start | bytes 688136 | tf_op jit(solution)/shard_map/ppermute | solution.py:1122
  468.8 66.6 %collective-permute-start.70 = (bf16[896,128]{1,0:T(8,128)(2,1)}, bf16[896,128]{1,0:T(8,128)(2,1)}, u32[]{:S(2)}, u32[]{:S(2)}) collective-permute-start(bf16[896,128]{1,0:T(8,128)(2,1)} %add_convert_fusion.30), channel_id=1, source_target_pairs={{4,0},{12,4},{5,1},{13,5},{6,2},{14,6},{7,3},{15,7},{20,16},{28,20... | collective-permute-start | bytes 688136 | tf_op jit(solution)/shard_map/ppermute | solution.py:1121
  470.3 22.0 %collective-permute-start.46 = (bf16[1792,128]{1,0:T(8,128)(2,1)S(1)}, bf16[1792,128]{1,0:T(8,128)(2,1)S(1)}, u32[]{:S(2)}, u32[]{:S(2)}) collective-permute-start(bf16[1792,128]{1,0:T(8,128)(2,1)S(1)} %get-tuple-element.123), channel_id=1, source_target_pairs={{0,16},{16,0},{1,17},{17,1},{2,18},{18,2},{3,19},{19,3},{4,20},{20... | collective-permute-start | bytes 1376264 | tf_op jit(solution)/shard_map/ppermute | solution.py:899
  473.2 17.0 %collective-permute-start.57 = (bf16[1792,128]{1,0:T(8,128)(2,1)S(1)}, bf16[1792,128]{1,0:T(8,128)(2,1)S(1)}, u32[]{:S(2)}, u32[]{:S(2)}) collective-permute-start(bf16[1792,128]{1,0:T(8,128)(2,1)S(1)} %get-tuple-element.127), channel_id=1, source_target_pairs={{0,16},{16,0},{1,17},{17,1},{2,18},{18,2},{3,19},{19,3},{4,20},{20... | collective-permute-start | bytes 1376264 | tf_op jit(solution)/shard_map/ppermute | solution.py:899
  475.5 18.1 %collective-permute-start.48 = (bf16[1792,128]{1,0:T(8,128)(2,1)S(1)}, bf16[1792,128]{1,0:T(8,128)(2,1)S(1)}, u32[]{:S(2)}, u32[]{:S(2)}) collective-permute-start(bf16[1792,128]{1,0:T(8,128)(2,1)S(1)} %add_convert_fusion.19), channel_id=1, source_target_pairs={{0,2},{1,3},{2,0},{3,1},{4,6},{5,7},{6,4},{7,5},{8,10},{9,11},{10,... | collective-permute-start | bytes 1376264 | tf_op jit(solution)/shard_map/ppermute | solution.py:905
  496.6 11.7 %collective-permute-start.52 = (bf16[1792,128]{1,0:T(8,128)(2,1)S(1)}, bf16[1792,128]{1,0:T(8,128)(2,1)S(1)}, u32[]{:S(2)}, u32[]{:S(2)}) collective-permute-start(bf16[1792,128]{1,0:T(8,128)(2,1)S(1)} %fusion.5), channel_id=1, source_target_pairs={{0,4},{12,0},{1,5},{13,1},{2,6},{14,2},{3,7},{15,3},{16,20},{28,16... | collective-permute-start | bytes 1376264 | tf_op jit(solution)/shard_map/ppermute | solution.py:909
  512.9 13.1 %collective-permute-start.63 = (bf16[1792,128]{1,0:T(8,128)(2,1)S(1)}, bf16[1792,128]{1,0:T(8,128)(2,1)S(1)}, u32[]{:S(2)}, u32[]{:S(2)}) collective-permute-start(bf16[1792,128]{1,0:T(8,128)(2,1)S(1)} %add_convert_fusion.2), channel_id=1, source_target_pairs={{8,12},{12,0},{9,13},{13,1},{10,14},{14,2},{11,15},{15,3},{24,28},... | collective-permute-start | bytes 1376264 | tf_op jit(solution)/shard_map/ppermute | solution.py:909
  521.0 15.4 %collective-permute-start.54 = (bf16[1792,128]{1,0:T(8,128)(2,1)}, bf16[1792,128]{1,0:T(8,128)(2,1)S(1)}, u32[]{:S(2)}, u32[]{:S(2)}) collective-permute-start(bf16[1792,128]{1,0:T(8,128)(2,1)} %add_convert_fusion.12), channel_id=1, source_target_pairs={{4,8},{8,12},{5,9},{9,13},{6,10},{10,14},{7,11},{11,15},{20,24},{2... | collective-permute-start | bytes 1376264 | tf_op jit(solution)/shard_map/ppermute | solution.py:909
  528.3 12.1 %collective-permute-start.64 = (bf16[1792,128]{1,0:T(8,128)(2,1)}, bf16[1792,128]{1,0:T(8,128)(2,1)}, u32[]{:S(2)}, u32[]{:S(2)}) collective-permute-start(bf16[1792,128]{1,0:T(8,128)(2,1)} %add_convert_fusion.1), channel_id=1, source_target_pairs={{0,4},{12,0},{1,5},{13,1},{2,6},{14,2},{3,7},{15,3},{16,20},{28,16... | collective-permute-start | bytes 1376264 | tf_op jit(solution)/shard_map/ppermute | solution.py:909
  545.5 21.5 %collective-permute-start.72 = (bf16[1792,128]{1,0:T(8,128)(2,1)S(1)}, bf16[1792,128]{1,0:T(8,128)(2,1)S(1)}, u32[]{:S(2)}, u32[]{:S(2)}) collective-permute-start(bf16[1792,128]{1,0:T(8,128)(2,1)S(1)} %broadcast_select_fusion.1.refs_0_), channel_id=1, source_target_pairs={{0,2},{1,3},{2,0},{3,1},{4,6},{5,7},{6,4},{7,5},{8,10},{9,11},{10,... | collective-permute-start | bytes 1376264 | tf_op jit(solution)/shard_map/ppermute | solution.py:905
  552.2 15.3 %collective-permute-start.73 = (bf16[1792,128]{1,0:T(8,128)(2,1)S(1)}, bf16[1792,128]{1,0:T(8,128)(2,1)}, u32[]{:S(2)}, u32[]{:S(2)}) collective-permute-start(bf16[1792,128]{1,0:T(8,128)(2,1)S(1)} %collective-permute-done.71.refs_1_), channel_id=1, source_target_pairs={{0,2},{1,3},{2,0},{3,1},{4,6},{5,7},{6,4},{7,5},{8,10},{9,11},{10,... | collective-permute-start | bytes 1376264 | tf_op jit(solution)/shard_map/ppermute | solution.py:905
  553.5 23.6 %collective-permute-start.74 = (bf16[1792,128]{1,0:T(8,128)(2,1)S(1)}, bf16[1792,128]{1,0:T(8,128)(2,1)}, u32[]{:S(2)}, u32[]{:S(2)}) collective-permute-start(bf16[1792,128]{1,0:T(8,128)(2,1)S(1)} %broadcast_select_fusion.1.refs_0_), channel_id=1, source_target_pairs={{0,1},{1,0},{2,3},{3,2},{4,5},{5,4},{6,7},{7,6},{8,9},{9,8},{10,11... | collective-permute-start | bytes 1376264 | tf_op jit(solution)/shard_map/ppermute | solution.py:902
  (60 other events, 1189.5 us)

commit v2 on v1

--- a/solution.py
+++ b/solution.py
@@ -130,7 +130,7 @@
 
 
 def lane_block(group, start=0):
-    return pl.ds(pl.multiple_of(start + group * LANES, LANES), LANES)
+    return slice(start + group * LANES, start + (group + 1) * LANES)
 
 
 def flip(values):
@@ -142,23 +142,24 @@
     scale = f32(head_dim ** (-0.5))
     per_group = LANES // head_dim
 
-    def one_group(group, carry):
+    def one_group(group):
         queries = qkv_ref[:, lane_block(group)]
         keys = qkv_ref[:, lane_block(group, width)]
         values_t = flip(qkv_ref[:, lane_block(group, 2 * width)])
-        for sub in range(per_group):
-            scores = dot_nt(keys, queries * head_mask(sub, head_dim)) * scale
-            scores = keep(scores)
-            expo = jnp.exp(scores - jnp.max(scores, axis=0, keepdims=True))
-            probs = expo * (1.0 / col_sum(expo))
-            probs_ref[group * per_group + sub] = probs
-            rows = pl.ds(pl.multiple_of(group * LANES + sub * head_dim, head_dim), head_dim)
-            joined_ref[rows, :] = dot(
-                values_t[sub * head_dim : (sub + 1) * head_dim], probs.astype(bf16)
-            )
-        return carry
-
-    lax.fori_loop(0, width // LANES, one_group, 0)
+        subs = range(per_group)
+        scores = [dot_nt(keys, queries * head_mask(sub, head_dim)) for sub in subs]
+        scores = [keep(s * scale) for s in scores]
+        expo = [jnp.exp(s - jnp.max(s, axis=0, keepdims=True)) for s in scores]
+        probs = [e * (1.0 / col_sum(e)) for e in expo]
+        for sub in subs:
+            probs_ref[group * per_group + sub] = probs[sub]
+        outs = [
+            dot(values_t[sub * head_dim : (sub + 1) * head_dim], probs[sub].astype(bf16)) for sub in subs
+        ]
+        joined_ref[group * LANES : (group + 1) * LANES, :] = jnp.concatenate(outs, axis=0)
+
+    for group in range(width // LANES):
+        one_group(group)
 
 
 def attention_backward(qkv_ref, probs_ref, grad_ref, low_ref, width, heads):
@@ -166,31 +167,31 @@
     scale = f32(head_dim ** (-0.5))
     per_group = LANES // head_dim
 
-    def one_group(group, carry):
+    def one_group(group):
         queries = qkv_ref[:, lane_block(group)]
         keys = qkv_ref[:, lane_block(group, width)]
         values = qkv_ref[:, lane_block(group, 2 * width)]
         grads = grad_ref[:, lane_block(group)]
         keys_t = flip(keys)
-        grad_values = jnp.zeros(values.shape, f32)
-        grad_keys = jnp.zeros(values.shape, f32)
-        grad_queries = []
-        for sub in range(per_group):
-            mask = head_mask(sub, head_dim)
-            probs = probs_ref[group * per_group + sub]
-            own = grads * mask
-            grad_values += dot(probs.astype(bf16), own)
-            grad_probs = dot_nt(values, own)
-            delta = col_sum(probs * grad_probs)
-            low = (probs * (grad_probs - delta)).astype(bf16)
-            grad_keys += dot(low, queries * mask)
-            grad_queries.append(dot(keys_t[sub * head_dim : (sub + 1) * head_dim], low))
+        subs = range(per_group)
+        masks = [head_mask(sub, head_dim) for sub in subs]
+        own = [grads * m for m in masks]
+        grad_probs = [dot_nt(values, o) for o in own]
+        probs = [probs_ref[group * per_group + sub] for sub in subs]
+        grad_values = sum(dot(p.astype(bf16), o) for p, o in zip(probs, own))
+        low = [
+            (p * (g - col_sum(p * g))).astype(bf16) for p, g in zip(probs, grad_probs)
+        ]
+        grad_keys = sum(dot(l, queries * m) for l, m in zip(low, masks))
+        grad_queries = [
+            dot(keys_t[sub * head_dim : (sub + 1) * head_dim], low[sub]) for sub in subs
+        ]
         low_ref[:, lane_block(group)] = (jnp.concatenate(grad_queries, axis=0).T * scale).astype(bf16)
         low_ref[:, lane_block(group, width)] = (grad_keys * scale).astype(bf16)
         low_ref[:, lane_block(group, 2 * width)] = grad_values.astype(bf16)
-        return carry
-
-    lax.fori_loop(0, width // LANES, one_group, 0)
+
+    for group in range(width // LANES):
+        one_group(group)
 
 
 def encode_kernel(
@@ -217,7 +218,7 @@
     normed2_ref[...] = (hat * vec[4:5, :width] + vec[5:6, :width]).astype(bf16)
     joined_ref[...] = jnp.zeros_like(joined_ref)
     total = jnp.zeros((inputs.shape[0], width), f32)
-    part = 512
+    part = 1536
     for start in range(0, hidden, part):
         cols = slice(start, start + part)
         upward = dot(normed2_ref[...], up_w[:, cols]) + vec[6:7, cols]
@@ -237,7 +238,7 @@
     vec_grad[...] = jnp.zeros_like(vec_grad)
     vec_grad[7:8, :width] = col_sum(grad_out.astype(f32))
     grad_normed2 = jnp.zeros((grad_out.shape[0], width), f32)
-    part = 512
+    part = 3072
     for start in range(0, hidden, part):
         cols = slice(start, start + part)
         low = (dot_nt(grad_out, down_w[cols, :]) * slope_ref[:, cols]).astype(bf16)
@@ -316,7 +317,7 @@
     add_vec(7, col_sum(cot.astype(f32)))
     total = jnp.zeros((length, width), f32)
     grad_normed2 = jnp.zeros((length, width), f32)
-    part = 512
+    part = 1024
     for start in range(0, hidden, part):
         cols = slice(start, start + part)
         upward = dot(normed2_ref[...], up_w[:, cols]) + vec[6:7, cols]
@@ -361,7 +362,7 @@
 
 
 def cost(microseconds):
-    return pl.CostEstimate(flops=int(microseconds * 1e9), bytes_accessed=0, transcendentals=0)
+    return pl.CostEstimate(flops=int(microseconds * 1e11), bytes_accessed=int(microseconds * 3e8), transcendentals=0)
 
 
 def params_of(**extra):
@@ -504,13 +505,15 @@
         self.piece = up_to(-(-self.chunk // self.pieces), 64)
         self.half = self.piece // 2
         self.room = self.piece * self.pieces
+        self.tables = 4 if self.ny == 2 else 2
+        self.units = 2 * self.pieces
         self.full = self.ng // 2
         self.rest = flat_starts(DEC_LAYOUT)[1] - self.full * self.chunk
         assert 0 < self.rest <= self.chunk
-        whole = self.chunk // self.half * self.half
-        last_piece_used = whole == self.room - self.half
-        free = self.half - (self.chunk - whole) if last_piece_used else self.half
-        self.part_in = free // 16 * 16
+        self.unit = up_to(-(-self.chunk // (self.units - 1)), 64)
+        self.dec_room = self.unit * self.units
+        whole = self.chunk // self.unit * self.unit
+        self.part_in = self.unit if whole < self.dec_room - self.unit else 0
         self.parts_in = -(-self.rest // self.part_in)
         assert self.parts_in <= self.full
         self.enc_starts = [self.kept_row(ENC_LAYOUT, z * self.chunk) // 16 * 16 for z in range(self.ng)]
@@ -537,22 +540,35 @@
                 return kept[name] + flat_row - flat[name]
         return kept[name] + rows_of(extent)
 
-    def ranges(self, first, count, cut, chunks):
+    def ranges(self, first, count, cut, chunks, chunk_room):
         found = []
         whole = self.chunk // cut * cut
         while count:
             z, row = divmod(first, self.chunk)
             if z >= chunks:
                 k, row = divmod(row, self.part_in)
-                here, room = (k + 1) * self.room - self.half + row, self.part_in - row
+                here, room = (k + 1) * chunk_room - cut + row, self.part_in - row
             elif row < whole:
-                here, room = z * self.room + row, whole - row
+                here, room = z * chunk_room + row, whole - row
             else:
-                here, room = z * self.room + row + cut - (self.chunk - whole), self.chunk - row
+                here, room = z * chunk_room + row + cut - (self.chunk - whole), self.chunk - row
             take = min(count, room)
             found.append((here, take))
             first, count = first + take, count - take
         return found
+
+    def packed_row(self, size, groups, group_first, index, row, away_x, away_y):
+        owner = away_x * self.ny + away_y
+        turned = away_y * 2 + away_x
+        if self.ny != 2:
+            first = index * (2 * self.ny) + owner if group_first else owner * groups + index
+            return first * size + row
+        if group_first:
+            second, row = divmod(row, size // 2)
+            return index * (4 * size) + second * (2 * size) + (turned if second else owner) * (size // 2) + row
+        second, index = divmod(index, groups // 2)
+        half = groups // 2 * size
+        return second * (4 * half) + (turned if second else owner) * half + index * size + row
 
     def enc_regions(self, groups):
         return [(self.enc_starts[z], self.enc_ends[z], k, 0) for k, z in enumerate(groups)]
@@ -618,13 +634,13 @@
     return 0
 
 
-def unpack_kernel(plan, layout, unit, cut, chunks, counts, place_ref, *refs):
+def unpack_kernel(plan, layout, unit, cut, chunks, room, counts, place_ref, *refs):
     sources = refs[: len(counts)]
     refs = refs[len(counts) :]
     matrices = [(n, e) for n, e in layout if len(e) == 2]
     outs, vec = refs[: len(matrices)], refs[len(matrices)]
     held, wide, spare, sems = refs[len(matrices) + 1 :]
-    per_chunk = plan.room // unit
+    per_chunk = room // unit
     number = 0
     for source, count in zip(sources, counts):
         for k in range(count):
@@ -636,10 +652,10 @@
 
     def arrive(ranges):
         for start, count in ranges:
-            z = start // plan.room
+            z = start // room
             if z not in arrived:
                 arrived.add(z)
-                part = held.at[pl.ds(z * plan.room, plan.room), :]
+                part = held.at[pl.ds(z * room, room), :]
                 pltpu.make_async_copy(part, part, sems.at[z]).wait()
 
     vec[...] = jnp.zeros_like(vec)
@@ -654,7 +670,7 @@
                 out[...] = jnp.zeros_like(out)
             for first in range(0, depth, step):
                 size = min(step, depth - first)
-                ranges = plan.ranges(flat[name] + first * lanes, size * lanes, cut, chunks)
+                ranges = plan.ranges(flat[name] + first * lanes, size * lanes, cut, chunks, room)
                 arrive(ranges)
                 skip = widen_block(held, wide, spare, ranges)
                 for j in range(lanes):
@@ -662,25 +678,25 @@
                     out[first : first + size, j * LANES : (j + 1) * LANES] = block
         else:
             lanes = extent[0] // LANES
-            ranges = plan.ranges(flat[name], lanes, cut, chunks)
+            ranges = plan.ranges(flat[name], lanes, cut, chunks, room)
             arrive(ranges)
             skip = widen_block(held, wide, spare, ranges)
             row, shift = {QB: (2, 0), VB: (2, 2 * extent[0])}.get(name, (VEC.get(name), 0))
             for j in range(lanes):
                 vec[row : row + 1, shift + j * LANES : shift + (j + 1) * LANES] = wide[skip + j : skip + j + 1, :]
     for z in range(chunks):
-        arrive([(z * plan.room, 1)])
-
-
-def unpack(plan, layout, unit, cut, chunks, place, sources):
+        arrive([(z * room, 1)])
+
+
+def unpack(plan, layout, unit, cut, chunks, room, place, sources):
     matrices = [(n, e) for n, e in layout if len(e) == 2]
     outs = [
         shape((SLOT_PAD if n == POS else e[0], e[1]), bf16) for n, e in matrices
     ] + [shape((VEC_ROWS, 4 * dict(layout)[PB][0]), f32)]
     operands = list(sources)
-    rows = chunks * plan.room
+    rows = chunks * room
     result = pl.pallas_call(
-        partial(unpack_kernel, plan, layout, unit, cut, chunks, [s.shape[0] // unit for s in sources]),
+        partial(unpack_kernel, plan, layout, unit, cut, chunks, room, [s.shape[0] // unit for s in sources]),
         in_specs=[pl.BlockSpec(memory_space=pltpu.SMEM)]
         + [pl.BlockSpec(memory_space=pl.ANY)] * len(operands),
         out_shape=outs,
@@ -697,7 +713,7 @@
     return dict(zip([n for n, _ in matrices] + [VECS], result))
 
 
-def pack_kernel(plan, layout, names, regions, size, groups, place_ref, *refs):
+def pack_kernel(plan, layout, names, regions, size, groups, group_first, place_ref, *refs):
     pairs = {}
     for name in names:
         pairs[name], refs = refs[:2], refs[2:]
@@ -716,10 +732,13 @@
             start, stop = max(first, low), min(first + rows, high)
             while start < stop:
                 number, row = divmod(base + start - low, size)
+                c, s, y = number // (2 * ny), number // ny % 2, number % ny
+                away_x, away_y = lax.rem(s - place_ref[0] + 2, 2), lax.rem(y - place_ref[1] + ny, ny)
                 count = min(stop - start, size - row)
-                c, s, y = number // (2 * ny), number // ny % 2, number % ny
-                owner = lax.rem(s - place_ref[0] + 2, 2) * ny + lax.rem(y - place_ref[1] + ny, ny)
-                target = pl.ds(pl.multiple_of(owner * (groups * size), 16) + index * size + row, count)
+                if group_first:
+                    count = min(count, size // 2 - row % (size // 2))
+                where = plan.packed_row(size, groups, group_first, index, row, away_x, away_y)
+                target = pl.ds(pl.multiple_of(where, 16), count)
                 block = source.at[pl.ds(start - first, count), :]
                 for same, table in ((True, mine), (False, theirs)):
 
@@ -788,6 +807,130 @@
     pltpu.make_async_copy(block, block, sems.at[2]).wait()
 
 
+def pack_enc_kernel(plan, names, regions, size, groups, place_ref, *refs):
+    pairs = {}
+    for name in names:
+        pairs[name], refs = refs[:4], refs[4:]
+    vec, vec_other, *tables = refs[: 2 + plan.tables]
+    wide, stage, small, sems = refs[2 + plan.tables :]
+    kept, _ = kept_starts(ENC_LAYOUT)
+    extents = dict(ENC_LAYOUT)
+    ny = plan.ny
+
+    def pieces(first, rows, core):
+        for low, high, index, base in regions:
+            start, stop = max(first, low), min(first + rows, high)
+            while start < stop:
+                number, row = divmod(base + start - low, size)
+                count = min(stop - start, size - row)
+                if number // (2 * ny) == core:
+                    yield start - first, count, index, row, number // ny % 2, number % ny
+                start += count
+
+    def send(source, first, rows, sem, core):
+        moved = 0
+        for skip, count, index, row, s, y in pieces(first, rows, core):
+            away_x, away_y = lax.rem(s - place_ref[0] + 2, 2), lax.rem(y - place_ref[1] + ny, ny)
+            if ny == 2 and index >= groups // 2:
+                keep, away, other, index = tables[2:], away_y, away_x, index - groups // 2
+            else:
+                keep, away, other = tables[:2], away_x, away_y
+            length = (groups // 2 if ny == 2 else groups) * size
+            target = pl.ds(pl.multiple_of(other * length, 16) + index * size + row, count)
+            block = source.at[pl.ds(skip, count), :]
+            for k in range(2):
+
+                @pl.when(away == k)
+                def _():
+                    pltpu.make_async_copy(block, keep[k].at[target, :], sem).start()
+
+            moved += count
+        return moved
+
+    def wait(rows, slot):
+        if rows:
+            block = stage.at[slot, pl.ds(0, rows), :]
+            pltpu.make_async_copy(block, block, sems.at[slot]).wait()
+
+    def run(core):
+        turn = 0
+        pending = [0, 0]
+        for name in names:
+            left, left_other, right, right_other = pairs[name]
+            depth, width = extents[name]
+            lanes = width // LANES
+            step = max(k for k in (128, 256, 384, 512) if depth % k == 0 and k * lanes <= 3072)
+            rows = step * lanes
+            for first in range(0, depth, step):
+                begin = kept[name] + first * lanes
+                if not list(pieces(begin, rows, core)):
+                    continue
+                slot = turn % 2
+                turn += 1
+                columns = flip(left[:, first : first + step])
+                others = flip(left_other[:, first : first + step])
+                part = 256
+                for start in range(0, width, part):
+                    cols = slice(start, start + part)
+                    block = dot(columns, right[:, cols]) + dot(others, right_other[:, cols])
+                    for j in range(part // LANES):
+                        wide[pl.ds(start // LANES + j, step, stride=lanes), :] = block[:, j * LANES : (j + 1) * LANES]
+                wait(pending[slot], slot)
+                stage[slot, 0:rows, :] = wide[0:rows, :].astype(bf16)
+                pending[slot] = send(stage.at[slot], begin, rows, sems.at[slot], core)
+        here = 0
+        total = 0
+        for name, extent in ENC_LAYOUT:
+            if name not in kept_names(names):
+                continue
+            rows = rows_of(extent)
+            room = up_to(rows, 16)
+            if list(pieces(kept[name], room, core)):
+                wide[0:room, :] = jnp.zeros((room, LANES), f32)
+                row, shift = {QB: (2, 0), VB: (2, 2 * extent[0])}.get(name, (VEC.get(name), 0))
+                for j in range(rows):
+                    cols = slice(shift + j * LANES, shift + (j + 1) * LANES)
+                    wide[j : j + 1, :] = vec[row : row + 1, cols] + vec_other[row : row + 1, cols]
+                small[here : here + room, :] = wide[0:room, :].astype(bf16)
+                total += send(small.at[pl.ds(here, room), :], kept[name], room, sems.at[2], core)
+            here += room
+        wait(pending[0], 0)
+        wait(pending[1], 1)
+        if total:
+            block = small.at[pl.ds(0, total), :]
+            pltpu.make_async_copy(block, block, sems.at[2]).wait()
+
+    for core in range(2):
+
+        @pl.when(place_ref[2] == core)
+        def _():
+            run(core)
+
+
+def pack_enc(plan, regions, size, groups, place, pairs, vec, vec_other):
+    names = list(pairs)
+    operands = [a for name in names for a in pairs[name]] + [vec, vec_other]
+    extents = dict(ENC_LAYOUT)
+    small = sum(up_to(rows_of(extents[n]), 16) for n in kept_names(names))
+    rows = 2 * plan.ny * groups * size // plan.tables
+    return pl.pallas_call(
+        partial(pack_enc_kernel, plan, names, regions, size, groups),
+        in_specs=[pl.BlockSpec(memory_space=pltpu.SMEM)]
+        + [pl.BlockSpec(memory_space=pltpu.VMEM)] * len(operands),
+        out_specs=[pl.BlockSpec(memory_space=pl.ANY)] * plan.tables,
+        out_shape=[shape((rows, LANES), bf16)] * plan.tables,
+        scratch_shapes=[
+            pltpu.VMEM((3072, LANES), f32),
+            pltpu.VMEM((2, 3072 + 64, LANES), bf16),
+            pltpu.VMEM((small + 64, LANES), bf16),
+            pltpu.SemaphoreType.DMA((3,)),
+        ],
+        compiler_params=params_of(),
+        cost_estimate=cost(8),
+        name="pack_enc",
+    )(place, *operands)
+
+
 def kept_names(names):
     with_matrix = {
         QKV_W: [N1G, N1B, QB, VB],
@@ -800,14 +943,14 @@
     return [v for n in names for v in with_matrix[n]]
 
 
-def pack(plan, layout, regions, size, groups, place, pairs, vec):
+def pack(plan, layout, regions, size, groups, group_first, place, pairs, vec):
     names = list(pairs)
     operands = [a for name in names for a in pairs[name]] + [vec]
     extents = dict(layout)
     small = sum(up_to(rows_of(extents[n]), 16) for n in kept_names(names))
     rows = 2 * plan.ny * groups * size
     return pl.pallas_call(
-        partial(pack_kernel, plan, layout, names, regions, size, groups),
+        partial(pack_kernel, plan, layout, names, regions, size, groups, group_first),
         in_specs=[pl.BlockSpec(memory_space=pltpu.SMEM)]
         + [pl.BlockSpec(memory_space=pltpu.VMEM)] * len(operands),
         out_specs=[pl.BlockSpec(memory_space=pl.ANY)] * 2,
@@ -882,6 +1025,12 @@
     )(place, segments, *sources)
 
 
+def completed(pairs, count):
+    senders = [k for k in range(count) if k not in [a for a, _ in pairs]]
+    receivers = [k for k in range(count) if k not in [b for _, b in pairs]]
+    return list(pairs) + list(zip(senders, receivers))
+
+
 def after(values, *before):
     return lax.optimization_barrier((values, before))[0]
 
@@ -908,83 +1057,112 @@
         senders = range(ng) if senders is None else senders
         return lax.ppermute(block, GRP, [(g, (g + 1) % ng) for g in senders])
 
-    def share(start):
-        cut = lax.dynamic_slice(params, (0, start * LANES), (1, half * LANES))
-        return cut.astype(f32).reshape(half, LANES).astype(bf16)
-
-    def shares(section):
+    unit = plan.unit
+
+    def share(start, params):
+        cut = lax.dynamic_slice(params, (0, start * LANES), (1, unit * LANES))
+        return cut.astype(f32).reshape(unit, LANES).astype(bf16)
+
+    def shares(section, params):
         number = section * nd + dp
         enc_first = jnp.minimum(number * piece, chunk - piece)
-        dec_first = [jnp.minimum((h * plan.pieces + number) * half, chunk - half) for h in range(2)]
-        starts = [
-            jnp.where(first_section, enc_first, dec_first[0]),
-            jnp.where(first_section, enc_first + half, dec_first[1]),
-        ]
-        return jnp.concatenate([share(s) for s in starts])
-
-    send = shares(1 - sec)
-    got = over_x(send)
-    keep = shares(sec)
-    rest = params[:, : plan.part_in * plan.parts_in * LANES].astype(f32).reshape(-1, LANES).astype(bf16)
-    enc_piece = jnp.where(first_section, keep, got)
-    dec_pieces = jnp.where(first_section, got, keep)
-
-    def gather(parts, first, wait_for=()):
-        here = jnp.concatenate(parts) if len(parts) > 1 else parts[0]
-        here = after(here, *wait_for)
-        size = here.shape[0]
-        if ny == 2:
-            from_x, from_y = over_x(here), over_y(here)
-            corner_0 = over_y(from_x[: size // 2])
-            corner_1 = over_x(from_y[size // 2 :])
-            sources = [here, from_x, from_y, corner_0, corner_1]
-            owners = [(sec, yy), (1 - sec, yy), (sec, 1 - yy), (1 - sec, 1 - yy)]
-            early, late = (from_x, from_y), (corner_0, corner_1)
-        else:
-            column = [here]
-            for _ in range(ny - 1):
-                column.append(over_y(column[-1]))
-            sources = column + [over_x(block) for block in column]
-            owners = [(s, (yy - k) % ny) for s in (sec, 1 - sec) for k in range(ny)]
-            early, late = (column[1],), (sources[-1],)
-        sources = sources + [over_core(block) for block in sources]
-        places = []
-        for c in (core, 1 - core):
-            for s, y in owners:
-                for k in range(len(parts)):
-                    number = (grp - first - k) % ng * plan.pieces + s * nd + y * 2 + c
-                    places += [2 * number, 2 * number + 1]
-        return sources, jnp.stack(places).astype(jnp.int32), early, late
-
-    near = ng // 2
-    enc_parts = [enc_piece]
-    for _ in range(near - 1):
-        enc_parts.append(over_z(enc_parts[-1]))
-    sources_0, places_0, early_0, late_0 = gather(enc_parts[:near], 0)
-    enc_parts.append(over_z(enc_parts[-1]))
-    enc_parts[-1] = after(enc_parts[-1], *early_0)
-    for _ in range(ng - near - 1):
-        enc_parts.append(over_z(enc_parts[-1]))
-    sources_1, places_1, early_1, late_1 = gather(enc_parts[near:], near, late_0)
-    enc_sources, enc_places = sources_0 + sources_1, jnp.concatenate([places_0, places_1])
-
-    dec_pieces, rest = after((dec_pieces, rest), enc_parts[-1])
-    spread = [
-        lax.ppermute(dec_pieces[h * half : (h + 1) * half], GRP, [(z, 2 * z + h) for z in range(plan.full)])
-        for h in range(2)
-    ]
-    dec_piece = jnp.where(grp % 2 == 0, spread[0], spread[1])
+        dec_first = [jnp.minimum((h * plan.pieces + number) * unit, chunk - unit) for h in range(2)]
+        if plan.parts_in == 1:
+            dec_first[0] = jnp.where(grp == plan.full, 0, dec_first[0])
+        return (
+            share(jnp.where(first_section, enc_first, dec_first[0]), params),
+            share(jnp.where(first_section, enc_first + piece - unit, dec_first[1]), params),
+        )
+
+    send = shares(1 - sec, params)
+    keep = shares(sec, after(params, *send))
+
+    def whole_piece(parts):
+        return jnp.concatenate([parts[0][:half], parts[1][unit - half :]])
+
+    routes = [[(z, 2 * z + h) for z in range(plan.full)] for h in range(2)]
+    if plan.parts_in == 1:
+        routes[0].append((plan.full, 1))
+    routes = [completed(route, ng) for route in routes]
+    crossed = []
+    for h in range(2):
+        pairs = [(z, ng + z) for z in range(ng)] + [(ng + a, b) for a, b in routes[h]]
+        crossed.append(lax.ppermute(send[h], (SEC, GRP), pairs))
+    spread = [lax.ppermute(keep[h], GRP, routes[h]) for h in range(2)]
+    enc_piece = jnp.where(first_section, whole_piece(keep), whole_piece(crossed))
+    even, odd = (jnp.where(first_section, crossed[h], spread[h]) for h in range(2))
+    dec_piece = jnp.where(grp % 2 == 0, even, odd)
+    class Gather:
+        def __init__(self, here):
+            self.here = here
+            if ny == 2:
+                self.arrays = [here, over_x(here), over_y(here)]
+                self.owners = [(sec, yy), (1 - sec, yy), (sec, 1 - yy), (1 - sec, 1 - yy)]
+            else:
+                column = [here]
+                for _ in range(ny - 1):
+                    column.append(over_y(column[-1]))
+                self.arrays = column
+                self.owners = [(s, (yy - k) % ny) for s in (sec, 1 - sec) for k in range(ny)]
+
+        def second(self):
+            if ny == 2:
+                middle = self.here.shape[0] // 2
+                self.corners = [self.arrays[1][:middle], self.arrays[2][middle:]]
+            else:
+                self.corners = self.arrays
+            return tuple(self.corners)
+
+        def third(self):
+            if ny == 2:
+                self.arrays += [over_y(self.corners[0]), over_x(self.corners[1])]
+            else:
+                self.arrays = self.arrays + [over_x(block) for block in self.corners]
+            return tuple(self.arrays[-2:])
+
+        def fourth(self, joined=True):
+            arrays = [jnp.concatenate(self.arrays)] if joined else self.arrays
+            return arrays + [over_core(block) for block in arrays]
+
+        def places(self, parts):
+            found = []
+            for c in (core, 1 - core):
+                for s, y in self.owners:
+                    for k in parts:
+                        number = (grp - k) % ng * plan.pieces + s * nd + y * 2 + c
+                        found += [2 * number, 2 * number + 1]
+            return found
+
     last = jnp.logical_and(sec == ns - 1, dp == nd - 1)
-    for k in range(plan.parts_in):
-        part = lax.ppermute(
-            rest[k * plan.part_in : (k + 1) * plan.part_in], GRP, [(plan.full, 2 * k + 1)]
-        )
-        filled = lax.dynamic_update_slice(dec_piece, part, (0, 0))
-        dec_piece = jnp.where(jnp.logical_and(last, grp == 2 * k + 1), filled, dec_piece)
+    if plan.parts_in == 1:
+        dec_piece = jnp.where(jnp.logical_and(last, grp == 1), even, dec_piece)
+    else:
+        for k in range(plan.parts_in):
+            part = share(jnp.minimum(k * unit, chunk - unit), params)
+            part = lax.ppermute(part, GRP, [(plan.full, 2 * k + 1)])
+            dec_piece = jnp.where(jnp.logical_and(last, grp == 2 * k + 1), part, dec_piece)
+    gathers = [Gather(enc_piece)]
+    both = jnp.concatenate([enc_piece, dec_piece])
     dec_parts = [dec_piece]
-    for _ in range(ng - 1):
-        dec_parts.append(over_z(dec_parts[-1]))
-    dec_sources, dec_places, early_2, late_2 = gather(dec_parts, 0, late_1)
+    for k in range(1, ng):
+        both = over_z(both)
+        if k >= 2:
+            both = after(both, *gathers[k - 2].second())
+        if k >= 3:
+            both = after(both, *gathers[k - 3].third())
+        dec_parts.append(both[piece:])
+        gathers.append(Gather(both[:piece]))
+    gathers[-2].second()
+    gathers[-1].second()
+    enc_sources, enc_places = [], []
+    for k, g in enumerate(gathers):
+        if k >= ng - 3:
+            g.third()
+        enc_sources += g.fourth()
+        enc_places += g.places([k])
+    enc_places = jnp.stack(enc_places).astype(jnp.int32)
+    dec_gather = Gather(after(jnp.concatenate(dec_parts), *gathers[-1].corners))
+    dec_places = jnp.stack(dec_gather.places(range(ng))).astype(jnp.int32)
 
     micro_rows = enc_input.reshape(ROW, WIDTH)
     seg = lax.dynamic_index_in_dim(segments, sec, 0, keepdims=False).reshape(ROW)
@@ -993,12 +1171,16 @@
         cot.reshape(IMAGES_ROW, SLOTS, DEC_WIDTH), ((0, 0), (0, SLOT_PAD - SLOTS), (0, 0))
     ).reshape(IMAGES_ROW * SLOT_PAD, DEC_WIDTH)
 
-    enc_weights = unpack(plan, ENC_LAYOUT, half, piece, ng, enc_places, enc_sources)
-    micro_rows = after(micro_rows, *early_2)
+    enc_weights = unpack(plan, ENC_LAYOUT, half, piece, ng, room, enc_places, enc_sources)
+    dec_gather.arrays[1:] = after(dec_gather.arrays[1:], enc_weights[VECS])
+    micro_rows = after(micro_rows, *dec_gather.second())
     saved = dict(
         zip([SENT, H1, QKV, PROBS, ATT, MID, H2, ACT, SLOPE], encode(micro_rows, seg, enc_weights))
     )
-    dec_weights = unpack(plan, DEC_LAYOUT, half // 2, half, plan.full, dec_places, dec_sources)
+    others = {k: over_core(saved[k]) for k in (H1, ATT, H2, ACT)}
+    dec_gather.third()
+    dec_sources = dec_gather.fourth(False)
+    dec_weights = unpack(plan, DEC_LAYOUT, plan.unit // 2, plan.unit, plan.full, plan.dec_room, dec_places, dec_sources)
     dec = dict(
         zip(
             [OUT, H1, QKV_L, ATT, PROJ_L, H2, UP_L, ACT, EMBED_L, GSENT, VECS, GPOS],
@@ -1012,120 +1194,132 @@
             total = total + other.astype(f32)
         return total.astype(bf16)
 
-    class Reduction:
-        def __init__(self, tables, groups, size):
-            self.mine, theirs = tables
-            self.groups, self.size = groups, size
-            self.from_core = over_core(theirs)
-
-        def block(self, k, low=0, high=None):
-            rows = len(self.groups) * self.size
-            low, high = k * rows + low, k * rows + (rows if high is None else high)
-            return add(self.mine[low:high], self.from_core[low:high])
-
-        def corners(self):
-            rows = len(self.groups) * self.size
+    class Square:
+        def __init__(self, tables):
+            self.keep, self.sends = tables[0::2], tables[1::2]
+            self.m = tables[0].shape[0] // ny
+
+        def second(self, *before):
+            m = self.m
             if ny == 2:
-                self.middle = rows // 2
-                self.corner_x = over_x(self.block(3, 0, self.middle))
-                self.corner_y = over_y(self.block(3, self.middle))
-                self.early_y = over_y(self.block(1, self.middle))
-                self.early_x = over_x(self.block(2, 0, self.middle))
-                return self.corner_x, self.corner_y
-            held = [self.block(k) for k in range(2 * ny)]
-            self.column = [add(held[k], over_x(held[ny + k])) for k in range(ny)]
-            return tuple(self.column)
-
-        def sides(self):
-            rows = len(self.groups) * self.size
+                self.ax, self.by = after((over_x(self.sends[0]), over_y(self.sends[1])), *before)
+                self.sends = (add(self.keep[0][m:], self.ax[m:]), add(self.keep[1][m:], self.by[m:]))
+            else:
+                column = add(self.keep[0], after(over_x(self.sends[0]), *before))
+                total = column[(ny - 1) * m :]
+                for k in range(ny - 2, -1, -1):
+                    total = add(column[k * m : (k + 1) * m], over_y(total))
+                self.sends = (total,)
+            return self.sends
+
+        def third(self, *before):
+            m = self.m
             if ny == 2:
-                m = self.middle
-                late_y = over_y(add(self.mine[rows : rows + m], self.from_core[rows : rows + m], self.corner_x))
-                low, high = 2 * rows + m, 3 * rows
-                late_x = over_x(add(self.mine[low:high], self.from_core[low:high], self.corner_y))
-                self.own = jnp.concatenate(
-                    [
-                        add(self.mine[:m], self.from_core[:m], self.early_x, late_y),
-                        add(self.mine[m:rows], self.from_core[m:rows], late_x, self.early_y),
-                    ]
+                ay, bx = after((over_y(self.sends[0]), over_x(self.sends[1])), *before)
+                self.own = (
+                    add(self.keep[0][:m], self.ax[:m], ay), add(self.keep[1][:m], self.by[:m], bx),
                 )
             else:
-                total = self.column[ny - 1]
-                for k in range(ny - 2, -1, -1):
-                    total = add(self.column[k], over_y(total))
-                self.own = total
+                self.own = (self.sends[0][: m // 2], self.sends[0][m // 2 :])
             return self.own
 
-        def along(self):
-            def one(g):
-                index = (g - self.groups[0]) % ng
-                index = jnp.minimum(index, len(self.groups) - 1)
-                return lax.dynamic_slice(self.own, (index * self.size, 0), (self.size, LANES))
-
-            total = one(grp - 1)
-            for step in range(ng - 1):
-                senders = [g for g in range(ng) if (g - 1 - step) % ng in self.groups]
-                total = add(one(grp - 2 - step), over_z(total, senders))
-            return total
+    class Ring:
+        def __init__(self, one):
+            self.one, self.step = one, 0
+            self.total = add(*one(grp - 1))
+
+        def next(self, *before):
+            self.total = after(over_z(self.total), *before)
+            self.step += 1
+            self.total = add(*self.one(grp - 1 - self.step), self.total)
+            return self.total
 
     place = jnp.stack([sec, yy, core]).astype(jnp.int32)
     every = list(range(ng))
-    dec_red = Reduction(
-        pack(
-            plan, DEC_LAYOUT, plan.dec_regions(), half, ng, place,
-            {
-                EMBED_W: (saved[SENT], dec[EMBED_L]),
-                QKV_W: (dec[H1], dec[QKV_L]),
-                PROJ_W: (dec[ATT], dec[PROJ_L]),
-                UP_W: (dec[H2], dec[UP_L]),
-                DOWN_W: (dec[ACT], cot_rows),
-                POS: (dec[GPOS], dec[GPOS]),
-            },
-            dec[VECS],
-        ),
-        every,
-        half,
+    near = ng // 2
+    upper, lower = every[near:], every[:near]
+    dec_mine, dec_theirs = pack(
+        plan, DEC_LAYOUT, plan.dec_regions(), half, ng, True, place,
+        {
+            EMBED_W: (saved[SENT], dec[EMBED_L]),
+            QKV_W: (dec[H1], dec[QKV_L]),
+            PROJ_W: (dec[ATT], dec[PROJ_L]),
+            UP_W: (dec[H2], dec[UP_L]),
+            DOWN_W: (dec[ACT], cot_rows),
+            POS: (dec[GPOS], dec[GPOS]),
+        },
+        dec[VECS],
     )
-    grad_sent = after(dec[GSENT], dec_red.mine)
+    dec_core = over_core(dec_theirs)
+    grad_sent = after(dec[GSENT], dec_mine)
+    grad_other = over_core(grad_sent)
     up_low, proj_low, grad_middle, enc_vec = mlp_back(grad_sent, saved, enc_weights)
-    up_low = after(up_low, *dec_red.corners())
-    upper, lower = every[near:], every[:near]
-    enc_up = Reduction(
-        pack(
-            plan, ENC_LAYOUT, plan.enc_regions(upper), piece, len(upper), place,
-            {DOWN_W: (saved[ACT], grad_sent), UP_W: (saved[H2], up_low)},
-            enc_vec,
-        ),
-        upper,
-        piece,
+    dec_core, grad_other = after((dec_core, grad_other), up_low)
+
+    def dec_block(g):
+        rows = 2 * ny * half
+        return [lax.dynamic_slice(t, (g % ng * rows, 0), (rows, LANES)) for t in (dec_mine, dec_core)]
+
+    dec_ring = Ring(dec_block)
+    up_other, proj_other = over_core(up_low), over_core(proj_low)
+    in_grad, qkv_low, enc_vec = attention_back(
+        after(grad_middle, dec_ring.total), proj_low, micro_rows, saved, enc_weights, enc_vec
     )
-    grad_middle = after(grad_middle, enc_up.mine, dec_red.sides())
-    in_grad, qkv_low, enc_vec = attention_back(grad_middle, proj_low, micro_rows, saved, enc_weights, enc_vec)
-    qkv_low = after(qkv_low, *enc_up.corners())
-    enc_low = Reduction(
-        pack(
-            plan, ENC_LAYOUT, plan.enc_regions(lower), piece, len(lower), place,
-            {
-                PROJ_W: (saved[ATT], proj_low),
-                QKV_W: (saved[H1], qkv_low),
-                UP_W: (saved[H2], up_low),
-            },
-            enc_vec,
-        ),
-        lower,
-        piece,
+    up_other, proj_other = after((up_other, proj_other), qkv_low)
+    qkv_other, vec_other = over_core(qkv_low), over_core(enc_vec)
+    others = after(others, enc_vec)
+    up_tables = pack_enc(
+        plan, plan.enc_regions(upper), piece, len(upper), place,
+        {
+            DOWN_W: (saved[ACT], others[ACT], grad_sent, grad_other),
+            UP_W: (saved[H2], others[H2], up_low, up_other),
+        },
+        enc_vec, vec_other,
     )
-    dec_sum = dec_red.along()
-    spread_back = [[(2 * z + h, z) for z in range(plan.full)] for h in range(2)]
-    spread_back[0].append((1, plan.full))
-    dec_low, dec_high = (lax.ppermute(dec_sum, GRP, pairs) for pairs in spread_back)
-    dec_rest = lax.ppermute(dec_sum, GRP, [(3, plan.full)])
+    qkv_other = after(qkv_other, up_tables[0])
+    low_tables = pack_enc(
+        plan, plan.enc_regions(lower), piece, len(lower), place,
+        {
+            PROJ_W: (saved[ATT], others[ATT], proj_low, proj_other),
+            QKV_W: (saved[H1], others[H1], qkv_low, qkv_other),
+            UP_W: (saved[H2], others[H2], up_low, up_other),
+        },
+        enc_vec, vec_other,
+    )
+    upper_sum, lower_sum = Square(up_tables), Square(low_tables)
+    dec_ring.next(low_tables[0])
+    upper_sum.second(low_tables[0], dec_ring.total)
+    dec_ring.next(*upper_sum.sends)
+    upper_sum.third(dec_ring.total)
+    lower_sum.second(*upper_sum.own)
+    for _ in range(ng - 3):
+        dec_ring.next(*lower_sum.sends)
+    m = dec_ring.total.shape[0] // (2 * ny)
+    if ny == 2:
+        dec_sum = Square([dec_ring.total[k * m : (k + 1) * m] for k in range(4)])
+    else:
+        dec_sum = Square([dec_ring.total[: ny * m], dec_ring.total[ny * m :]])
+    dec_sum.second(*lower_sum.sends)
+    lower_sum.third(*dec_sum.sends)
+    blocks = list(lower_sum.own) + list(upper_sum.own)
+
+    def enc_block(g):
+        g = g % ng
+        if ng == 4:
+            return [jnp.where(g < 2, jnp.where(g == 0, *blocks[:2]), jnp.where(g == 2, *blocks[2:]))]
+        return [lax.dynamic_slice(jnp.concatenate(blocks), (g * piece, 0), (piece, LANES))]
+
+    enc_ring = Ring(enc_block)
+    dec_own = jnp.concatenate(dec_sum.third(enc_ring.total))
+    back = [[(2 * z + h, z) for z in range(plan.full)] for h in range(2)]
+    back[0].append((1, plan.full))
+    back.append([(3, plan.full)])
+    dec_low, dec_high, dec_rest = (lax.ppermute(dec_own, GRP, completed(pairs, ng)) for pairs in back)
+    enc_ring.next()
     dec_own = jnp.concatenate([dec_low, jnp.where(grp == plan.full, dec_rest, dec_high)])
-    enc_up.sides()
-    up_own = enc_up.along()
-    enc_low.corners()
-    enc_low.sides()
-    enc_own = jnp.where(grp >= near, up_own, enc_low.along())
+    for _ in range(ng - 2):
+        enc_ring.next(dec_own)
+    enc_own = enc_ring.total
 
     own = jnp.where(first_section, enc_own, dec_own)
     other = jnp.where(first_section, dec_own, enc_own)

time: 594 us -> 452 us (0.76)
  waiting for transfers between devices: 200 us -> 130 us
  Pallas kernels: 195 us -> 157 us
  starting transfers between devices: 116 us -> 91.7 us
  other arithmetic: 47.1 us -> 24.2 us
  local copies, waits for them, and re-layouts: 26 us -> 38.9 us
    ppermute x17, waiting for transfers between devices: 98.4 us -> 54.5 us  [over_x(): return lax.ppermute(block, SEC, [(0, 1), (1, 0)])]
    pallas_call x1, Pallas kernels: 85.2 us -> 54.4 us  [decode(): pl.pallas_call(decode_kernel, grid=(IMAGES_ROW,), in_specs=[whole(a) for...]
    convert_element_type x21 -> x13, other arithmetic: 35.7 us -> 17.1 us  [add(): return total.astype(bf16)]
    ppermute x15 -> x9, starting transfers between devices: 19.1 us -> 0.72 us  [over_z(): return lax.ppermute(block, GRP, [(g, (g + 1) % ng) for g in senders])]
    pallas_call x3 -> x1, Pallas kernels: 37.2 us -> 19.1 us  [pack(): pl.pallas_call(partial(pack_kernel, plan, layout, names, regions, size, g...]
    ppermute x17 -> x18, waiting for transfers between devices: 25.3 us -> 7.7 us  [over_y(): return lax.ppermute(block, DP, [(d, (d + 2) % nd) for d in range(nd)])]
    pallas_call x2 -> x4, Pallas kernels: 24.7 us -> 42 us  [the longest x2 24.8 us: unpack(): pl.pallas_call(partial(unpack_kernel, plan, layout, unit, cut, chunks, ro...]
    ppermute x22 -> x23, starting transfers between devices: 54.8 us -> 42.4 us  [over_core(): return lax.ppermute(block, DP, [(d, d ^ 1) for d in range(nd)])]
  transfers between devices with their start and end apart: 78 -> 74, of which waited for: 35 -> 29; matrix products, arithmetic and copies ran while one was open for 9% -> 12% of each run, Pallas kernels for 9% -> 34%
where the time goes in v2:
time: 452 us; the launch traced here: 444 us
  Pallas kernels  157 us (35%)
  waiting for transfers between devices  130 us (29%)
  starting transfers between devices  91.7 us (20%)
  local copies, waits for them, and re-layouts  38.9 us (9%)
  other arithmetic  24.2 us (5%)
    ppermute x9, waiting for transfers between devices, over_z(): return lax.ppermute(block, GRP, [(g, (g + 1) % ng) for g in senders])  55 us
    ppermute x17, waiting for transfers between devices, over_x(): return lax.ppermute(block, SEC, [(0, 1), (1, 0)])  54.5 us
    pallas_call x1, Pallas kernels, decode(): pl.pallas_call(decode_kernel, grid=(IMAGES_ROW,), in_specs=[whole(a) for...  54.4 us
    ppermute x23, starting transfers between devices, over_core(): return lax.ppermute(block, DP, [(d, d ^ 1) for d in range(nd)])  42.4 us
    pallas_call x2, Pallas kernels, unpack(): pl.pallas_call(partial(unpack_kernel, plan, layout, unit, cut, chunks, ro...  24.8 us
    ppermute x17, starting transfers between devices, over_x(): return lax.ppermute(block, SEC, [(0, 1), (1, 0)])  22.8 us
    pallas_call x1, Pallas kernels, pack(): pl.pallas_call(partial(pack_kernel, plan, layout, names, regions, size, g...  19.1 us
    pallas_call x2, Pallas kernels, pack_enc(): pl.pallas_call(partial(pack_enc_kernel, plan, names, regions, size, group...  17.2 us
  transfers between devices with their start and end apart: 74, of which 29 were waited for; matrix products, arithmetic and copies ran while one was open for 12% of the time, Pallas kernels for 34%

profile of v2, /device:TPU:1, one launch (start us, length us, event | category | flops | bytes accessed | tf_op | source)
XLA Modules:
  0.0 443.7 jit_solution(8242394069537230608)
XLA Ops:
  0.7 4.0 dynamic-slice_reduce_fusion.3
  4.7 2.1 collective-permute-start
  6.8 4.0 dynamic-slice_reduce_fusion.1
  11.5 4.0 collective-permute-start.3
  15.5 3.8 dynamic-slice_reduce_fusion.5
  19.3 2.1 collective-permute-done.2
  22.4 4.0 collective-permute-done.3
  26.6 5.9 %collective-permute-start.6 = (bf16[1792,128]{1,0:T(8,128)(2,1)S(1)}, bf16[1792,128]{1,0:T(8,128)(2,1)S(1)}, u32[]{:S(2)}, u32[]{:S(2)}) collective-permute-start(bf16[1792,128]{1,0:T(8,128)(2,1)S(1)} %get-tuple-element.187), channel_id=1, source_target_pairs={{0,16},{16,0},{1,17},{17,1},{2,18},{18,2},{3,19},{19,3},{4,20},{20... | collective-permute-start | bytes 1376264 | tf_op jit(solution)/shard_map/ppermute | solution.py:1048
  33.7 8.0 %collective-permute-done.6 = bf16[1792,128]{1,0:T(8,128)(2,1)S(1)} collective-permute-done((bf16[1792,128]{1,0:T(8,128)(2,1)S(1)}, bf16[1792,128]{1,0:T(8,128)(2,1)S(1)}, u32[]{:S(2)}, u32[]{:S(2)}) %collective-permute-start.6) | collective-permute-done | bytes 458784 | tf_op jit(solution)/shard_map/ppermute | solution.py:1048
  46.0 4.8 %collective-permute-start.9 = (bf16[1792,128]{1,0:T(8,128)(2,1)S(1)}, bf16[1792,128]{1,0:T(8,128)(2,1)S(1)}, u32[]{:S(2)}, u32[]{:S(2)}) collective-permute-start(bf16[1792,128]{1,0:T(8,128)(2,1)S(1)} %get-tuple-element.199), channel_id=1, source_target_pairs={{0,16},{16,0},{1,17},{17,1},{2,18},{18,2},{3,19},{19,3},{4,20},{20... | collective-permute-start | bytes 1376264 | tf_op jit(solution)/shard_map/ppermute | solution.py:1048
  54.2 4.9 %collective-permute-done.9 = bf16[1792,128]{1,0:T(8,128)(2,1)S(1)} collective-permute-done((bf16[1792,128]{1,0:T(8,128)(2,1)S(1)}, bf16[1792,128]{1,0:T(8,128)(2,1)S(1)}, u32[]{:S(2)}, u32[]{:S(2)}) %collective-permute-start.9) | collective-permute-done | bytes 458784 | tf_op jit(solution)/shard_map/ppermute | solution.py:1048
  62.6 5.5 %collective-permute-done.5 = bf16[2752,128]{1,0:T(8,128)(2,1)S(1)} collective-permute-done((bf16[2752,128]{1,0:T(8,128)(2,1)S(1)}, bf16[2752,128]{1,0:T(8,128)(2,1)S(1)}, u32[]{:S(2)}, u32[]{:S(2)}) %collective-permute-start.5) | collective-permute-done | bytes 704544 | tf_op jit(solution)/shard_map/ppermute | solution.py:1058
  70.5 4.2 collective-permute-start.17
  79.9 3.6 collective-permute-done.8
  85.9 5.3 %collective-permute-start.20 = (bf16[7168,128]{1,0:T(8,128)(2,1)}, bf16[7168,128]{1,0:T(8,128)(2,1)}, u32[]{:S(2)}, u32[]{:S(2)}) collective-permute-start(bf16[7168,128]{1,0:T(8,128)(2,1)} %constant_dynamic-update-slice_fusion.5.refs_2_), channel_id=1, source_target_pairs={{0,1},{1,0},{2,3},{3,2},{4,5},{5,4},{6,7},{7,6},{8,9},{9,8},{10,11... | collective-permute-start | bytes 5505032 | tf_op jit(solution)/shard_map/ppermute | solution.py:1051
  93.6 2.7 collective-permute-done.13
  98.4 2.8 collective-permute-done.26
  102.7 4.6 %collective-permute-start.28 = (bf16[7168,128]{1,0:T(8,128)(2,1)}, bf16[7168,128]{1,0:T(8,128)(2,1)}, u32[]{:S(2)}, u32[]{:S(2)}) collective-permute-start(bf16[7168,128]{1,0:T(8,128)(2,1)} %constant_dynamic-update-slice_fusion.15.refs_6_), channel_id=1, source_target_pairs={{0,1},{1,0},{2,3},{3,2},{4,5},{5,4},{6,7},{7,6},{8,9},{9,8},{10,11... | collective-permute-start | bytes 5505032 | tf_op jit(solution)/shard_map/ppermute | solution.py:1051
  111.1 14.3 %unpack.2 = (bf16[768,2304]{1,0:T(8,128)(2,1)}, bf16[768,768]{1,0:T(8,128)(2,1)}, bf16[768,3072]{1,0:T(8,128)(2,1)}, bf16[3072,768]{1,0:T(8,128)(2,1)}, f32[16,3072]{1,0:T(8,128)}) custom-call(s32[64]{0:T(128)} %stack.389.place_ref, bf16[7168,128]{1,0:T(8,128)(2,1)} %constant_dynamic-update-slice_fusion.refs_0_, ...), custom_call_target="tpu_custom_call" | custom-call | flops 1199999942656 | bytes 3600000000 | tf_op jit(solution)/shard_map/unpack/pallas_call | solution.py:698
  125.4 7.4 %collective-permute-done.15.refs_1_ = bf16[3840,128]{1,0:T(8,128)(2,1)} collective-permute-done((bf16[3840,128]{1,0:T(8,128)(2,1)}, bf16[3840,128]{1,0:T(8,128)(2,1)}, u32[]{:S(2)}, u32[]{:S(2)}) %collective-permute-start.15) | collective-permute-done | bytes 983072 | tf_op jit(solution)/shard_map/ppermute | solution.py:1048
  148.2 2.3 collective-permute-start.35
  150.4 14.9 %encode.1 = (bf16[256,768]{1,0:T(8,128)(2,1)}, bf16[256,768]{1,0:T(8,128)(2,1)}, bf16[256,2304]{1,0:T(8,128)(2,1)}, f32[12,256,256]{2,1,0:T(8,128)}, bf16[256,76...) custom-call(bf16[256,768]{1,0:T(8,128)(2,1)} %bitcast.111, ...), custom_call_target="tpu_custom_call" | custom-call | flops 1799999979520 | bytes 5400000000 | tf_op jit(solution)/shard_map/encode/pallas_call | solution.py:379
  166.0 10.5 %unpack.3 = (bf16[768,512]{1,0:T(8,128)(2,1)}, bf16[208,512]{1,0:T(8,128)(2,1)}, bf16[512,1536]{1,0:T(8,128)(2,1)}, bf16[512,512]{1,0:T(8,128)(2,1)}, bf16[512,2...) custom-call(s32[64]{0:T(128)} %stack.390.place_ref, bf16[3840,128]{1,0:T(8,128)(2,1)} %pad_maximum_fusion.refs_0_, ...), custom_call_target="tpu_custom_call" | custom-call | flops 1199999942656 | bytes 3600000000 | tf_op jit(solution)/shard_map/unpack/pallas_call | solution.py:698
  176.5 54.4 %decode.1 = (bf16[1040,512]{1,0:T(8,128)(2,1)}, bf16[1040,512]{1,0:T(8,128)(2,1)}, bf16[1040,1536]{1,0:T(8,128)(2,1)}, bf16[1040,512]{1,0:T(8,128)(2,1)}, bf16[1...) custom-call(bf16[256,768]{1,0:T(8,128)(2,1)} %get-tuple-element.102., ...), custom_call_target="tpu_custom_call" | custom-call | flops 8499999801344 | bytes 25500000256 | tf_op jit(solution)/shard_map/decode/pallas_call | solution.py:454
  230.9 19.1 %pack.1 = (bf16[14336,128]{1,0:T(8,128)(2,1)}, bf16[14336,128]{1,0:T(8,128)(2,1)}) custom-call(s32[3]{0:T(128)} %pad_add_fusion.place_ref, bf16[256,768]{1,0:T(8,128)(2,1)} %get-tuple-element.102.sent_ref.refs_0_, bf16[256,512]{1,0:T(8,128)(2,1)} %get-tuple-element.112.refs_1_, bf16[1040,512]{1,0:T(8,128)(2,1)} %get-tuple-element.113.refs_2_, ...), custom_call_target="tpu_custom_call" | custom-call | flops 2499999956992 | bytes 7500000256 | tf_op jit(solution)/shard_map/pack/pallas_call | solution.py:952
  250.6 9.2 %mlp_back.1 = (bf16[256,3072]{1,0:T(8,128)(2,1)}, bf16[256,768]{1,0:T(8,128)(2,1)}, f32[256,768]{1,0:T(8,128)}, f32[16,3072]{1,0:T(8,128)}) custom-call(bf16[256,768]{1,0:T(8,128)(2,1)} %get-tuple-element.123.grad_ref.refs_2_, f32[256,768]{1,0:T(8,128)} %get-tuple-element.124.middle_ref, bf16[256,3072]{1,0:T(8,128)(2,1)} %get-tuple-element.125.slope_ref, ...), custom_call_target="tpu_custom_call" | custom-call | flops 899999989760 | bytes 2700000000 | tf_op jit(solution)/shard_map/mlp_back/pallas_call | solution.py:401
  260.3 2.6 add_convert_fusion.3
  263.3 9.4 %attention_back.1 = (f32[256,768]{1,0:T(8,128)}, bf16[256,2304]{1,0:T(8,128)(2,1)}, f32[16,3072]{1,0:T(8,128)}) custom-call(f32[256,768]{1,0:T(8,128)} %get-tuple-element.130.grad_middle_ref, bf16[256,768]{1,0:T(8,128)(2,1)} %get-tuple-element.131.proj_low_ref.refs_2_, bf16[256,768]{1,0:T(8,128)(2,1)} %bitcast.112, ...), custom_call_target="tpu_custom_call" | custom-call | flops 999999995904 | bytes 3000000000 | tf_op jit(solution)/shard_map/attention_back/pallas_call | solution.py:417
  275.0 8.6 %pack_enc.2 = (bf16[3584,128]{1,0:T(8,128)(2,1)}, bf16[3584,128]{1,0:T(8,128)(2,1)}, bf16[3584,128]{1,0:T(8,128)(2,1)}, bf16[3584,128]{1,0:T(8,128)(2,1)}) custom-call(s32[3]{0:T(128)} %pad_add_fusion.place_ref, bf16[256,3072]{1,0:T(8,128)(2,1)} %get-tuple-element.139.refs_0_, bf16[256,3072]{1,0:T(8,128)(2,1)} %collective-permute-done.41.refs_1_, ...), custom_call_target="tpu_custom_call" | custom-call | flops 799999983616 | bytes 2400000000 | tf_op jit(solution)/shard_map/pack_enc/pallas_call | solution.py:916
  284.7 8.6 %pack_enc.3 = (bf16[3584,128]{1,0:T(8,128)(2,1)}, bf16[3584,128]{1,0:T(8,128)(2,1)}, bf16[3584,128]{1,0:T(8,128)(2,1)}, bf16[3584,128]{1,0:T(8,128)(2,1)}) custom-call(s32[3]{0:T(128)} %pad_add_fusion.place_ref, bf16[256,768]{1,0:T(8,128)(2,1)} %get-tuple-element.136.refs_0_, bf16[256,768]{1,0:T(8,128)(2,1)} %collective-permute-done.39.refs_1_, ...), custom_call_target="tpu_custom_call" | custom-call | flops 799999983616 | bytes 2400000000 | tf_op jit(solution)/shard_map/pack_enc/pallas_call | solution.py:916
  293.3 3.8 collective-permute-done.50
  299.1 5.6 %collective-permute-done.48 = bf16[3584,128]{1,0:T(8,128)(2,1)} collective-permute-done((bf16[3584,128]{1,0:T(8,128)(2,1)}, bf16[3584,128]{1,0:T(8,128)(2,1)}, u32[]{:S(2)}, u32[]{:S(2)}) %collective-permute-start.48) | collective-permute-done | bytes 917536 | tf_op jit(solution)/shard_map/ppermute | solution.py:1048
  310.4 11.3 %collective-permute-done.53 = bf16[3584,128]{1,0:T(8,128)(2,1)S(1)} collective-permute-done((bf16[3584,128]{1,0:T(8,128)(2,1)S(1)}, bf16[3584,128]{1,0:T(8,128)(2,1)S(1)}, u32[]{:S(2)}, u32[]{:S(2)}) %collective-permute-start.53) | collective-permute-done | bytes 917536 | tf_op jit(solution)/shard_map/ppermute | solution.py:1058
  325.0 10.6 %collective-permute-done.46 = bf16[3584,128]{1,0:T(8,128)(2,1)S(1)} collective-permute-done((bf16[3584,128]{1,0:T(8,128)(2,1)S(1)}, bf16[3584,128]{1,0:T(8,128)(2,1)S(1)}, u32[]{:S(2)}, u32[]{:S(2)}) %collective-permute-start.46) | collective-permute-done | bytes 917536 | tf_op jit(solution)/shard_map/ppermute | solution.py:1048
  337.7 7.5 %collective-permute-done.56 = bf16[3584,128]{1,0:T(8,128)(2,1)S(1)} collective-permute-done((bf16[3584,128]{1,0:T(8,128)(2,1)S(1)}, bf16[3584,128]{1,0:T(8,128)(2,1)S(1)}, u32[]{:S(2)}, u32[]{:S(2)}) %collective-permute-start.56) | collective-permute-done | bytes 917536 | tf_op jit(solution)/shard_map/ppermute | solution.py:1058
  350.7 2.3 collective-permute-done.57
  356.5 5.8 %collective-permute-done.55 = bf16[1792,128]{1,0:T(8,128)(2,1)S(1)} collective-permute-done((bf16[1792,128]{1,0:T(8,128)(2,1)S(1)}, bf16[1792,128]{1,0:T(8,128)(2,1)S(1)}, u32[]{:S(2)}, u32[]{:S(2)}) %collective-permute-start.55) | collective-permute-done | bytes 458784 | tf_op jit(solution)/shard_map/ppermute | solution.py:1048
  362.6 2.9 select_select_fusion
  367.3 4.8 %collective-permute-start.65 = (bf16[896,128]{1,0:T(8,128)(2,1)S(1)}, bf16[896,128]{1,0:T(8,128)(2,1)S(1)}, u32[]{:S(2)}, u32[]{:S(2)}) collective-permute-start(bf16[896,128]{1,0:T(8,128)(2,1)S(1)} %pad_maximum_fusion.3), channel_id=1, source_target_pairs={{4,0},{12,4},{0,8},{8,12},{5,1},{13,5},{1,9},{9,13},{6,2},{14,6},{... | collective-permute-start | bytes 688136 | tf_op jit(solution)/shard_map/ppermute | solution.py:1317
  372.8 2.2 collective-permute-done.59
  376.4 5.7 %collective-permute-done.65 = bf16[896,128]{1,0:T(8,128)(2,1)S(1)} collective-permute-done((bf16[896,128]{1,0:T(8,128)(2,1)S(1)}, bf16[896,128]{1,0:T(8,128)(2,1)S(1)}, u32[]{:S(2)}, u32[]{:S(2)}) %collective-permute-start.65) | collective-permute-done | bytes 229408 | tf_op jit(solution)/shard_map/ppermute | solution.py:1317
  382.2 11.5 %collective-permute-done.60 = bf16[1792,128]{1,0:T(8,128)(2,1)S(1)} collective-permute-done((bf16[1792,128]{1,0:T(8,128)(2,1)S(1)}, bf16[1792,128]{1,0:T(8,128)(2,1)S(1)}, u32[]{:S(2)}, u32[]{:S(2)}) %collective-permute-start.60) | collective-permute-done | bytes 458784 | tf_op jit(solution)/shard_map/ppermute | solution.py:1058
  395.0 9.5 %collective-permute-done.66 = bf16[1792,128]{1,0:T(8,128)(2,1)} collective-permute-done((bf16[1792,128]{1,0:T(8,128)(2,1)}, bf16[1792,128]{1,0:T(8,128)(2,1)}, u32[]{:S(2)}, u32[]{:S(2)}) %collective-permute-start.66) | collective-permute-done | bytes 458784 | tf_op jit(solution)/shard_map/ppermute | solution.py:1058
  407.4 6.0 %collective-permute-done.67.refs_1_ = bf16[1792,128]{1,0:T(8,128)(2,1)} collective-permute-done((bf16[1792,128]{1,0:T(8,128)(2,1)S(1)}, bf16[1792,128]{1,0:T(8,128)(2,1)}, u32[]{:S(2)}, u32[]{:S(2)}) %collective-permute-start.67) | collective-permute-done | bytes 458784 | tf_op jit(solution)/shard_map/ppermute | solution.py:1048
  413.8 10.2 %collective-permute-start.70 = (bf16[1792,128]{1,0:T(8,128)(2,1)S(1)}, bf16[1792,128]{1,0:T(8,128)(2,1)}, u32[]{:S(2)}, u32[]{:S(2)}) collective-permute-start(bf16[1792,128]{1,0:T(8,128)(2,1)S(1)} %broadcast_select_fusion.1.refs_0_), channel_id=1, source_target_pairs={{0,1},{1,0},{2,3},{3,2},{4,5},{5,4},{6,7},{7,6},{8,9},{9,8},{10,11... | collective-permute-start | bytes 1376264 | tf_op jit(solution)/shard_map/ppermute | solution.py:1051
  424.1 2.5 collective-permute-start.72
  426.6 5.5 %collective-permute-start.73 = (bf16[1792,128]{1,0:T(8,128)(2,1)S(1)}, bf16[1792,128]{1,0:T(8,128)(2,1)}, u32[]{:S(2)}, u32[]{:S(2)}) collective-permute-start(bf16[1792,128]{1,0:T(8,128)(2,1)S(1)} %collective-permute-done.69.refs_3_), channel_id=1, source_target_pairs={{0,1},{1,0},{2,3},{3,2},{4,5},{5,4},{6,7},{7,6},{8,9},{9,8},{10,11... | collective-permute-start | bytes 1376264 | tf_op jit(solution)/shard_map/ppermute | solution.py:1051
  435.3 8.1 %finish.1 = f32[13844,1,128]{2,1,0:T(1,128)} custom-call(s32[16]{0:T(128)} %stack.411.place_ref, s32[57]{0:T(128)} %reshape_squeeze.3.seg_ref, bf16[1792,128]{1,0:T(8,128)(2,1)} %copy-done.9, bf16[1792,128]{1,0:T(8,128)(2,1)} %collective-permute-done.67.refs_1_, bf16[1792,128]{1,0:T(8,128)(2,1)} %copy-done.14, bf16[1792,128]{1,0:T(8,128)(2,1)} %copy-done.15, ...), custom_call_target="tpu_custom_call" | custom-call | flops 799999983616 | bytes 2400000000 | tf_op jit(solution)/shard_map/finish/pallas_call | solution.py:1010
  (218 shorter events, 88.5 us)
Async XLA Ops:
  4.7 14.6 %collective-permute-start = (bf16[960,128]{1,0:T(8,128)(2,1)S(1)}, bf16[960,128]{1,0:T(8,128)(2,1)S(1)}, u32[]{:S(2)}, u32[]{:S(2)}) collective-permute-start(bf16[960,128]{1,0:T(8,128)(2,1)S(1)} %bitcast.108), channel_id=1, source_target_pairs={{0,16},{4,20},{8,24},{12,28},{16,0},{20,8},{24,4},{28,12},{1,17},{... | collective-permute-start | bytes 737288 | tf_op jit(solution)/shard_map/ppermute | solution.py:1090
  6.8 14.7 %collective-permute-start.2 = (bf16[960,128]{1,0:T(8,128)(2,1)S(1)}, bf16[960,128]{1,0:T(8,128)(2,1)S(1)}, u32[]{:S(2)}, u32[]{:S(2)}) collective-permute-start(bf16[960,128]{1,0:T(8,128)(2,1)S(1)} %bitcast.107), channel_id=1, source_target_pairs={{0,16},{4,20},{8,24},{12,28},{16,4},{20,12},{24,0},{28,8},{1,17},{... | collective-permute-start | bytes 737288 | tf_op jit(solution)/shard_map/ppermute | solution.py:1090
  10.8 11.6 %collective-permute-start.1 = (bf16[960,128]{1,0:T(8,128)(2,1)S(1)}, bf16[960,128]{1,0:T(8,128)(2,1)S(1)}, u32[]{:S(2)}, u32[]{:S(2)}) collective-permute-start(bf16[960,128]{1,0:T(8,128)(2,1)S(1)} %bitcast.110), channel_id=1, source_target_pairs={{0,0},{4,8},{8,4},{12,12},{1,1},{5,9},{9,5},{13,13},{2,2},{6,10},{... | collective-permute-start | bytes 737288 | tf_op jit(solution)/shard_map/ppermute | solution.py:1091
  11.5 14.9 %collective-permute-start.3 = (bf16[960,128]{1,0:T(8,128)(2,1)S(1)}, bf16[960,128]{1,0:T(8,128)(2,1)S(1)}, u32[]{:S(2)}, u32[]{:S(2)}) collective-permute-start(bf16[960,128]{1,0:T(8,128)(2,1)S(1)} %bitcast.109), channel_id=1, source_target_pairs={{0,4},{4,12},{8,0},{12,8},{1,5},{5,13},{9,1},{13,9},{2,6},{6,14},{... | collective-permute-start | bytes 737288 | tf_op jit(solution)/shard_map/ppermute | solution.py:1091
  26.5 18.7 %collective-permute-start.4 = (bf16[2752,128]{1,0:T(8,128)(2,1)S(1)}, bf16[2752,128]{1,0:T(8,128)(2,1)S(1)}, u32[]{:S(2)}, u32[]{:S(2)}) collective-permute-start(bf16[2752,128]{1,0:T(8,128)(2,1)S(1)} %pad_maximum_fusion.1), channel_id=1, source_target_pairs={{0,4},{4,8},{8,12},{12,0},{1,5},{5,9},{9,13},{13,1},{2,6},{6,10},{... | collective-permute-start | bytes 2113544 | tf_op jit(solution)/shard_map/ppermute | solution.py:1058
  26.6 15.2 %collective-permute-start.6 = (bf16[1792,128]{1,0:T(8,128)(2,1)S(1)}, bf16[1792,128]{1,0:T(8,128)(2,1)S(1)}, u32[]{:S(2)}, u32[]{:S(2)}) collective-permute-start(bf16[1792,128]{1,0:T(8,128)(2,1)S(1)} %get-tuple-element.187), channel_id=1, source_target_pairs={{0,16},{16,0},{1,17},{17,1},{2,18},{18,2},{3,19},{19,3},{4,20},{20... | collective-permute-start | bytes 1376264 | tf_op jit(solution)/shard_map/ppermute | solution.py:1048
  46.0 13.1 %collective-permute-start.9 = (bf16[1792,128]{1,0:T(8,128)(2,1)S(1)}, bf16[1792,128]{1,0:T(8,128)(2,1)S(1)}, u32[]{:S(2)}, u32[]{:S(2)}) collective-permute-start(bf16[1792,128]{1,0:T(8,128)(2,1)S(1)} %get-tuple-element.199), channel_id=1, source_target_pairs={{0,16},{16,0},{1,17},{17,1},{2,18},{18,2},{3,19},{19,3},{4,20},{20... | collective-permute-start | bytes 1376264 | tf_op jit(solution)/shard_map/ppermute | solution.py:1048
  52.0 16.0 %collective-permute-start.5 = (bf16[2752,128]{1,0:T(8,128)(2,1)S(1)}, bf16[2752,128]{1,0:T(8,128)(2,1)S(1)}, u32[]{:S(2)}, u32[]{:S(2)}) collective-permute-start(bf16[2752,128]{1,0:T(8,128)(2,1)S(1)} %collective-permute-done.4), channel_id=1, source_target_pairs={{0,4},{4,8},{8,12},{12,0},{1,5},{5,9},{9,13},{13,1},{2,6},{6,10},{... | collective-permute-start | bytes 2113544 | tf_op jit(solution)/shard_map/ppermute | solution.py:1058
  59.2 11.4 %collective-permute-start.18 = (bf16[896,128]{1,0:T(8,128)(2,1)S(1)}, bf16[896,128]{1,0:T(8,128)(2,1)S(1)}, u32[]{:S(2)}, u32[]{:S(2)}) collective-permute-start(bf16[896,128]{1,0:T(8,128)(2,1)S(1)} %slice.208), channel_id=1, source_target_pairs={{0,2},{1,3},{2,0},{3,1},{4,6},{5,7},{6,4},{7,5},{8,10},{9,11},{10,... | collective-permute-start | bytes 688136 | tf_op jit(solution)/shard_map/ppermute | solution.py:1054
  60.5 15.0 %collective-permute-start.19 = (bf16[896,128]{1,0:T(8,128)(2,1)S(1)}, bf16[896,128]{1,0:T(8,128)(2,1)S(1)}, u32[]{:S(2)}, u32[]{:S(2)}) collective-permute-start(bf16[896,128]{1,0:T(8,128)(2,1)S(1)} %slice.209), channel_id=1, source_target_pairs={{0,16},{16,0},{1,17},{17,1},{2,18},{18,2},{3,19},{19,3},{4,20},{20... | collective-permute-start | bytes 688136 | tf_op jit(solution)/shard_map/ppermute | solution.py:1048
  68.1 15.4 %collective-permute-start.8 = (bf16[2752,128]{1,0:T(8,128)(2,1)S(1)}, bf16[2752,128]{1,0:T(8,128)(2,1)S(1)}, u32[]{:S(2)}, u32[]{:S(2)}) collective-permute-start(bf16[2752,128]{1,0:T(8,128)(2,1)S(1)} %collective-permute-done.5), channel_id=1, source_target_pairs={{0,4},{4,8},{8,12},{12,0},{1,5},{5,9},{9,13},{13,1},{2,6},{6,10},{... | collective-permute-start | bytes 2113544 | tf_op jit(solution)/shard_map/ppermute | solution.py:1058
  70.5 39.4 %collective-permute-start.17 = (bf16[7168,128]{1,0:T(8,128)(2,1)}, bf16[7168,128]{1,0:T(8,128)(2,1)}, u32[]{:S(2)}, u32[]{:S(2)}) collective-permute-start(bf16[7168,128]{1,0:T(8,128)(2,1)} %constant_dynamic-update-slice_fusion.refs_0_), channel_id=1, source_target_pairs={{0,1},{1,0},{2,3},{3,2},{4,5},{5,4},{6,7},{7,6},{8,9},{9,8},{10,11... | collective-permute-start | bytes 5505032 | tf_op jit(solution)/shard_map/ppermute | solution.py:1051
  77.6 14.3 %collective-permute-start.24 = (bf16[896,128]{1,0:T(8,128)(2,1)S(1)}, bf16[896,128]{1,0:T(8,128)(2,1)S(1)}, u32[]{:S(2)}, u32[]{:S(2)}) collective-permute-start(bf16[896,128]{1,0:T(8,128)(2,1)S(1)} %slice.213), channel_id=1, source_target_pairs={{0,16},{16,0},{1,17},{17,1},{2,18},{18,2},{3,19},{19,3},{4,20},{20... | collective-permute-start | bytes 688136 | tf_op jit(solution)/shard_map/ppermute | solution.py:1048
  84.3 12.0 %collective-permute-start.13 = (bf16[1792,128]{1,0:T(8,128)(2,1)S(1)}, bf16[1792,128]{1,0:T(8,128)(2,1)S(1)}, u32[]{:S(2)}, u32[]{:S(2)}) collective-permute-start(bf16[1792,128]{1,0:T(8,128)(2,1)S(1)} %get-tuple-element.195), channel_id=1, source_target_pairs={{0,16},{16,0},{1,17},{17,1},{2,18},{18,2},{3,19},{19,3},{4,20},{20... | collective-permute-start | bytes 1376264 | tf_op jit(solution)/shard_map/ppermute | solution.py:1048
  84.9 11.5 %collective-permute-start.14 = (bf16[1792,128]{1,0:T(8,128)(2,1)S(1)}, bf16[1792,128]{1,0:T(8,128)(2,1)S(1)}, u32[]{:S(2)}, u32[]{:S(2)}) collective-permute-start(bf16[1792,128]{1,0:T(8,128)(2,1)S(1)} %get-tuple-element.195), channel_id=1, source_target_pairs={{0,2},{1,3},{2,0},{3,1},{4,6},{5,7},{6,4},{7,5},{8,10},{9,11},{10,... | collective-permute-start | bytes 1376264 | tf_op jit(solution)/shard_map/ppermute | solution.py:1054
  85.9 25.1 %collective-permute-start.20 = (bf16[7168,128]{1,0:T(8,128)(2,1)}, bf16[7168,128]{1,0:T(8,128)(2,1)}, u32[]{:S(2)}, u32[]{:S(2)}) collective-permute-start(bf16[7168,128]{1,0:T(8,128)(2,1)} %constant_dynamic-update-slice_fusion.5.refs_2_), channel_id=1, source_target_pairs={{0,1},{1,0},{2,3},{3,2},{4,5},{5,4},{6,7},{7,6},{8,9},{9,8},{10,11... | collective-permute-start | bytes 5505032 | tf_op jit(solution)/shard_map/ppermute | solution.py:1051
  92.6 18.5 %collective-permute-start.25 = (bf16[7168,128]{1,0:T(8,128)(2,1)}, bf16[7168,128]{1,0:T(8,128)(2,1)}, u32[]{:S(2)}, u32[]{:S(2)}) collective-permute-start(bf16[7168,128]{1,0:T(8,128)(2,1)} %constant_dynamic-update-slice_fusion.10.refs_4_), channel_id=1, source_target_pairs={{0,1},{1,0},{2,3},{3,2},{4,5},{5,4},{6,7},{7,6},{8,9},{9,8},{10,11... | collective-permute-start | bytes 5505032 | tf_op jit(solution)/shard_map/ppermute | solution.py:1051
  109.1 23.7 %collective-permute-start.15 = (bf16[3840,128]{1,0:T(8,128)(2,1)}, bf16[3840,128]{1,0:T(8,128)(2,1)}, u32[]{:S(2)}, u32[]{:S(2)}) collective-permute-start(bf16[3840,128]{1,0:T(8,128)(2,1)} %pad_maximum_fusion.refs_0_), channel_id=1, source_target_pairs={{0,16},{16,0},{1,17},{17,1},{2,18},{18,2},{3,19},{19,3},{4,20},{20... | collective-permute-start | bytes 2949128 | tf_op jit(solution)/shard_map/ppermute | solution.py:1048
  109.9 23.4 %collective-permute-start.16 = (bf16[3840,128]{1,0:T(8,128)(2,1)}, bf16[3840,128]{1,0:T(8,128)(2,1)}, u32[]{:S(2)}, u32[]{:S(2)}) collective-permute-start(bf16[3840,128]{1,0:T(8,128)(2,1)} %pad_maximum_fusion.refs_0_), channel_id=1, source_target_pairs={{0,2},{1,3},{2,0},{3,1},{4,6},{5,7},{6,4},{7,5},{8,10},{9,11},{10,... | collective-permute-start | bytes 2949128 | tf_op jit(solution)/shard_map/ppermute | solution.py:1054
  134.4 11.8 %collective-permute-start.29 = (bf16[1920,128]{1,0:T(8,128)(2,1)S(1)}, bf16[1920,128]{1,0:T(8,128)(2,1)}, u32[]{:S(2)}, u32[]{:S(2)}) collective-permute-start(bf16[1920,128]{1,0:T(8,128)(2,1)S(1)} %slice.173), channel_id=1, source_target_pairs={{0,2},{1,3},{2,0},{3,1},{4,6},{5,7},{6,4},{7,5},{8,10},{9,11},{10,... | collective-permute-start | bytes 1474568 | tf_op jit(solution)/shard_map/ppermute | solution.py:1054
  136.6 11.6 %collective-permute-start.30 = (bf16[1920,128]{1,0:T(8,128)(2,1)S(1)}, bf16[1920,128]{1,0:T(8,128)(2,1)}, u32[]{:S(2)}, u32[]{:S(2)}) collective-permute-start(bf16[1920,128]{1,0:T(8,128)(2,1)S(1)} %slice.174), channel_id=1, source_target_pairs={{0,16},{16,0},{1,17},{17,1},{2,18},{18,2},{3,19},{19,3},{4,20},{20... | collective-permute-start | bytes 1474568 | tf_op jit(solution)/shard_map/ppermute | solution.py:1048
  142.7 22.7 %collective-permute-start.31 = (bf16[3840,128]{1,0:T(8,128)(2,1)}, bf16[3840,128]{1,0:T(8,128)(2,1)}, u32[]{:S(2)}, u32[]{:S(2)}) collective-permute-start(bf16[3840,128]{1,0:T(8,128)(2,1)} %pad_maximum_fusion.refs_0_), channel_id=1, source_target_pairs={{0,1},{1,0},{2,3},{3,2},{4,5},{5,4},{6,7},{7,6},{8,9},{9,8},{10,11... | collective-permute-start | bytes 2949128 | tf_op jit(solution)/shard_map/ppermute | solution.py:1051
  144.3 21.7 %collective-permute-start.32 = (bf16[3840,128]{1,0:T(8,128)(2,1)}, bf16[3840,128]{1,0:T(8,128)(2,1)}, u32[]{:S(2)}, u32[]{:S(2)}) collective-permute-start(bf16[3840,128]{1,0:T(8,128)(2,1)} %collective-permute-done.15.refs_1_), channel_id=1, source_target_pairs={{0,1},{1,0},{2,3},{3,2},{4,5},{5,4},{6,7},{7,6},{8,9},{9,8},{10,11... | collective-permute-start | bytes 2949128 | tf_op jit(solution)/shard_map/ppermute | solution.py:1051
  144.3 21.7 %collective-permute-start.33 = (bf16[3840,128]{1,0:T(8,128)(2,1)}, bf16[3840,128]{1,0:T(8,128)(2,1)}, u32[]{:S(2)}, u32[]{:S(2)}) collective-permute-start(bf16[3840,128]{1,0:T(8,128)(2,1)} %collective-permute-done.16.refs_2_), channel_id=1, source_target_pairs={{0,1},{1,0},{2,3},{3,2},{4,5},{5,4},{6,7},{7,6},{8,9},{9,8},{10,11... | collective-permute-start | bytes 2949128 | tf_op jit(solution)/shard_map/ppermute | solution.py:1051
  146.1 19.3 %collective-permute-start.34 = (bf16[1920,128]{1,0:T(8,128)(2,1)}, bf16[1920,128]{1,0:T(8,128)(2,1)}, u32[]{:S(2)}, u32[]{:S(2)}) collective-permute-start(bf16[1920,128]{1,0:T(8,128)(2,1)} %collective-permute-done.29.refs_3_), channel_id=1, source_target_pairs={{0,1},{1,0},{2,3},{3,2},{4,5},{5,4},{6,7},{7,6},{8,9},{9,8},{10,11... | collective-permute-start | bytes 1474568 | tf_op jit(solution)/shard_map/ppermute | solution.py:1051
  148.2 17.7 %collective-permute-start.35 = (bf16[1920,128]{1,0:T(8,128)(2,1)}, bf16[1920,128]{1,0:T(8,128)(2,1)}, u32[]{:S(2)}, u32[]{:S(2)}) collective-permute-start(bf16[1920,128]{1,0:T(8,128)(2,1)} %collective-permute-done.30.refs_4_), channel_id=1, source_target_pairs={{0,1},{1,0},{2,3},{3,2},{4,5},{5,4},{6,7},{7,6},{8,9},{9,8},{10,11... | collective-permute-start | bytes 1474568 | tf_op jit(solution)/shard_map/ppermute | solution.py:1051
  165.3 107.9 %collective-permute-start.41 = (bf16[256,3072]{1,0:T(8,128)(2,1)}, bf16[256,3072]{1,0:T(8,128)(2,1)}, u32[]{:S(2)}, u32[]{:S(2)}) collective-permute-start(bf16[256,3072]{1,0:T(8,128)(2,1)} %get-tuple-element.139.refs_0_), channel_id=1, source_target_pairs={{0,1},{1,0},{2,3},{3,2},{4,5},{5,4},{6,7},{7,6},{8,9},{9,8},{10,11... | collective-permute-start | bytes 4718600 | tf_op jit(solution)/shard_map/ppermute | solution.py:1051
  165.4 107.4 %collective-permute-start.38 = (bf16[256,768]{1,0:T(8,128)(2,1)}, bf16[256,768]{1,0:T(8,128)(2,1)}, u32[]{:S(2)}, u32[]{:S(2)}) collective-permute-start(bf16[256,768]{1,0:T(8,128)(2,1)} %get-tuple-element.137.refs_4_), channel_id=1, source_target_pairs={{0,1},{1,0},{2,3},{3,2},{4,5},{5,4},{6,7},{7,6},{8,9},{9,8},{10,11... | collective-permute-start | bytes 1179656 | tf_op jit(solution)/shard_map/ppermute | solution.py:1051
  165.9 107.3 %collective-permute-start.39 = (bf16[256,768]{1,0:T(8,128)(2,1)}, bf16[256,768]{1,0:T(8,128)(2,1)}, u32[]{:S(2)}, u32[]{:S(2)}) collective-permute-start(bf16[256,768]{1,0:T(8,128)(2,1)} %get-tuple-element.136.refs_0_), channel_id=1, source_target_pairs={{0,1},{1,0},{2,3},{3,2},{4,5},{5,4},{6,7},{7,6},{8,9},{9,8},{10,11... | collective-permute-start | bytes 1179656 | tf_op jit(solution)/shard_map/ppermute | solution.py:1051
  259.8 13.4 %collective-permute-start.40 = (bf16[256,768]{1,0:T(8,128)(2,1)}, bf16[256,768]{1,0:T(8,128)(2,1)}, u32[]{:S(2)}, u32[]{:S(2)}) collective-permute-start(bf16[256,768]{1,0:T(8,128)(2,1)} %get-tuple-element.138.refs_4_.refs_8_), channel_id=1, source_target_pairs={{0,1},{1,0},{2,3},{3,2},{4,5},{5,4},{6,7},{7,6},{8,9},{9,8},{10,11... | collective-permute-start | bytes 1179656 | tf_op jit(solution)/shard_map/ppermute | solution.py:1051
  272.8 11.8 %collective-permute-start.44 = (bf16[256,2304]{1,0:T(8,128)(2,1)}, bf16[256,2304]{1,0:T(8,128)(2,1)}, u32[]{:S(2)}, u32[]{:S(2)}) collective-permute-start(bf16[256,2304]{1,0:T(8,128)(2,1)} %get-tuple-element.142.refs_6_), channel_id=1, source_target_pairs={{0,1},{1,0},{2,3},{3,2},{4,5},{5,4},{6,7},{7,6},{8,9},{9,8},{10,11... | collective-permute-start | bytes 3538952 | tf_op jit(solution)/shard_map/ppermute | solution.py:1051
  273.2 23.9 %collective-permute-start.50 = (bf16[3584,128]{1,0:T(8,128)(2,1)}, bf16[3584,128]{1,0:T(8,128)(2,1)}, u32[]{:S(2)}, u32[]{:S(2)}) collective-permute-start(bf16[3584,128]{1,0:T(8,128)(2,1)} %add_convert_fusion.3), channel_id=1, source_target_pairs={{0,4},{4,8},{8,12},{12,0},{1,5},{5,9},{9,13},{13,1},{2,6},{6,10},{... | collective-permute-start | bytes 2752520 | tf_op jit(solution)/shard_map/ppermute | solution.py:1058
  283.6 21.1 %collective-permute-start.48 = (bf16[3584,128]{1,0:T(8,128)(2,1)}, bf16[3584,128]{1,0:T(8,128)(2,1)}, u32[]{:S(2)}, u32[]{:S(2)}) collective-permute-start(bf16[3584,128]{1,0:T(8,128)(2,1)} %get-tuple-element.154), channel_id=1, source_target_pairs={{0,16},{16,0},{1,17},{17,1},{2,18},{18,2},{3,19},{19,3},{4,20},{20... | collective-permute-start | bytes 2752520 | tf_op jit(solution)/shard_map/ppermute | solution.py:1048
  284.3 20.8 %collective-permute-start.49 = (bf16[3584,128]{1,0:T(8,128)(2,1)}, bf16[3584,128]{1,0:T(8,128)(2,1)}, u32[]{:S(2)}, u32[]{:S(2)}) collective-permute-start(bf16[3584,128]{1,0:T(8,128)(2,1)} %get-tuple-element.155), channel_id=1, source_target_pairs={{0,2},{1,3},{2,0},{3,1},{4,6},{5,7},{6,4},{7,5},{8,10},{9,11},{10,... | collective-permute-start | bytes 2752520 | tf_op jit(solution)/shard_map/ppermute | solution.py:1054
  299.0 22.8 %collective-permute-start.53 = (bf16[3584,128]{1,0:T(8,128)(2,1)S(1)}, bf16[3584,128]{1,0:T(8,128)(2,1)S(1)}, u32[]{:S(2)}, u32[]{:S(2)}) collective-permute-start(bf16[3584,128]{1,0:T(8,128)(2,1)S(1)} %add_convert_fusion.2), channel_id=1, source_target_pairs={{0,4},{4,8},{8,12},{12,0},{1,5},{5,9},{9,13},{13,1},{2,6},{6,10},{... | collective-permute-start | bytes 2752520 | tf_op jit(solution)/shard_map/ppermute | solution.py:1058
  306.2 17.2 %collective-permute-start.52 = (bf16[1792,128]{1,0:T(8,128)(2,1)S(1)}, bf16[1792,128]{1,0:T(8,128)(2,1)S(1)}, u32[]{:S(2)}, u32[]{:S(2)}) collective-permute-start(bf16[1792,128]{1,0:T(8,128)(2,1)S(1)} %add_convert_fusion.13), channel_id=1, source_target_pairs={{0,16},{16,0},{1,17},{17,1},{2,18},{18,2},{3,19},{19,3},{4,20},{20... | collective-permute-start | bytes 1376264 | tf_op jit(solution)/shard_map/ppermute | solution.py:1048
  308.3 15.1 %collective-permute-start.51 = (bf16[1792,128]{1,0:T(8,128)(2,1)S(1)}, bf16[1792,128]{1,0:T(8,128)(2,1)S(1)}, u32[]{:S(2)}, u32[]{:S(2)}) collective-permute-start(bf16[1792,128]{1,0:T(8,128)(2,1)S(1)} %add_convert_fusion.14), channel_id=1, source_target_pairs={{0,2},{1,3},{2,0},{3,1},{4,6},{5,7},{6,4},{7,5},{8,10},{9,11},{10,... | collective-permute-start | bytes 1376264 | tf_op jit(solution)/shard_map/ppermute | solution.py:1054
  308.7 26.9 %collective-permute-start.46 = (bf16[3584,128]{1,0:T(8,128)(2,1)S(1)}, bf16[3584,128]{1,0:T(8,128)(2,1)S(1)}, u32[]{:S(2)}, u32[]{:S(2)}) collective-permute-start(bf16[3584,128]{1,0:T(8,128)(2,1)S(1)} %copy-done.13), channel_id=1, source_target_pairs={{0,16},{16,0},{1,17},{17,1},{2,18},{18,2},{3,19},{19,3},{4,20},{20... | collective-permute-start | bytes 2752520 | tf_op jit(solution)/shard_map/ppermute | solution.py:1048
  309.4 28.0 %collective-permute-start.47 = (bf16[3584,128]{1,0:T(8,128)(2,1)S(1)}, bf16[3584,128]{1,0:T(8,128)(2,1)S(1)}, u32[]{:S(2)}, u32[]{:S(2)}) collective-permute-start(bf16[3584,128]{1,0:T(8,128)(2,1)S(1)} %copy-done.12), channel_id=1, source_target_pairs={{0,2},{1,3},{2,0},{3,1},{4,6},{5,7},{6,4},{7,5},{8,10},{9,11},{10,... | collective-permute-start | bytes 2752520 | tf_op jit(solution)/shard_map/ppermute | solution.py:1054
  323.3 21.8 %collective-permute-start.56 = (bf16[3584,128]{1,0:T(8,128)(2,1)S(1)}, bf16[3584,128]{1,0:T(8,128)(2,1)S(1)}, u32[]{:S(2)}, u32[]{:S(2)}) collective-permute-start(bf16[3584,128]{1,0:T(8,128)(2,1)S(1)} %add_convert_fusion.1), channel_id=1, source_target_pairs={{0,4},{4,8},{8,12},{12,0},{1,5},{5,9},{9,13},{13,1},{2,6},{6,10},{... | collective-permute-start | bytes 2752520 | tf_op jit(solution)/shard_map/ppermute | solution.py:1058
  348.8 13.5 %collective-permute-start.55 = (bf16[1792,128]{1,0:T(8,128)(2,1)S(1)}, bf16[1792,128]{1,0:T(8,128)(2,1)S(1)}, u32[]{:S(2)}, u32[]{:S(2)}) collective-permute-start(bf16[1792,128]{1,0:T(8,128)(2,1)S(1)} %add_convert_fusion.9), channel_id=1, source_target_pairs={{0,16},{16,0},{1,17},{17,1},{2,18},{18,2},{3,19},{19,3},{4,20},{20... | collective-permute-start | bytes 1376264 | tf_op jit(solution)/shard_map/ppermute | solution.py:1048
  349.6 13.0 %collective-permute-start.54 = (bf16[1792,128]{1,0:T(8,128)(2,1)S(1)}, bf16[1792,128]{1,0:T(8,128)(2,1)}, u32[]{:S(2)}, u32[]{:S(2)}) collective-permute-start(bf16[1792,128]{1,0:T(8,128)(2,1)S(1)} %add_convert_fusion.10), channel_id=1, source_target_pairs={{0,2},{1,3},{2,0},{3,1},{4,6},{5,7},{6,4},{7,5},{8,10},{9,11},{10,... | collective-permute-start | bytes 1376264 | tf_op jit(solution)/shard_map/ppermute | solution.py:1054
  367.3 14.9 %collective-permute-start.65 = (bf16[896,128]{1,0:T(8,128)(2,1)S(1)}, bf16[896,128]{1,0:T(8,128)(2,1)S(1)}, u32[]{:S(2)}, u32[]{:S(2)}) collective-permute-start(bf16[896,128]{1,0:T(8,128)(2,1)S(1)} %pad_maximum_fusion.3), channel_id=1, source_target_pairs={{4,0},{12,4},{0,8},{8,12},{5,1},{13,5},{1,9},{9,13},{6,2},{14,6},{... | collective-permute-start | bytes 688136 | tf_op jit(solution)/shard_map/ppermute | solution.py:1317
  376.3 17.4 %collective-permute-start.60 = (bf16[1792,128]{1,0:T(8,128)(2,1)S(1)}, bf16[1792,128]{1,0:T(8,128)(2,1)S(1)}, u32[]{:S(2)}, u32[]{:S(2)}) collective-permute-start(bf16[1792,128]{1,0:T(8,128)(2,1)S(1)} %add_convert_fusion.6), channel_id=1, source_target_pairs={{0,4},{4,8},{8,12},{12,0},{1,5},{5,9},{9,13},{13,1},{2,6},{6,10},{... | collective-permute-start | bytes 1376264 | tf_op jit(solution)/shard_map/ppermute | solution.py:1058
  407.0 17.1 %collective-permute-start.68 = (bf16[1792,128]{1,0:T(8,128)(2,1)S(1)}, bf16[1792,128]{1,0:T(8,128)(2,1)S(1)}, u32[]{:S(2)}, u32[]{:S(2)}) collective-permute-start(bf16[1792,128]{1,0:T(8,128)(2,1)S(1)} %broadcast_select_fusion.1.refs_0_), channel_id=1, source_target_pairs={{0,2},{1,3},{2,0},{3,1},{4,6},{5,7},{6,4},{7,5},{8,10},{9,11},{10,... | collective-permute-start | bytes 1376264 | tf_op jit(solution)/shard_map/ppermute | solution.py:1054
  413.4 13.2 %collective-permute-start.69 = (bf16[1792,128]{1,0:T(8,128)(2,1)}, bf16[1792,128]{1,0:T(8,128)(2,1)S(1)}, u32[]{:S(2)}, u32[]{:S(2)}) collective-permute-start(bf16[1792,128]{1,0:T(8,128)(2,1)} %collective-permute-done.67.refs_1_), channel_id=1, source_target_pairs={{0,2},{1,3},{2,0},{3,1},{4,6},{5,7},{6,4},{7,5},{8,10},{9,11},{10,... | collective-permute-start | bytes 1376264 | tf_op jit(solution)/shard_map/ppermute | solution.py:1054
  413.8 21.4 %collective-permute-start.70 = (bf16[1792,128]{1,0:T(8,128)(2,1)S(1)}, bf16[1792,128]{1,0:T(8,128)(2,1)}, u32[]{:S(2)}, u32[]{:S(2)}) collective-permute-start(bf16[1792,128]{1,0:T(8,128)(2,1)S(1)} %broadcast_select_fusion.1.refs_0_), channel_id=1, source_target_pairs={{0,1},{1,0},{2,3},{3,2},{4,5},{5,4},{6,7},{7,6},{8,9},{9,8},{10,11... | collective-permute-start | bytes 1376264 | tf_op jit(solution)/shard_map/ppermute | solution.py:1051
  424.1 11.2 %collective-permute-start.71 = (bf16[1792,128]{1,0:T(8,128)(2,1)}, bf16[1792,128]{1,0:T(8,128)(2,1)}, u32[]{:S(2)}, u32[]{:S(2)}) collective-permute-start(bf16[1792,128]{1,0:T(8,128)(2,1)} %collective-permute-done.67.refs_1_), channel_id=1, source_target_pairs={{0,1},{1,0},{2,3},{3,2},{4,5},{5,4},{6,7},{7,6},{8,9},{9,8},{10,11... | collective-permute-start | bytes 1376264 | tf_op jit(solution)/shard_map/ppermute | solution.py:1051
  (43 other events, 453.4 us)
